TPU v7x, 256 devices: a whole 4x4x8 slice. The times are simulated.
256 devices in a mesh: tm: 16 (over z_hi, x), space: 16 (over z_lo, y, core).
Axes of the slice: x: 4, y: 4, z: 8 (z_hi: 4, z_lo: 2; z = z_hi * 2 + z_lo), core: 2. Of those that a mesh axis runs over, the one named last changes fastest.
Arguments:
- forcing: float32 [16, 32, 128, 256], P('tm', 'space'), may hold values from -4 to 4
- iterate: float32 [16, 32, 128, 256], P('tm', 'space'), may hold values from -4 to 4
- kappa: float32 [32, 128, 256], P('space'), may hold values from 0.5 to 2
- velocity: float32 [3, 32, 128, 256], P(None, 'space'), may hold values from -1 to 1
Outputs:
- updated: float32 [16, 32, 128, 256], P('tm', 'space')
All inputs are finite; a program needn't handle non-finite values.
Results may differ from a plain program's by a relative error of at most 0.0003.
Values sent between devices are 32-bit elements; how exact they have to be, the bound alone decides.
No kernel may reach another device: no remote copies, remote signals or barrier semaphores. Data moves between devices by JAX's collectives and lax.ppermute only.
A program may use at most 64 MiB of HBM per device.

v0:
```python
import math

import jax
import jax.numpy as jnp
from jax import lax
from jax.sharding import PartitionSpec as P

SWEEPS = 8


ALPHA = 0.05
TIME_STEP = 0.5


def extended(block, sides, width):
    for axis, dim in sides:
        count = lax.axis_size(axis)
        forward = [(i, i + 1) for i in range(count - 1)]
        backward = [(target, source) for source, target in forward]
        low = lax.ppermute(
            lax.slice_in_dim(block, block.shape[dim] - width, None, axis=dim), axis, forward
        )
        high = lax.ppermute(lax.slice_in_dim(block, 0, width, axis=dim), axis, backward)
        block = jnp.concatenate([low, block, high], axis=dim)
    return block


def passed_along(shard, axis, by):
    count = lax.axis_size(axis)
    pairs = [(i, i + by) for i in range(count) if 0 <= i + by < count]
    return lax.ppermute(shard, axis, pairs)


def from_partner(shard, axis, apart):
    return lax.ppermute(shard, axis, [(i, i ^ 1 << apart) for i in range(lax.axis_size(axis))])


def coefficients(kappa_rim, velocity):
    padded = jnp.pad(kappa_rim, ((0, 0), (1, 1), (1, 1)))
    centre = padded[1:-1, 1:-1, 1:-1]
    plus_z = 0.5 * (centre + padded[2:, 1:-1, 1:-1])
    minus_z = 0.5 * (centre + padded[:-2, 1:-1, 1:-1])
    plus_y = 0.5 * (centre + padded[1:-1, 2:, 1:-1])
    minus_y = 0.5 * (centre + padded[1:-1, :-2, 1:-1])
    plus_x = 0.5 * (centre + padded[1:-1, 1:-1, 2:])
    minus_x = 0.5 * (centre + padded[1:-1, 1:-1, :-2])
    diagonal = plus_z + minus_z + plus_y + minus_y + plus_x + minus_x
    half_velocity = 0.5 * velocity
    coeffs = (
        plus_z - half_velocity[0],
        minus_z + half_velocity[0],
        plus_y - half_velocity[1],
        minus_y + half_velocity[1],
        plus_x - half_velocity[2],
        minus_x + half_velocity[2],
    )
    return (coeffs, diagonal)


def neighbour_sum(coeffs, field_rim):
    lead = [(0, 0)] * (field_rim.ndim - 3)
    padded = jnp.pad(field_rim, lead + [(0, 0), (1, 1), (1, 1)])
    total = coeffs[0] * padded[..., 2:, 1:-1, 1:-1] + coeffs[1] * padded[..., :-2, 1:-1, 1:-1]
    total = (
        total + coeffs[2] * padded[..., 1:-1, 2:, 1:-1] + coeffs[3] * padded[..., 1:-1, :-2, 1:-1]
    )
    total = (
        total + coeffs[4] * padded[..., 1:-1, 1:-1, 2:] + coeffs[5] * padded[..., 1:-1, 1:-1, :-2]
    )
    return total


def rotate(values, phase_angle):
    cosine = jnp.cos(phase_angle)
    sine = jnp.sin(phase_angle)
    return jnp.stack([values[0] * cosine - values[1] * sine, values[0] * sine + values[1] * cosine])


def shards(forcing, iterate, kappa, velocity):
    window = lax.axis_size("tm")
    step_index = lax.axis_index("tm")
    bit_count = window.bit_length() - 1
    current = iterate[0]
    rims = extended(jnp.stack([kappa, current]), (("space", 1),), 1)
    coeffs, diagonal = coefficients(rims[0], velocity)
    applied = diagonal * current - neighbour_sum(coeffs, rims[1])
    previous = passed_along(current, "tm", 1)
    resid = forcing[0] - (current - previous) / TIME_STEP - applied
    log_alpha = jnp.log(jnp.float32(ALPHA))
    growth = jnp.exp(step_index.astype(jnp.float32) / window * log_alpha)
    scaled = resid * growth
    values = jnp.stack([scaled, jnp.zeros_like(scaled)])
    for bit_number in reversed(range(bit_count)):
        half_span = 1 << bit_number
        partner = from_partner(values, "tm", bit_number)
        upper_half = step_index // half_span % 2
        offset = (step_index % half_span).astype(jnp.float32)
        turned = rotate(partner - values, -math.pi * offset / half_span)
        values = jnp.where(upper_half == 1, turned, values + partner)
    spectrum = values
    frequency = jnp.zeros((), jnp.int32)
    for bit_number in range(bit_count):
        frequency = frequency + step_index // (1 << bit_number) % 2 * (
            1 << bit_count - 1 - bit_number
        )
    decay = jnp.exp(log_alpha / window)
    phase_angle = 2.0 * math.pi * frequency.astype(jnp.float32) / window
    sigma_real = (1.0 - decay * jnp.cos(phase_angle)) / TIME_STEP
    sigma_imag = decay * jnp.sin(phase_angle) / TIME_STEP
    denom_real = sigma_real + diagonal
    scale_inv = 1.0 / (denom_real * denom_real + sigma_imag * sigma_imag)
    inverse_real = denom_real * scale_inv
    inverse_imag = -sigma_imag * scale_inv

    def divide(values):
        return jnp.stack(
            [
                values[0] * inverse_real - values[1] * inverse_imag,
                values[0] * inverse_imag + values[1] * inverse_real,
            ]
        )

    solved = divide(spectrum)
    for repeat in range(SWEEPS - 1):
        padded = extended(solved, (("space", 1),), 1)
        solved = divide(spectrum + neighbour_sum(coeffs, padded))
    values = solved
    for bit_number in range(bit_count):
        half_span = 1 << bit_number
        partner = from_partner(values, "tm", bit_number)
        upper_half = step_index // half_span % 2
        offset = (step_index % half_span).astype(jnp.float32)
        twiddle = math.pi * offset / half_span
        values = jnp.where(
            upper_half == 1, partner - rotate(values, twiddle), values + rotate(partner, twiddle)
        )
    correction = values[0] / window
    return (current + correction / growth)[None]


def solution(mesh):
    in_specs = (
        P("tm", "space", None, None),
        P("tm", "space", None, None),
        P("space", None, None),
        P(None, "space", None, None),
    )
    out_specs = P("tm", "space", None, None)
    return jax.shard_map(shards, mesh=mesh, in_specs=in_specs, out_specs=out_specs, check_vma=False)
```

profile of v0, /device:TPU:24, one launch (start us, length us, event | category | flops | bytes accessed | tf_op | source)
XLA Modules:
  0.0 277.2 jit_solution(18075479255748061687)
XLA Ops:
  6.6 3.6 %collective-permute-start.1 = (f32[2,1,128,256]{3,2,1,0:T(8,128)S(1)}, f32[2,1,128,256]{3,2,1,0:T(8,128)S(1)}, u32[]{:S(2)}, u32[]{:S(2)}) collective-permute-start(f32[2,1,128,256]{3,2,1,0:T(8,128)S(1)} %get-tuple-element.69), channel_id=1, source_target_pairs={{1,0},{2,1},{3,2},{4,3},{5,4},{6,5},{7,6},{8,7},{9,8},{10,9},{11,1... | collective-permute-start | bytes 786440 | tf_op jit(solution)/shard_map/ppermute | solution.py:23
  15.4 13.6 %collective-permute-start.3 = (f32[2,2,128,256]{3,2,1,0:T(8,128)S(1)}, f32[2,2,128,256]{3,2,1,0:T(8,128)S(1)}, u32[]{:S(2)}, u32[]{:S(2)}) collective-permute-start(f32[2,2,128,256]{3,2,1,0:T(8,128)S(1)} %stack.151), channel_id=1, source_target_pairs={{0,128},{16,144},{32,160},{48,176},{64,192},{80,208},{96,224},{112... | collective-permute-start | bytes 1572872 | tf_op jit(solution)/shard_map/ppermute | solution.py:35
  29.2 15.9 %collective-permute-done.3 = f32[2,2,128,256]{3,2,1,0:T(8,128)S(1)} collective-permute-done((f32[2,2,128,256]{3,2,1,0:T(8,128)S(1)}, f32[2,2,128,256]{3,2,1,0:T(8,128)S(1)}, u32[]{:S(2)}, u32[]{:S(2)}) %collective-permute-start.3) | collective-permute-done | bytes 524320 | tf_op jit(solution)/shard_map/ppermute | solution.py:35
  46.2 6.8 %collective-permute-start.4 = (f32[2,2,128,256]{3,2,1,0:T(8,128)}, f32[2,2,128,256]{3,2,1,0:T(8,128)}, u32[]{:S(2)}, u32[]{:S(2)}) collective-permute-start(f32[2,2,128,256]{3,2,1,0:T(8,128)} %maximum_select_fusion), channel_id=1, source_target_pairs={{0,64},{16,80},{32,96},{48,112},{64,0},{80,16},{96,32},{112,48},{1... | collective-permute-start | bytes 1572872 | tf_op jit(solution)/shard_map/ppermute | solution.py:35
  53.1 22.3 %collective-permute-done.4 = f32[2,2,128,256]{3,2,1,0:T(8,128)} collective-permute-done((f32[2,2,128,256]{3,2,1,0:T(8,128)}, f32[2,2,128,256]{3,2,1,0:T(8,128)}, u32[]{:S(2)}, u32[]{:S(2)}) %collective-permute-start.4) | collective-permute-done | bytes 524320 | tf_op jit(solution)/shard_map/ppermute | solution.py:35
  78.2 13.9 %collective-permute-done.5 = f32[2,2,128,256]{3,2,1,0:T(8,128)S(1)} collective-permute-done((f32[2,2,128,256]{3,2,1,0:T(8,128)S(1)}, f32[2,2,128,256]{3,2,1,0:T(8,128)S(1)}, u32[]{:S(2)}, u32[]{:S(2)}) %collective-permute-start.5) | collective-permute-done | bytes 524320 | tf_op jit(solution)/shard_map/ppermute | solution.py:35
  92.7 11.5 %collective-permute-done.6 = f32[2,2,128,256]{3,2,1,0:T(8,128)S(1)} collective-permute-done((f32[2,2,128,256]{3,2,1,0:T(8,128)S(1)}, f32[2,2,128,256]{3,2,1,0:T(8,128)S(1)}, u32[]{:S(2)}, u32[]{:S(2)}) %collective-permute-start.6) | collective-permute-done | bytes 524320 | tf_op jit(solution)/shard_map/ppermute | solution.py:35
  106.6 3.6 %collective-permute-start.7 = (f32[2,1,128,256]{3,2,1,0:T(8,128)S(1)}, f32[2,1,128,256]{3,2,1,0:T(8,128)S(1)}, u32[]{:S(2)}, u32[]{:S(2)}) collective-permute-start(f32[2,1,128,256]{3,2,1,0:T(8,128)S(1)} %get-tuple-element.59), channel_id=1, source_target_pairs={{1,0},{2,1},{3,2},{4,3},{5,4},{6,5},{7,6},{8,7},{9,8},{10,9},{11,1... | collective-permute-start | bytes 786440 | tf_op jit(solution)/shard_map/ppermute | solution.py:23
  115.4 5.4 %collective-permute-start.10 = (f32[2,1,128,256]{3,2,1,0:T(8,128)S(1)}, f32[2,1,128,256]{3,2,1,0:T(8,128)S(1)}, u32[]{:S(2)}, u32[]{:S(2)}) collective-permute-start(f32[2,1,128,256]{3,2,1,0:T(8,128)S(1)} %get-tuple-element.56), channel_id=1, source_target_pairs={{0,1},{1,2},{2,3},{3,4},{4,5},{5,6},{6,7},{7,8},{8,9},{9,10},{10,1... | collective-permute-start | bytes 786440 | tf_op jit(solution)/shard_map/ppermute | solution.py:20
  127.9 5.9 %collective-permute-start.12 = (f32[2,1,128,256]{3,2,1,0:T(8,128)S(1)}, f32[2,1,128,256]{3,2,1,0:T(8,128)S(1)}, u32[]{:S(2)}, u32[]{:S(2)}) collective-permute-start(f32[2,1,128,256]{3,2,1,0:T(8,128)S(1)} %get-tuple-element.54), channel_id=1, source_target_pairs={{0,1},{1,2},{2,3},{3,4},{4,5},{5,6},{6,7},{7,8},{8,9},{9,10},{10,1... | collective-permute-start | bytes 786440 | tf_op jit(solution)/shard_map/ppermute | solution.py:20
  135.8 3.9 %collective-permute-done.11 = f32[2,1,128,256]{3,2,1,0:T(8,128)S(1)} collective-permute-done((f32[2,1,128,256]{3,2,1,0:T(8,128)S(1)}, f32[2,1,128,256]{3,2,1,0:T(8,128)S(1)}, u32[]{:S(2)}, u32[]{:S(2)}) %collective-permute-start.11) | collective-permute-done | bytes 262176 | tf_op jit(solution)/shard_map/ppermute | solution.py:23
  140.9 5.9 %collective-permute-start.14 = (f32[2,1,128,256]{3,2,1,0:T(8,128)S(1)}, f32[2,1,128,256]{3,2,1,0:T(8,128)S(1)}, u32[]{:S(2)}, u32[]{:S(2)}) collective-permute-start(f32[2,1,128,256]{3,2,1,0:T(8,128)S(1)} %get-tuple-element.52), channel_id=1, source_target_pairs={{0,1},{1,2},{2,3},{3,4},{4,5},{5,6},{6,7},{7,8},{8,9},{9,10},{10,1... | collective-permute-start | bytes 786440 | tf_op jit(solution)/shard_map/ppermute | solution.py:20
  148.8 3.9 %collective-permute-done.13 = f32[2,1,128,256]{3,2,1,0:T(8,128)S(1)} collective-permute-done((f32[2,1,128,256]{3,2,1,0:T(8,128)S(1)}, f32[2,1,128,256]{3,2,1,0:T(8,128)S(1)}, u32[]{:S(2)}, u32[]{:S(2)}) %collective-permute-start.13) | collective-permute-done | bytes 262176 | tf_op jit(solution)/shard_map/ppermute | solution.py:23
  153.9 5.9 %collective-permute-start.16 = (f32[2,1,128,256]{3,2,1,0:T(8,128)S(1)}, f32[2,1,128,256]{3,2,1,0:T(8,128)S(1)}, u32[]{:S(2)}, u32[]{:S(2)}) collective-permute-start(f32[2,1,128,256]{3,2,1,0:T(8,128)S(1)} %get-tuple-element.50), channel_id=1, source_target_pairs={{0,1},{1,2},{2,3},{3,4},{4,5},{5,6},{6,7},{7,8},{8,9},{9,10},{10,1... | collective-permute-start | bytes 786440 | tf_op jit(solution)/shard_map/ppermute | solution.py:20
  162.0 3.7 %collective-permute-done.15 = f32[2,1,128,256]{3,2,1,0:T(8,128)S(1)} collective-permute-done((f32[2,1,128,256]{3,2,1,0:T(8,128)S(1)}, f32[2,1,128,256]{3,2,1,0:T(8,128)S(1)}, u32[]{:S(2)}, u32[]{:S(2)}) %collective-permute-start.15) | collective-permute-done | bytes 262176 | tf_op jit(solution)/shard_map/ppermute | solution.py:23
  167.0 5.9 %collective-permute-start.18 = (f32[2,1,128,256]{3,2,1,0:T(8,128)S(1)}, f32[2,1,128,256]{3,2,1,0:T(8,128)S(1)}, u32[]{:S(2)}, u32[]{:S(2)}) collective-permute-start(f32[2,1,128,256]{3,2,1,0:T(8,128)S(1)} %get-tuple-element.48), channel_id=1, source_target_pairs={{0,1},{1,2},{2,3},{3,4},{4,5},{5,6},{6,7},{7,8},{8,9},{9,10},{10,1... | collective-permute-start | bytes 786440 | tf_op jit(solution)/shard_map/ppermute | solution.py:20
  174.8 3.9 %collective-permute-done.17 = f32[2,1,128,256]{3,2,1,0:T(8,128)S(1)} collective-permute-done((f32[2,1,128,256]{3,2,1,0:T(8,128)S(1)}, f32[2,1,128,256]{3,2,1,0:T(8,128)S(1)}, u32[]{:S(2)}, u32[]{:S(2)}) %collective-permute-start.17) | collective-permute-done | bytes 262176 | tf_op jit(solution)/shard_map/ppermute | solution.py:23
  180.0 5.9 %collective-permute-start.20 = (f32[2,1,128,256]{3,2,1,0:T(8,128)S(1)}, f32[2,1,128,256]{3,2,1,0:T(8,128)S(1)}, u32[]{:S(2)}, u32[]{:S(2)}) collective-permute-start(f32[2,1,128,256]{3,2,1,0:T(8,128)S(1)} %get-tuple-element.46), channel_id=1, source_target_pairs={{0,1},{1,2},{2,3},{3,4},{4,5},{5,6},{6,7},{7,8},{8,9},{9,10},{10,1... | collective-permute-start | bytes 786440 | tf_op jit(solution)/shard_map/ppermute | solution.py:20
  187.9 3.9 %collective-permute-done.19 = f32[2,1,128,256]{3,2,1,0:T(8,128)S(1)} collective-permute-done((f32[2,1,128,256]{3,2,1,0:T(8,128)S(1)}, f32[2,1,128,256]{3,2,1,0:T(8,128)S(1)}, u32[]{:S(2)}, u32[]{:S(2)}) %collective-permute-start.19) | collective-permute-done | bytes 262176 | tf_op jit(solution)/shard_map/ppermute | solution.py:23
  193.4 11.4 %collective-permute-done.21 = f32[2,2,128,256]{3,2,1,0:T(8,128)S(1)} collective-permute-done((f32[2,2,128,256]{3,2,1,0:T(8,128)S(1)}, f32[2,2,128,256]{3,2,1,0:T(8,128)S(1)}, u32[]{:S(2)}, u32[]{:S(2)}) %collective-permute-start.21) | collective-permute-done | bytes 524320 | tf_op jit(solution)/shard_map/ppermute | solution.py:35
  205.9 13.4 %collective-permute-done.22 = f32[2,2,128,256]{3,2,1,0:T(8,128)S(1)} collective-permute-done((f32[2,2,128,256]{3,2,1,0:T(8,128)S(1)}, f32[2,2,128,256]{3,2,1,0:T(8,128)S(1)}, u32[]{:S(2)}, u32[]{:S(2)}) %collective-permute-start.22) | collective-permute-done | bytes 524320 | tf_op jit(solution)/shard_map/ppermute | solution.py:35
  223.3 23.6 %collective-permute-done.23 = f32[2,2,128,256]{3,2,1,0:T(8,128)S(1)} collective-permute-done((f32[2,2,128,256]{3,2,1,0:T(8,128)S(1)}, f32[2,2,128,256]{3,2,1,0:T(8,128)S(1)}, u32[]{:S(2)}, u32[]{:S(2)}) %collective-permute-start.23) | collective-permute-done | bytes 524320 | tf_op jit(solution)/shard_map/ppermute | solution.py:35
  247.2 3.9 %collective-permute-start.24 = (f32[2,2,128,256]{3,2,1,0:T(8,128)S(1)}, f32[2,2,128,256]{3,2,1,0:T(8,128)S(1)}, u32[]{:S(2)}, u32[]{:S(2)}) collective-permute-start(f32[2,2,128,256]{3,2,1,0:T(8,128)S(1)} %fusion.61), channel_id=1, source_target_pairs={{0,128},{16,144},{32,160},{48,176},{64,192},{80,208},{96,224},{112... | collective-permute-start | bytes 1572872 | tf_op jit(solution)/shard_map/ppermute | solution.py:35
  251.2 25.1 %collective-permute-done.24 = f32[2,2,128,256]{3,2,1,0:T(8,128)S(1)} collective-permute-done((f32[2,2,128,256]{3,2,1,0:T(8,128)S(1)}, f32[2,2,128,256]{3,2,1,0:T(8,128)S(1)}, u32[]{:S(2)}, u32[]{:S(2)}) %collective-permute-start.24) | collective-permute-done | bytes 524320 | tf_op jit(solution)/shard_map/ppermute | solution.py:35
  (105 shorter events, 52.4 us)
Async XLA Ops:
  0.0 14.3 %collective-permute-start = (f32[2,128,256]{2,1,0:T(8,128)}, f32[2,128,256]{2,1,0:T(8,128)S(1)}, u32[]{:S(2)}, u32[]{:S(2)}) collective-permute-start(f32[2,128,256]{2,1,0:T(8,128)} %bitcast.223), channel_id=1, source_target_pairs={{0,16},{16,32},{32,48},{48,64},{64,80},{80,96},{96,112},{112,128},... | collective-permute-start | bytes 786440 | tf_op jit(solution)/shard_map/ppermute | solution.py:31
  4.7 7.7 %collective-permute-start.2 = (f32[2,1,128,256]{3,2,1,0:T(8,128)S(1)}, f32[2,1,128,256]{3,2,1,0:T(8,128)S(1)}, u32[]{:S(2)}, u32[]{:S(2)}) collective-permute-start(f32[2,1,128,256]{3,2,1,0:T(8,128)S(1)} %get-tuple-element.68), channel_id=1, source_target_pairs={{0,1},{1,2},{2,3},{3,4},{4,5},{5,6},{6,7},{7,8},{8,9},{9,10},{10,1... | collective-permute-start | bytes 786440 | tf_op jit(solution)/shard_map/ppermute | solution.py:20
  6.6 7.5 %collective-permute-start.1 = (f32[2,1,128,256]{3,2,1,0:T(8,128)S(1)}, f32[2,1,128,256]{3,2,1,0:T(8,128)S(1)}, u32[]{:S(2)}, u32[]{:S(2)}) collective-permute-start(f32[2,1,128,256]{3,2,1,0:T(8,128)S(1)} %get-tuple-element.69), channel_id=1, source_target_pairs={{1,0},{2,1},{3,2},{4,3},{5,4},{6,5},{7,6},{8,7},{9,8},{10,9},{11,1... | collective-permute-start | bytes 786440 | tf_op jit(solution)/shard_map/ppermute | solution.py:23
  15.4 29.7 %collective-permute-start.3 = (f32[2,2,128,256]{3,2,1,0:T(8,128)S(1)}, f32[2,2,128,256]{3,2,1,0:T(8,128)S(1)}, u32[]{:S(2)}, u32[]{:S(2)}) collective-permute-start(f32[2,2,128,256]{3,2,1,0:T(8,128)S(1)} %stack.151), channel_id=1, source_target_pairs={{0,128},{16,144},{32,160},{48,176},{64,192},{80,208},{96,224},{112... | collective-permute-start | bytes 1572872 | tf_op jit(solution)/shard_map/ppermute | solution.py:35
  46.2 29.3 %collective-permute-start.4 = (f32[2,2,128,256]{3,2,1,0:T(8,128)}, f32[2,2,128,256]{3,2,1,0:T(8,128)}, u32[]{:S(2)}, u32[]{:S(2)}) collective-permute-start(f32[2,2,128,256]{3,2,1,0:T(8,128)} %maximum_select_fusion), channel_id=1, source_target_pairs={{0,64},{16,80},{32,96},{48,112},{64,0},{80,16},{96,32},{112,48},{1... | collective-permute-start | bytes 1572872 | tf_op jit(solution)/shard_map/ppermute | solution.py:35
  77.9 14.2 %collective-permute-start.5 = (f32[2,2,128,256]{3,2,1,0:T(8,128)S(1)}, f32[2,2,128,256]{3,2,1,0:T(8,128)S(1)}, u32[]{:S(2)}, u32[]{:S(2)}) collective-permute-start(f32[2,2,128,256]{3,2,1,0:T(8,128)S(1)} %maximum_select_fusion.1), channel_id=1, source_target_pairs={{0,32},{16,48},{32,0},{48,16},{64,96},{80,112},{96,64},{112,80},{1... | collective-permute-start | bytes 1572872 | tf_op jit(solution)/shard_map/ppermute | solution.py:35
  92.4 11.8 %collective-permute-start.6 = (f32[2,2,128,256]{3,2,1,0:T(8,128)S(1)}, f32[2,2,128,256]{3,2,1,0:T(8,128)S(1)}, u32[]{:S(2)}, u32[]{:S(2)}) collective-permute-start(f32[2,2,128,256]{3,2,1,0:T(8,128)S(1)} %maximum_select_fusion.2), channel_id=1, source_target_pairs={{0,16},{16,0},{32,48},{48,32},{64,80},{80,64},{96,112},{112,96},{1... | collective-permute-start | bytes 1572872 | tf_op jit(solution)/shard_map/ppermute | solution.py:35
  104.7 7.7 %collective-permute-start.8 = (f32[2,1,128,256]{3,2,1,0:T(8,128)S(1)}, f32[2,1,128,256]{3,2,1,0:T(8,128)S(1)}, u32[]{:S(2)}, u32[]{:S(2)}) collective-permute-start(f32[2,1,128,256]{3,2,1,0:T(8,128)S(1)} %get-tuple-element.58), channel_id=1, source_target_pairs={{0,1},{1,2},{2,3},{3,4},{4,5},{5,6},{6,7},{7,8},{8,9},{9,10},{10,1... | collective-permute-start | bytes 786440 | tf_op jit(solution)/shard_map/ppermute | solution.py:20
  106.6 7.5 %collective-permute-start.7 = (f32[2,1,128,256]{3,2,1,0:T(8,128)S(1)}, f32[2,1,128,256]{3,2,1,0:T(8,128)S(1)}, u32[]{:S(2)}, u32[]{:S(2)}) collective-permute-start(f32[2,1,128,256]{3,2,1,0:T(8,128)S(1)} %get-tuple-element.59), channel_id=1, source_target_pairs={{1,0},{2,1},{3,2},{4,3},{5,4},{6,5},{7,6},{8,7},{9,8},{10,9},{11,1... | collective-permute-start | bytes 786440 | tf_op jit(solution)/shard_map/ppermute | solution.py:23
  115.4 7.9 %collective-permute-start.10 = (f32[2,1,128,256]{3,2,1,0:T(8,128)S(1)}, f32[2,1,128,256]{3,2,1,0:T(8,128)S(1)}, u32[]{:S(2)}, u32[]{:S(2)}) collective-permute-start(f32[2,1,128,256]{3,2,1,0:T(8,128)S(1)} %get-tuple-element.56), channel_id=1, source_target_pairs={{0,1},{1,2},{2,3},{3,4},{4,5},{5,6},{6,7},{7,8},{8,9},{9,10},{10,1... | collective-permute-start | bytes 786440 | tf_op jit(solution)/shard_map/ppermute | solution.py:20
  120.8 5.8 %collective-permute-start.9 = (f32[2,1,128,256]{3,2,1,0:T(8,128)S(1)}, f32[2,1,128,256]{3,2,1,0:T(8,128)S(1)}, u32[]{:S(2)}, u32[]{:S(2)}) collective-permute-start(f32[2,1,128,256]{3,2,1,0:T(8,128)S(1)} %get-tuple-element.57), channel_id=1, source_target_pairs={{1,0},{2,1},{3,2},{4,3},{5,4},{6,5},{7,6},{8,7},{9,8},{10,9},{11,1... | collective-permute-start | bytes 786440 | tf_op jit(solution)/shard_map/ppermute | solution.py:23
  127.9 7.9 %collective-permute-start.12 = (f32[2,1,128,256]{3,2,1,0:T(8,128)S(1)}, f32[2,1,128,256]{3,2,1,0:T(8,128)S(1)}, u32[]{:S(2)}, u32[]{:S(2)}) collective-permute-start(f32[2,1,128,256]{3,2,1,0:T(8,128)S(1)} %get-tuple-element.54), channel_id=1, source_target_pairs={{0,1},{1,2},{2,3},{3,4},{4,5},{5,6},{6,7},{7,8},{8,9},{9,10},{10,1... | collective-permute-start | bytes 786440 | tf_op jit(solution)/shard_map/ppermute | solution.py:20
  133.8 5.8 %collective-permute-start.11 = (f32[2,1,128,256]{3,2,1,0:T(8,128)S(1)}, f32[2,1,128,256]{3,2,1,0:T(8,128)S(1)}, u32[]{:S(2)}, u32[]{:S(2)}) collective-permute-start(f32[2,1,128,256]{3,2,1,0:T(8,128)S(1)} %get-tuple-element.55), channel_id=1, source_target_pairs={{1,0},{2,1},{3,2},{4,3},{5,4},{6,5},{7,6},{8,7},{9,8},{10,9},{11,1... | collective-permute-start | bytes 786440 | tf_op jit(solution)/shard_map/ppermute | solution.py:23
  140.9 7.9 %collective-permute-start.14 = (f32[2,1,128,256]{3,2,1,0:T(8,128)S(1)}, f32[2,1,128,256]{3,2,1,0:T(8,128)S(1)}, u32[]{:S(2)}, u32[]{:S(2)}) collective-permute-start(f32[2,1,128,256]{3,2,1,0:T(8,128)S(1)} %get-tuple-element.52), channel_id=1, source_target_pairs={{0,1},{1,2},{2,3},{3,4},{4,5},{5,6},{6,7},{7,8},{8,9},{9,10},{10,1... | collective-permute-start | bytes 786440 | tf_op jit(solution)/shard_map/ppermute | solution.py:20
  146.9 5.8 %collective-permute-start.13 = (f32[2,1,128,256]{3,2,1,0:T(8,128)S(1)}, f32[2,1,128,256]{3,2,1,0:T(8,128)S(1)}, u32[]{:S(2)}, u32[]{:S(2)}) collective-permute-start(f32[2,1,128,256]{3,2,1,0:T(8,128)S(1)} %get-tuple-element.53), channel_id=1, source_target_pairs={{1,0},{2,1},{3,2},{4,3},{5,4},{6,5},{7,6},{8,7},{9,8},{10,9},{11,1... | collective-permute-start | bytes 786440 | tf_op jit(solution)/shard_map/ppermute | solution.py:23
  153.9 8.0 %collective-permute-start.16 = (f32[2,1,128,256]{3,2,1,0:T(8,128)S(1)}, f32[2,1,128,256]{3,2,1,0:T(8,128)S(1)}, u32[]{:S(2)}, u32[]{:S(2)}) collective-permute-start(f32[2,1,128,256]{3,2,1,0:T(8,128)S(1)} %get-tuple-element.50), channel_id=1, source_target_pairs={{0,1},{1,2},{2,3},{3,4},{4,5},{5,6},{6,7},{7,8},{8,9},{9,10},{10,1... | collective-permute-start | bytes 786440 | tf_op jit(solution)/shard_map/ppermute | solution.py:20
  159.9 5.8 %collective-permute-start.15 = (f32[2,1,128,256]{3,2,1,0:T(8,128)S(1)}, f32[2,1,128,256]{3,2,1,0:T(8,128)S(1)}, u32[]{:S(2)}, u32[]{:S(2)}) collective-permute-start(f32[2,1,128,256]{3,2,1,0:T(8,128)S(1)} %get-tuple-element.51), channel_id=1, source_target_pairs={{1,0},{2,1},{3,2},{4,3},{5,4},{6,5},{7,6},{8,7},{9,8},{10,9},{11,1... | collective-permute-start | bytes 786440 | tf_op jit(solution)/shard_map/ppermute | solution.py:23
  167.0 7.9 %collective-permute-start.18 = (f32[2,1,128,256]{3,2,1,0:T(8,128)S(1)}, f32[2,1,128,256]{3,2,1,0:T(8,128)S(1)}, u32[]{:S(2)}, u32[]{:S(2)}) collective-permute-start(f32[2,1,128,256]{3,2,1,0:T(8,128)S(1)} %get-tuple-element.48), channel_id=1, source_target_pairs={{0,1},{1,2},{2,3},{3,4},{4,5},{5,6},{6,7},{7,8},{8,9},{9,10},{10,1... | collective-permute-start | bytes 786440 | tf_op jit(solution)/shard_map/ppermute | solution.py:20
  172.9 5.8 %collective-permute-start.17 = (f32[2,1,128,256]{3,2,1,0:T(8,128)S(1)}, f32[2,1,128,256]{3,2,1,0:T(8,128)S(1)}, u32[]{:S(2)}, u32[]{:S(2)}) collective-permute-start(f32[2,1,128,256]{3,2,1,0:T(8,128)S(1)} %get-tuple-element.49), channel_id=1, source_target_pairs={{1,0},{2,1},{3,2},{4,3},{5,4},{6,5},{7,6},{8,7},{9,8},{10,9},{11,1... | collective-permute-start | bytes 786440 | tf_op jit(solution)/shard_map/ppermute | solution.py:23
  180.0 7.9 %collective-permute-start.20 = (f32[2,1,128,256]{3,2,1,0:T(8,128)S(1)}, f32[2,1,128,256]{3,2,1,0:T(8,128)S(1)}, u32[]{:S(2)}, u32[]{:S(2)}) collective-permute-start(f32[2,1,128,256]{3,2,1,0:T(8,128)S(1)} %get-tuple-element.46), channel_id=1, source_target_pairs={{0,1},{1,2},{2,3},{3,4},{4,5},{5,6},{6,7},{7,8},{8,9},{9,10},{10,1... | collective-permute-start | bytes 786440 | tf_op jit(solution)/shard_map/ppermute | solution.py:20
  193.0 11.8 %collective-permute-start.21 = (f32[2,2,128,256]{3,2,1,0:T(8,128)S(1)}, f32[2,2,128,256]{3,2,1,0:T(8,128)S(1)}, u32[]{:S(2)}, u32[]{:S(2)}) collective-permute-start(f32[2,2,128,256]{3,2,1,0:T(8,128)S(1)} %pad_maximum_fusion.29), channel_id=1, source_target_pairs={{0,16},{16,0},{32,48},{48,32},{64,80},{80,64},{96,112},{112,96},{1... | collective-permute-start | bytes 1572872 | tf_op jit(solution)/shard_map/ppermute | solution.py:35
  205.0 14.4 %collective-permute-start.22 = (f32[2,2,128,256]{3,2,1,0:T(8,128)S(1)}, f32[2,2,128,256]{3,2,1,0:T(8,128)S(1)}, u32[]{:S(2)}, u32[]{:S(2)}) collective-permute-start(f32[2,2,128,256]{3,2,1,0:T(8,128)S(1)} %fusion.59), channel_id=1, source_target_pairs={{0,32},{16,48},{32,0},{48,16},{64,96},{80,112},{96,64},{112,80},{1... | collective-permute-start | bytes 1572872 | tf_op jit(solution)/shard_map/ppermute | solution.py:35
  219.6 27.3 %collective-permute-start.23 = (f32[2,2,128,256]{3,2,1,0:T(8,128)S(1)}, f32[2,2,128,256]{3,2,1,0:T(8,128)S(1)}, u32[]{:S(2)}, u32[]{:S(2)}) collective-permute-start(f32[2,2,128,256]{3,2,1,0:T(8,128)S(1)} %fusion.60), channel_id=1, source_target_pairs={{0,64},{16,80},{32,96},{48,112},{64,0},{80,16},{96,32},{112,48},{1... | collective-permute-start | bytes 1572872 | tf_op jit(solution)/shard_map/ppermute | solution.py:35
  247.2 29.2 %collective-permute-start.24 = (f32[2,2,128,256]{3,2,1,0:T(8,128)S(1)}, f32[2,2,128,256]{3,2,1,0:T(8,128)S(1)}, u32[]{:S(2)}, u32[]{:S(2)}) collective-permute-start(f32[2,2,128,256]{3,2,1,0:T(8,128)S(1)} %fusion.61), channel_id=1, source_target_pairs={{0,128},{16,144},{32,160},{48,176},{64,192},{80,208},{96,224},{112... | collective-permute-start | bytes 1572872 | tf_op jit(solution)/shard_map/ppermute | solution.py:35
  (10 other events, 85.7 us)
where the time goes:
time: 281 us; the launch traced here: 277 us
  waiting for transfers between devices  166 us (59%)
  starting transfers between devices  90.4 us (32%)
  other arithmetic  18.6 us (7%)
    ppermute x8, waiting for transfers between devices, from_partner(): lax.ppermute(shard, axis, [(i, i ^ 1 << apart) for i in range(lax.axis_si...  137 us
    ppermute x8, starting transfers between devices, extended(): lax.ppermute(lax.slice_in_dim(block, block.shape[dim] - width, None, axis...  38.9 us
    ppermute x8, starting transfers between devices, from_partner(): lax.ppermute(shard, axis, [(i, i ^ 1 << apart) for i in range(lax.axis_si...  29 us
    ppermute x8, waiting for transfers between devices, extended(): lax.ppermute(lax.slice_in_dim(block, 0, width, axis=dim), axis, backward)  26 us
    ppermute x8, starting transfers between devices, extended(): lax.ppermute(lax.slice_in_dim(block, 0, width, axis=dim), axis, backward)  19 us
  transfers between devices with their start and end apart: 25, of which 19 were waited for; matrix products, arithmetic and copies ran while one was open for 1% of the time, Pallas kernels for 0%

commit v1 on v0

v1 whole, which is shorter than its diff:
```python
import functools
import math

import jax
import jax.numpy as jnp
import numpy as np
from jax import lax
from jax.experimental import pallas as pl
from jax.experimental.pallas import tpu as pltpu
from jax.sharding import PartitionSpec as P

SWEEPS = 8
ALPHA = 0.05
TIME_STEP = 0.5
WINDOW = 16
DECAY = ALPHA ** (1.0 / WINDOW)
NZ, NY, NX = 32, 128, 256
OWN = NX // WINDOW
WIDE = OWN + 16
HALF = OWN // 2
HWIDE = HALF + 16


def time_tables():
    n = np.arange(WINDOW)
    ahead = np.zeros((WINDOW, WINDOW))
    back = np.zeros((WINDOW, WINDOW))
    for p in range(8):
        angle = 2.0 * np.pi * p * n / WINDOW
        ahead[p] = np.cos(angle)
        ahead[8 + p] = -np.sin(angle) if p else np.cos(np.pi * n)
        back[:, p] = np.cos(angle) * (2.0 if p else 1.0)
        back[:, 8 + p] = -2.0 * np.sin(angle) if p else np.cos(np.pi * n)
    ahead = ahead * DECAY**n[None, :]
    back = back / WINDOW * DECAY ** -n[:, None].astype(float)
    return ahead.astype(np.float32), back.astype(np.float32)


def shift_table():
    rows = []
    for s in range(16):
        p = s % 8
        angle = 2.0 * np.pi * p / WINDOW
        real = (1.0 - DECAY * np.cos(angle)) / TIME_STEP
        imag = DECAY * np.sin(angle) / TIME_STEP
        other = real if p else (1.0 + DECAY) / TIME_STEP
        rows.append([real, other, imag if p else 0.0])
    return np.asarray(rows, np.float32)


def swapped(block, axis, pairs):
    return lax.ppermute(block, axis, pairs)


def coefficients(kappa_rim, velocity):
    padded = jnp.pad(kappa_rim, ((0, 0), (1, 1), (1, 1)))
    centre = padded[1:-1, 1:-1, 1:-1]
    plus_z = 0.5 * (centre + padded[2:, 1:-1, 1:-1])
    minus_z = 0.5 * (centre + padded[:-2, 1:-1, 1:-1])
    plus_y = 0.5 * (centre + padded[1:-1, 2:, 1:-1])
    minus_y = 0.5 * (centre + padded[1:-1, :-2, 1:-1])
    plus_x = 0.5 * (centre + padded[1:-1, 1:-1, 2:])
    minus_x = 0.5 * (centre + padded[1:-1, 1:-1, :-2])
    diagonal = plus_z + minus_z + plus_y + minus_y + plus_x + minus_x
    half_velocity = 0.5 * velocity
    coeffs = (
        plus_z - half_velocity[0],
        minus_z + half_velocity[0],
        plus_y - half_velocity[1],
        minus_y + half_velocity[1],
        plus_x - half_velocity[2],
        minus_x + half_velocity[2],
    )
    return (coeffs, diagonal)


def neighbour_sum(coeffs, field_rim):
    padded = jnp.pad(field_rim, [(0, 0), (1, 1), (1, 1)])
    total = coeffs[0] * padded[2:, 1:-1, 1:-1] + coeffs[1] * padded[:-2, 1:-1, 1:-1]
    total = total + coeffs[2] * padded[1:-1, 2:, 1:-1] + coeffs[3] * padded[1:-1, :-2, 1:-1]
    total = total + coeffs[4] * padded[1:-1, 1:-1, 2:] + coeffs[5] * padded[1:-1, 1:-1, :-2]
    return total


def jacobi_kernel(where, shift, spec, fields, out, kap, cof, inv, field_a, field_b):
    first = pl.multiple_of(where[0], HALF)
    start = where[1]
    column = start + lax.broadcasted_iota(jnp.int32, (HWIDE, NY), 0)
    lane = lax.broadcasted_iota(jnp.int32, (HWIDE, NY), 1)
    real, other, imag = shift[0], shift[1], shift[2]
    zeros = jnp.zeros((HWIDE, NY), jnp.float32)
    kap[0] = zeros
    kap[NZ + 1] = zeros
    for buf in (field_a, field_b):
        for part in range(2):
            buf[0, part] = zeros
            buf[NZ + 1, part] = zeros

    def load_kappa(s, carry):
        for plane in range(2):
            kap[2 * s + plane + 1] = fields[s, 0, plane, pl.ds(first, HWIDE), :]
        return carry

    lax.fori_loop(0, NZ // 2, load_kappa, 0)

    def divide(z, total_real, total_imag):
        inv_real, inv_other, inv_imag = inv[z, 0], inv[z, 1], inv[z, 2]
        return (
            total_real * inv_real - total_imag * inv_imag,
            total_real * inv_imag + total_imag * inv_other,
        )

    def prepare(z, carry):
        centre = kap[z + 1]
        half = [
            0.5 * fields[z // 2, 1 + d, z % 2, pl.ds(first, HWIDE), :] for d in range(3)
        ]
        up_z = 0.5 * (centre + kap[z + 2])
        down_z = 0.5 * (centre + kap[z])
        up_y = 0.5 * (centre + jnp.where(lane < NY - 1, pltpu.roll(centre, NY - 1, 1), 0.0))
        down_y = 0.5 * (centre + jnp.where(lane > 0, pltpu.roll(centre, 1, 1), 0.0))
        up_x = 0.5 * (centre + pltpu.roll(centre, HWIDE - 1, 0))
        down_x = 0.5 * (centre + pltpu.roll(centre, 1, 0))
        diagonal = up_z + down_z + up_y + down_y + up_x + down_x
        cof[z, 0] = up_z - half[0]
        cof[z, 1] = down_z + half[0]
        cof[z, 2] = jnp.where(lane < NY - 1, up_y - half[1], 0.0)
        cof[z, 3] = jnp.where(lane > 0, down_y + half[1], 0.0)
        cof[z, 4] = jnp.where(column < NX - 1, up_x - half[2], 0.0)
        cof[z, 5] = jnp.where(column > 0, down_x + half[2], 0.0)
        den = real + diagonal
        den_other = other + diagonal
        scale = 1.0 / (den * den + imag * imag)
        inv[z, 0] = den * scale
        inv[z, 1] = den_other / (den_other * den_other + imag * imag)
        inv[z, 2] = -imag * scale
        new_real, new_imag = divide(z, spec[z, 0], spec[z, 1])
        field_a[z + 1, 0] = new_real
        field_a[z + 1, 1] = new_imag
        return carry

    lax.fori_loop(0, NZ, prepare, 0)

    def total_of(src, z, part):
        centre = src[z + 1, part]
        total = cof[z, 0] * src[z + 2, part] + cof[z, 1] * src[z, part]
        total += cof[z, 2] * pltpu.roll(centre, NY - 1, 1) + cof[z, 3] * pltpu.roll(centre, 1, 1)
        total += cof[z, 4] * pltpu.roll(centre, HWIDE - 1, 0) + cof[z, 5] * pltpu.roll(centre, 1, 0)
        return total + spec[z, part]

    def sweep(src, dst, last):
        def body(z, carry):
            new_real, new_imag = divide(z, total_of(src, z, 0), total_of(src, z, 1))
            if last:
                out[z, 0] = new_real[8 : 8 + HALF]
                out[z, 1] = new_imag[8 : 8 + HALF]
            else:
                dst[z + 1, 0] = new_real
                dst[z + 1, 1] = new_imag
            return carry

        lax.fori_loop(0, NZ, body, 0)

    buffers = (field_a, field_b)
    for repeat in range(SWEEPS - 1):
        sweep(buffers[repeat % 2], buffers[(repeat + 1) % 2], repeat == SWEEPS - 2)


def jacobi(where, shift, spec, fields):
    vmem = pl.BlockSpec(memory_space=pltpu.VMEM)
    smem = pl.BlockSpec(memory_space=pltpu.SMEM)
    return pl.pallas_call(
        jacobi_kernel,
        out_shape=jax.ShapeDtypeStruct((NZ, 2, HALF, NY), jnp.float32),
        in_specs=[smem, smem, vmem, vmem],
        out_specs=vmem,
        scratch_shapes=[
            pltpu.VMEM((NZ + 2, HWIDE, NY), jnp.float32),
            pltpu.VMEM((NZ, 6, HWIDE, NY), jnp.float32),
            pltpu.VMEM((NZ, 3, HWIDE, NY), jnp.float32),
            pltpu.VMEM((NZ + 2, 2, HWIDE, NY), jnp.float32),
            pltpu.VMEM((NZ + 2, 2, HWIDE, NY), jnp.float32),
        ],
        compiler_params=pltpu.CompilerParams(vmem_limit_bytes=32 * 1024 * 1024),
    )(where, shift, spec, fields)


def shards(forcing, iterate, kappa, velocity):
    step = lax.axis_index("tm")
    place = lax.axis_index("space")
    ahead, back = time_tables()
    current = iterate[0]
    both = jnp.stack([kappa, current])
    even = place % 2 == 0
    inner_send = jnp.where(even, both[:, 1], both[:, 0])
    outer_send = jnp.where(even, both[:, 0], both[:, 1])
    previous = lax.ppermute(current, "tm", [(i, i + 1) for i in range(WINDOW - 1)])
    inner = lax.ppermute(inner_send, "space", [(i, i ^ 1) for i in range(16)])
    pairs = [(i, i + 1) for i in range(1, 15, 2)] + [(i + 1, i) for i in range(1, 15, 2)]
    outer = lax.ppermute(outer_send, "space", pairs)
    low = jnp.where(even, outer, inner)
    high = jnp.where(even, inner, outer)
    rims = jnp.concatenate([low[:, None], both, high[:, None]], axis=1)

    fields = jnp.pad(jnp.concatenate([kappa[None], velocity]), ((0, 0), (0, 0), (0, 0), (8, 8)))
    fields = lax.dynamic_slice_in_dim(fields, step * OWN, WIDE, 3)
    fields = lax.all_gather(fields.transpose(0, 1, 3, 2), "space")

    coeffs, diagonal = coefficients(rims[0], velocity)
    applied = diagonal * current - neighbour_sum(coeffs, rims[1])
    resid = forcing[0] - (current - previous) / TIME_STEP - applied
    turned = jnp.pad(resid.transpose(0, 2, 1), ((0, 0), (8, 8), (0, 0)))
    sent = jnp.stack([turned[:, OWN * c : OWN * c + WIDE] for c in range(WINDOW)])
    times = lax.all_to_all(sent, "tm", 0, 0)
    spectrum = jnp.einsum("cn,nzxy->czxy", ahead, times, precision="highest")
    parts = spectrum.reshape(2, 8, 2, WIDE, NY).transpose(1, 2, 0, 3, 4)
    sent = jnp.concatenate([parts[:, :, :, :HWIDE], parts[:, :, :, HALF : HALF + HWIDE]])
    spec = lax.all_to_all(sent, "space", 0, 0).reshape(NZ, 2, HWIDE, NY)
    first = place // 8 * HALF
    where = jnp.stack([first, step * OWN - 8 + first]).astype(jnp.int32)
    shift = jnp.asarray(shift_table())[place]
    solved = jacobi(where, shift, spec, fields)
    solved = lax.all_to_all(solved.reshape(16, 2, 2, HALF, NY), "space", 0, 0)
    solved = solved.reshape(2, 8, 2, 2, HALF, NY).transpose(3, 1, 2, 0, 4, 5)
    solved = solved.reshape(WINDOW, 2, OWN, NY)
    correction = jnp.einsum("nc,czxy->nzxy", back, solved, precision="highest")
    correction = lax.all_to_all(correction, "tm", 0, 0)
    correction = correction.transpose(1, 3, 0, 2).reshape(2, NY, NX)
    return (current + correction)[None]


def solution(mesh):
    in_specs = (
        P("tm", "space", None, None),
        P("tm", "space", None, None),
        P("space", None, None),
        P(None, "space", None, None),
    )
    out_specs = P("tm", "space", None, None)
    return jax.shard_map(shards, mesh=mesh, in_specs=in_specs, out_specs=out_specs, check_vma=False)
```

time: 281 us -> 142 us (0.51); the launches traced: 277 us -> 141 us
  waiting for transfers between devices: 166 us -> 15.1 us
  starting transfers between devices: 90.4 us -> 11.9 us
  blocking collectives: 0 us -> 65.7 us
  Pallas kernels: 0 us -> 23.1 us
  other arithmetic: 18.6 us -> 4.16 us
  between operations: 1.97 us -> 13.7 us
  local copies, waits for them, and re-layouts: 0.67 us -> 6.55 us
    ppermute x25 -> x3, waiting for transfers between devices: 166 us -> 4.2 us  [the longest x1 4.06 us: shards(): lax.ppermute(current, 'tm', [(i, i + 1) for i in range(WINDOW - 1)])]
    ppermute x25 -> x3, starting transfers between devices: 90.4 us -> 6.3 us  [the longest x1 3.54 us: shards(): lax.ppermute(current, 'tm', [(i, i + 1) for i in range(WINDOW - 1)])]
    all_to_all x0 -> x3, blocking collectives: none -> 65.7 us  [the longest x1 38.7 us: shards(): times = lax.all_to_all(sent, 'tm', 0, 0)]
    pallas_call x0 -> x1, Pallas kernels: none -> 23.1 us  [jacobi(): pl.pallas_call(jacobi_kernel, out_shape=jax.ShapeDtypeStruct((NZ, 2, HALF...]
    all_to_all x0 -> x1, waiting for transfers between devices: none -> 10.9 us  [shards(): spec = lax.all_to_all(sent, 'space', 0, 0).reshape(NZ, 2, HWIDE, NY)]
    all_to_all x0 -> x1, starting transfers between devices: none -> 5.63 us  [shards(): spec = lax.all_to_all(sent, 'space', 0, 0).reshape(NZ, 2, HWIDE, NY)]
    add x8 -> x1, other arithmetic: 4.74 us -> 0.05 us  [shards(): return (current + correction)[None]]
    unnamed x18 -> x32, local copies, waits for them, and re-layouts: 0.56 us -> 4.45 us
  transfers between devices with their start and end apart: 25 -> 5, of which waited for: 19 -> 3; matrix products, arithmetic and copies ran while one was open for 1% -> 4% of each run, Pallas kernels for 0% -> 0%
where the time goes in v1:
time: 142 us; the launch traced here: 141 us
  blocking collectives  65.7 us (46%)
  Pallas kernels  23.1 us (16%)
  waiting for transfers between devices  15.1 us (11%)
  between operations  13.7 us (10%)
  starting transfers between devices  11.9 us (8%)
  local copies, waits for them, and re-layouts  6.55 us (5%)
  other arithmetic  4.16 us (3%)
    all_to_all x1, blocking collectives, shards(): times = lax.all_to_all(sent, 'tm', 0, 0)  38.7 us
    pallas_call x1, Pallas kernels, jacobi(): pl.pallas_call(jacobi_kernel, out_shape=jax.ShapeDtypeStruct((NZ, 2, HALF...  23.1 us
    all_to_all x1, blocking collectives, shards(): correction = lax.all_to_all(correction, 'tm', 0, 0)  16.4 us
    all_to_all x1, waiting for transfers between devices, shards(): spec = lax.all_to_all(sent, 'space', 0, 0).reshape(NZ, 2, HWIDE, NY)  10.9 us
    all_to_all x1, blocking collectives, shards(): solved = lax.all_to_all(solved.reshape(16, 2, 2, HALF, NY), 'space', 0, 0)  10.6 us
    all_to_all x1, starting transfers between devices, shards(): spec = lax.all_to_all(sent, 'space', 0, 0).reshape(NZ, 2, HWIDE, NY)  5.63 us
    unnamed x32, local copies, waits for them, and re-layouts  4.45 us
    ppermute x1, waiting for transfers between devices, shards(): lax.ppermute(current, 'tm', [(i, i + 1) for i in range(WINDOW - 1)])  4.06 us
  transfers between devices with their start and end apart: 5, of which 3 were waited for; matrix products, arithmetic and copies ran while one was open for 4% of the time, Pallas kernels for 0%

profile of v1, /device:TPU:24, one launch (start us, length us, event | category | flops | bytes accessed | tf_op | source)
XLA Modules:
  0.0 141.5 jit_solution(12983644781873949089)
XLA Ops:
  6.5 1.1 copy.86
  7.7 1.1 copy.84
  8.8 0.7 select_bitcast_fusion.2
  9.6 2.8 %collective-permute-start.2 = (f32[2,128,256]{1,2,0:T(8,128)S(1)}, f32[2,128,256]{1,2,0:T(8,128)}, u32[]{:S(2)}, u32[]{:S(2)}) collective-permute-start(f32[2,128,256]{1,2,0:T(8,128)S(1)} %get-tuple-element.11), channel_id=1, source_target_pairs={{1,2},{3,4},{5,6},{7,8},{9,10},{11,12},{13,14},{2,1},{4,3},{6,5},{... | collective-permute-start | bytes 786440 | tf_op jit(solution)/shard_map/ppermute | solution.py:200
  12.5 3.5 %collective-permute-start = (f32[2,128,256]{1,2,0:T(8,128)S(1)}, f32[2,128,256]{1,2,0:T(8,128)S(1)}, u32[]{:S(2)}, u32[]{:S(2)}) collective-permute-start(f32[2,128,256]{1,2,0:T(8,128)S(1)} %bitcast.171), channel_id=1, source_target_pairs={{0,16},{16,32},{32,48},{48,64},{64,80},{80,96},{96,112},{112,128},... | collective-permute-start | bytes 786440 | tf_op jit(solution)/shard_map/ppermute | solution.py:197
  16.0 0.3 copy.96
  16.3 0.7 fusion.33
  17.4 1.0 select_bitcast_fusion
  18.5 4.1 %collective-permute-done = f32[2,128,256]{1,2,0:T(8,128)S(1)} collective-permute-done((f32[2,128,256]{1,2,0:T(8,128)S(1)}, f32[2,128,256]{1,2,0:T(8,128)S(1)}, u32[]{:S(2)}, u32[]{:S(2)}) %collective-permute-start) | collective-permute-done | bytes 262176 | tf_op jit(solution)/shard_map/ppermute | solution.py:197
  22.6 0.6 fusion.18
  23.4 38.7 %all_to_all.20 = f32[16,2,32,128]{3,2,1,0:T(8,128)S(1)} all-to-all(f32[16,2,32,128]{3,2,1,0:T(8,128)S(1)} %constant_dynamic-update-slice_fusion), channel_id=1, replica_groups=mesh['tm'=16,'space'=16] {'tm'}, dimensions={0} | all-to-all | bytes 1048576 | tf_op jit(solution)/shard_map/all_to_all | solution.py:214
  62.1 0.8 convolution_bitcast_fusion
  62.9 0.2 copy.115
  63.2 0.9 pad_maximum_fusion.1
  64.1 5.6 %all-to-all-start.1 = ((f32[16,2,2,24,128]{4,3,2,1,0:T(8,128)}), f32[16,2,2,24,128]{4,3,2,1,0:T(8,128)S(1)}, u32[]{:S(2)}, u32[]{:S(2)}) async-start(f32[16,2,2,24,128]{4,3,2,1,0:T(8,128)} %pad_maximum_fusion.1), calls=%async_computation.1 | async-start | bytes 1572864 | tf_op jit(solution)/shard_map/all_to_all | solution.py:218
  69.8 0.7 fusion.40.shift
  70.5 10.9 %all-to-all-done.1 = f32[16,2,2,24,128]{4,3,2,1,0:T(8,128)S(1)} async-done(((f32[16,2,2,24,128]{4,3,2,1,0:T(8,128)}), f32[16,2,2,24,128]{4,3,2,1,0:T(8,128)S(1)}, u32[]{:S(2)}, u32[]{:S(2)}) %all-to-all-start.1) | async-done | bytes 786464 | tf_op jit(solution)/shard_map/all_to_all | solution.py:218
  81.4 1.6 %copy-done = f32[64,2,32,128]{3,2,1,0:T(8,128)S(1)} copy-done((f32[64,2,32,128]{3,2,1,0:T(8,128)S(1)}, f32[64,2,32,128]{3,2,1,0:T(8,128)}, u32[]{:S(2)}) %copy-start) | copy-done | bytes 2097176
  83.0 23.1 %shard_map.73 = f32[32,2,8,128]{3,2,1,0:T(8,128)S(1)} custom-call(s32[2]{0:T(128)S(1)} %pad_add_fusion.where, f32[3]{0:T(128)S(1)} %fusion.40.shift, f32[32,2,24,128]{3,2,1,0:T(8,128)S(1)} %bitcast.163, f32[16,4,2,32,128]{4,3,2,1,0:T(8,128)S(1)} %bitcast.164), custom_call_target="tpu_custom_call" | custom-call | tf_op jit(solution)/shard_map/pallas_call | solution.py:172
  106.2 10.6 %all_to_all.21 = f32[16,2,2,8,128]{4,3,2,1,0:T(8,128)S(1)} all-to-all(f32[16,2,2,8,128]{4,3,2,1,0:T(8,128)S(1)} %bitcast.165), channel_id=1, replica_groups=mesh['tm'=16,'space'=16] {'space'}, dimensions={0} | all-to-all | bytes 524288 | tf_op jit(solution)/shard_map/all_to_all | solution.py:223
  116.8 0.2 copy.101
  116.9 0.4 fusion.42
  117.4 16.4 %all_to_all.22 = f32[16,2,16,128]{3,2,1,0:T(8,128)S(1)} all-to-all(f32[16,2,16,128]{3,2,1,0:T(8,128)S(1)} %copy.102), channel_id=1, replica_groups=mesh['tm'=16,'space'=16] {'tm'}, dimensions={0} | all-to-all | bytes 524288 | tf_op jit(solution)/shard_map/all_to_all | solution.py:227
  133.8 0.8 copy.105
  (43 shorter events, 1.0 us)
Async XLA Ops:
  6.5 5.8 %copy-start.1 = (f32[1,2,128,256]{3,2,1,0:T(8,128)S(1)}, f32[1,2,128,256]{3,2,1,0:T(8,128)}, u32[]{:S(2)}) copy-start(f32[1,2,128,256]{3,2,1,0:T(8,128)} %param.8) | copy-start | bytes 786436
  6.5 74.9 %all-gather.3.cloned.1.call-start = ((), (), s32[]{:S(2)}) async-start(), calls=%async_computation.4 | async-start | bytes 2228224 | tf_op jit(solution)/shard_map/all_gather | solution.py:207
  7.7 8.4 %copy-start.2 = (f32[3,2,128,256]{3,2,1,0:T(8,128)S(1)}, f32[3,2,128,256]{3,2,1,0:T(8,128)}, u32[]{:S(2)}) copy-start(f32[3,2,128,256]{3,2,1,0:T(8,128)} %param.10) | copy-start | bytes 2359300
  9.6 7.6 %collective-permute-start.1 = (f32[2,128,256]{1,2,0:T(8,128)}, f32[2,128,256]{1,2,0:T(8,128)S(1)}, u32[]{:S(2)}, u32[]{:S(2)}) collective-permute-start(f32[2,128,256]{1,2,0:T(8,128)} %get-tuple-element.12), channel_id=1, source_target_pairs={{0,1},{1,0},{2,3},{3,2},{4,5},{5,4},{6,7},{7,6},{8,9},{9,8},{10,11... | collective-permute-start | bytes 786440 | tf_op jit(solution)/shard_map/ppermute | solution.py:198
  9.6 7.8 %collective-permute-start.2 = (f32[2,128,256]{1,2,0:T(8,128)S(1)}, f32[2,128,256]{1,2,0:T(8,128)}, u32[]{:S(2)}, u32[]{:S(2)}) collective-permute-start(f32[2,128,256]{1,2,0:T(8,128)S(1)} %get-tuple-element.11), channel_id=1, source_target_pairs={{1,2},{3,4},{5,6},{7,8},{9,10},{11,12},{13,14},{2,1},{4,3},{6,5},{... | collective-permute-start | bytes 786440 | tf_op jit(solution)/shard_map/ppermute | solution.py:200
  12.5 4.5 %copy-start.3 = (f32[1,2,128,256]{3,2,1,0:T(8,128)S(1)}, f32[1,2,128,256]{3,2,1,0:T(8,128)}, u32[]{:S(2)}) copy-start(f32[1,2,128,256]{3,2,1,0:T(8,128)} %param.7) | copy-start | bytes 786436
  12.5 10.1 %collective-permute-start = (f32[2,128,256]{1,2,0:T(8,128)S(1)}, f32[2,128,256]{1,2,0:T(8,128)S(1)}, u32[]{:S(2)}, u32[]{:S(2)}) collective-permute-start(f32[2,128,256]{1,2,0:T(8,128)S(1)} %bitcast.171), channel_id=1, source_target_pairs={{0,16},{16,32},{32,48},{48,64},{64,80},{80,96},{96,112},{112,128},... | collective-permute-start | bytes 786440 | tf_op jit(solution)/shard_map/ppermute | solution.py:197
  23.2 38.9 %copy-start.5 = (f32[16,16,1,1]{1,0,3,2:T(8,128)S(1)}, f32[16,16,1,1]{1,0,3,2:T(8,128)}, u32[]{:S(2)}) copy-start(f32[16,16,1,1]{1,0,3,2:T(8,128)} %constant.71) | copy-start | bytes 3076
  64.1 17.3 %all-to-all-start.1 = ((f32[16,2,2,24,128]{4,3,2,1,0:T(8,128)}), f32[16,2,2,24,128]{4,3,2,1,0:T(8,128)S(1)}, u32[]{:S(2)}, u32[]{:S(2)}) async-start(f32[16,2,2,24,128]{4,3,2,1,0:T(8,128)} %pad_maximum_fusion.1), calls=%async_computation.1 | async-start | bytes 1572864 | tf_op jit(solution)/shard_map/all_to_all | solution.py:218
  81.4 1.6 %copy-start = (f32[64,2,32,128]{3,2,1,0:T(8,128)S(1)}, f32[64,2,32,128]{3,2,1,0:T(8,128)}, u32[]{:S(2)}) copy-start(f32[64,2,32,128]{3,2,1,0:T(8,128)} %all-gather.3.cloned.1.call-done) | copy-start | bytes 6291460
  83.0 33.9 %copy-start.4 = (f32[16,16,1,1]{1,0,3,2:T(8,128)S(1)}, f32[16,16,1,1]{1,0,3,2:T(8,128)}, u32[]{:S(2)}) copy-start(f32[16,16,1,1]{1,0,3,2:T(8,128)} %constant.70) | copy-start | bytes 3076
Sparse Core Ops, SparseCore 0:
  17.1 43.1 all-gather.2

commit v2 on v0

v2 whole, which is shorter than its diff:
```python
import math

import jax
import jax.numpy as jnp
from jax import lax
from jax.experimental import pallas as pl
from jax.experimental.pallas import tpu as pltpu
from jax.sharding import PartitionSpec as P

SWEEPS = 8
ALPHA = 0.05
TIME_STEP = 0.5
WINDOW = 16
DECAY = ALPHA ** (1.0 / WINDOW)
NZ, NY, NX = 32, 128, 256
OWN = NX // WINDOW
WIDE = OWN + 16
SLAB = 2
CHIP = 4
CHIPS = NZ // CHIP
FIRST = 3
REACH = 10
NARROW = OWN + 8
REALS = 8


def time_scale(n):
    return DECAY**n


def shift_rows():
    rows = []
    for p in range(8):
        angle = 2.0 * math.pi * p / WINDOW
        real = (1.0 - DECAY * math.cos(angle)) / TIME_STEP
        imag = DECAY * math.sin(angle) / TIME_STEP
        other = real if p else (1.0 + DECAY) / TIME_STEP
        rows.append((real, other, imag if p else 0.0))
    return rows


def spectrum_of(times):
    even = [times[j] + times[j + 8] for j in range(8)]
    odd = [times[j] - times[j + 8] for j in range(8)]
    f = [even[j] + even[j + 4] for j in range(4)]
    g = [even[j] - even[j + 4] for j in range(4)]
    parts = [None] * 16
    parts[0] = (f[0] + f[2]) + (f[1] + f[3])
    parts[8] = (f[0] + f[2]) - (f[1] + f[3])
    parts[4] = f[0] - f[2]
    parts[12] = f[3] - f[1]
    root = math.sqrt(0.5)
    less, more = (g[1] - g[3]) * root, (g[1] + g[3]) * root
    parts[2] = g[0] + less
    parts[6] = g[0] - less
    parts[10] = -(g[2] + more)
    parts[14] = g[2] - more
    less = [odd[j] - odd[8 - j] for j in range(1, 4)]
    more = [odd[j] + odd[8 - j] for j in range(1, 4)]
    for k in (1, 3, 5, 7):
        angle = math.pi * k / 8
        parts[k] = odd[0] + sum(math.cos(angle * (j + 1)) * less[j] for j in range(3))
        tail = sum(math.sin(angle * (j + 1)) * more[j] for j in range(3))
        parts[8 + k] = -(tail + odd[4]) if k % 4 == 1 else odd[4] - tail
    return parts


def times_of(parts):
    plus, minus = parts[0] + parts[8], parts[0] - parts[8]
    two = [None if j in (0, 8) else 2.0 * parts[j] for j in range(16)]
    f = [plus + two[4], minus - two[12], plus - two[4], minus + two[12]]
    root = math.sqrt(0.5)
    g = [
        two[2] + two[6],
        root * ((two[2] - two[10]) - (two[6] + two[14])),
        two[14] - two[10],
        root * ((two[6] - two[14]) - (two[2] + two[10])),
    ]
    even = [f[j] + g[j] for j in range(4)] + [f[j] - g[j] for j in range(4)]
    odd = [None] * 8
    odd[0] = (two[1] + two[3]) + (two[5] + two[7])
    odd[4] = (two[11] + two[15]) - (two[9] + two[13])
    for n in range(1, 4):
        c = sum(math.cos(math.pi * p * n / 8) * two[p] for p in (1, 3, 5, 7))
        s = sum(math.sin(math.pi * p * n / 8) * two[8 + p] for p in (1, 3, 5, 7))
        odd[n] = c - s
        odd[8 - n] = -(c + s)
    return [even[n] + odd[n] for n in range(8)] + [even[n] - odd[n] for n in range(8)]


def entry_kernel(iterate, kappa, outer, inner, sems):
    parity = lax.axis_index("space") % 2
    copies = [
        pltpu.make_async_copy(iterate.at[0, parity], outer.at[0], sems.at[0]),
        pltpu.make_async_copy(kappa.at[parity], outer.at[1], sems.at[1]),
        pltpu.make_async_copy(iterate.at[0, 1 - parity], inner.at[0], sems.at[2]),
        pltpu.make_async_copy(kappa.at[1 - parity], inner.at[1], sems.at[3]),
    ]
    for copy in copies:
        copy.start()
    for copy in copies:
        copy.wait()


def fields_kernel(kappa, velocity, out, held, turned, sems):
    step = lax.axis_index("tm")
    copies = [pltpu.make_async_copy(kappa, held.at[0], sems.at[0])]
    copies += [pltpu.make_async_copy(velocity.at[d], held.at[1 + d], sems.at[1 + d]) for d in range(3)]
    for copy in copies:
        copy.start()
    edge = jnp.zeros((8, NY), jnp.float32)
    for field in range(4):
        copies[field].wait()
        for plane in range(2):
            spot = turned.at[2 * field + plane]
            spot[0:8] = edge
            spot[8 : 8 + NX] = held[field, plane].T
            spot[8 + NX : 16 + NX] = edge
            out[field, plane] = spot[pl.ds(pl.multiple_of(step * OWN, OWN), WIDE), :]


def inside_kernel(forcing, iterate, kappa, velocity, base, rim, value):
    row = lax.broadcasted_iota(jnp.int32, (NY, NX), 0)
    lane = lax.broadcasted_iota(jnp.int32, (NY, NX), 1)

    def shifted(array, dim, up):
        extent = NY if dim == 0 else NX
        index = row if dim == 0 else lane
        inside = index < extent - 1 if up else index > 0
        return jnp.where(inside, pltpu.roll(array, extent - 1 if up else 1, dim), 0.0)

    for plane in range(2):
        centre, here = kappa[plane], iterate[0, plane]
        towards = -1.0 if plane == 0 else 1.0
        half = 0.5 * velocity[0, plane]
        face = 0.5 * (centre + kappa[1 - plane])
        diagonal = face + 0.5 * centre
        total = (face + towards * half) * iterate[0, 1 - plane]
        rim[plane] = 0.5 * centre - towards * half
        for dim in range(2):
            half = 0.5 * velocity[1 + dim, plane]
            for up, sign in ((True, -1.0), (False, 1.0)):
                face = 0.5 * (centre + shifted(centre, dim, up))
                diagonal += face
                total += (face + sign * half) * shifted(here, dim, up)
        base[plane] = forcing[0, plane] - here * (1.0 / TIME_STEP) - (diagonal * here - total)
        value[plane] = here


def resid_kernel(base, rim, value, previous, outer, inner, out, turned):
    step = lax.axis_index("tm")
    place = lax.axis_index("space")
    even = place % 2 == 0
    growth = jnp.exp(jnp.full((1, 1), step.astype(jnp.float32) / WINDOW * math.log(ALPHA), jnp.float32))
    carried = jnp.where(step == 0, 0.0, 1.0 / TIME_STEP)
    edge = jnp.zeros((8, NY), jnp.float32)
    for plane in range(2):
        side, other = (outer, inner) if plane == 0 else (inner, outer)
        ends = place == 0 if plane == 0 else place == 2 * CHIPS - 1
        here = value[plane]
        near = jnp.where(ends, 0.0, jnp.where(even, side[0], other[0]))
        far = jnp.where(ends, 0.0, 0.5 * jnp.where(even, side[1], other[1]))
        resid = base[plane] + previous[0, plane] * carried + (rim[plane] + far) * near - far * here
        turned[plane, 0:8] = edge
        turned[plane, 8 : 8 + NX] = (resid * growth).T
        turned[plane, 8 + NX : 16 + NX] = edge
        for c in range(WINDOW):
            out[c, plane] = turned[plane, OWN * c : OWN * c + WIDE]


def ahead_kernel(times, fields, above, below, keep, send):
    core = lax.axis_index("space") % 2
    for plane in range(SLAB):
        for tile in range(WIDE // 8):
            rows = slice(8 * tile, 8 * tile + 8)
            parts = spectrum_of([times[n, plane, rows] for n in range(WINDOW)])
            for j in range(REALS):
                p, part = j % 4, j // 4
                low, high = parts[8 * part + p], parts[8 * part + 4 + p]
                keep[plane, j, rows] = jnp.where(core == 0, low, high)
                send[REALS * plane + j, rows] = jnp.where(core == 0, high, low)
    spot = SLAB * REALS
    for source in (below, fields, above):
        for field in range(4):
            for plane in range(SLAB):
                send[spot] = source[field, plane]
                spot += 1


def gather_kernel(keep, got, chip, up, down):
    core = lax.axis_index("space") % 2
    for j in range(REALS):
        for plane in range(CHIP):
            mine, theirs = keep[plane % SLAB, j], got[REALS * (plane % SLAB) + j]
            value = jnp.where(core == plane // SLAB, mine, theirs)
            chip[plane, j] = value
            if plane >= CHIP - FIRST:
                up[plane - (CHIP - FIRST), j] = value
            if plane < FIRST:
                down[plane, j] = value


def back_kernel(mine, theirs, out):
    core = lax.axis_index("space") % 2
    for plane in range(SLAB):
        for tile in range(OWN // 8):
            rows = slice(8 * tile, 8 * tile + 8)
            parts = [None] * 16
            for j in range(REALS):
                p, part = j % 4, j // 4
                one, two = mine[plane, j, rows], theirs[plane, j, rows]
                parts[8 * part + p] = jnp.where(core == 0, one, two)
                parts[8 * part + 4 + p] = jnp.where(core == 0, two, one)
            values = times_of(parts)
            for n in range(WINDOW):
                out[n, plane, rows] = values[n] * (time_scale(-n) / WINDOW)


def update_kernel(correction, iterate, out):
    for plane in range(SLAB):
        turned = correction[:, plane].reshape(NX, NY).T
        out[0, plane] = iterate[0, plane] + turned


def prepare_kernel(fields, above, below, got, cof, held):
    place = lax.axis_index("space")
    core, chip = place % 2, place // 2
    start = lax.axis_index("tm") * OWN - 8
    column = start + lax.broadcasted_iota(jnp.int32, (WIDE, NY), 0)
    lane = lax.broadcasted_iota(jnp.int32, (WIDE, NY), 1)
    rows = shift_rows()
    shifts = [[jnp.where(core == 0, rows[j][i], rows[4 + j][i]) for i in range(3)] for j in range(4)]
    spot = SLAB * REALS
    for third, source in enumerate((below, fields, above)):
        for field in range(4):
            for plane in range(SLAB):
                value, other = source[field, plane], got[spot]
                spot += 1
                if field == 0 and third != 1:
                    outside = chip == (0 if third == 0 else CHIPS - 1)
                    value, other = jnp.where(outside, 0.0, value), jnp.where(outside, 0.0, other)
                held[field, CHIP * third + plane] = jnp.where(core == 0, value, other)
                held[field, CHIP * third + SLAB + plane] = jnp.where(core == 0, other, value)
    for z in range(REACH):
        spot = z + 1
        centre = held[0, spot]
        half = [0.5 * held[1 + d, spot] for d in range(3)]
        up_z = 0.5 * (centre + held[0, spot + 1])
        down_z = 0.5 * (centre + held[0, spot - 1])
        up_y = 0.5 * (centre + jnp.where(lane < NY - 1, pltpu.roll(centre, NY - 1, 1), 0.0))
        down_y = 0.5 * (centre + jnp.where(lane > 0, pltpu.roll(centre, 1, 1), 0.0))
        up_x = 0.5 * (centre + pltpu.roll(centre, WIDE - 1, 0))
        down_x = 0.5 * (centre + pltpu.roll(centre, 1, 0))
        diagonal = up_z + down_z + up_y + down_y + up_x + down_x
        plus_z, minus_z = up_z - half[0], down_z + half[0]
        if spot == 2 * CHIP - 1:
            plus_z = jnp.where(chip == CHIPS - 1, 0.0, plus_z)
        if spot == CHIP:
            minus_z = jnp.where(chip == 0, 0.0, minus_z)
        cof[z, 0] = plus_z
        cof[z, 1] = minus_z
        cof[z, 2] = jnp.where(lane < NY - 1, up_y - half[1], 0.0)
        cof[z, 3] = jnp.where(lane > 0, down_y + half[1], 0.0)
        cof[z, 4] = jnp.where(column < NX - 1, up_x - half[2], 0.0)
        cof[z, 5] = jnp.where(column > 0, down_x + half[2], 0.0)
        for j, (real, other, imag) in enumerate(shifts):
            den = real + diagonal
            scale = 1.0 / (den * den + imag * imag)
            cof[z, 6 + 2 * j] = den * scale
            cof[z, 7 + 2 * j] = -imag * scale
            if j == 0:
                den = other + diagonal
                cof[z, 14] = den / (den * den + imag * imag)


def divide(cof, z, j, total_real, total_imag):
    inv_real, inv_imag = cof[z, 6 + 2 * j], cof[z, 7 + 2 * j]
    inv_other = cof[z, 14] if j == 0 else inv_real
    return (
        total_real * inv_real - total_imag * inv_imag,
        total_real * inv_imag + total_imag * inv_other,
    )


def part_of(field, z, r, ahead=0):
    start = 8 + WIDE * (REALS * z + r) + ahead
    return field.at[start : start + WIDE]


def sweeps(cof, spec_of, src, dst, planes, shift, finish):
    for number, (first, end) in enumerate(planes):
        for z in range(first, end):
            here = z + shift
            for j in range(4):
                totals = []
                for r in (j, 4 + j):
                    centre = part_of(src, here, r)[...]
                    total = cof[z, 0] * part_of(src, here + 1, r)[...] + cof[z, 1] * part_of(src, here - 1, r)[...]
                    total += cof[z, 2] * pltpu.roll(centre, NY - 1, 1) + cof[z, 3] * pltpu.roll(centre, 1, 1)
                    total += cof[z, 4] * part_of(src, here, r, 1)[...] + cof[z, 5] * part_of(src, here, r, -1)[...]
                    totals.append(total + spec_of(z, r))
                for r, value in zip((j, 4 + j), divide(cof, z, j, *totals)):
                    if number == len(planes) - 1:
                        finish(z, r, value)
                    else:
                        part_of(dst, here, r)[...] = value
        src, dst = dst, src


def spectrum_reader(chip, above, below):
    def spec_of(z, r):
        if z < FIRST:
            return below[z, r]
        return chip[z - FIRST, r] if z < FIRST + CHIP else above[z - FIRST - CHIP, r]

    return spec_of


def first_kernel(chip, above, below, cof, out, field_a, field_b):
    spec_of = spectrum_reader(chip, above, below)
    for field in (field_a, field_b):
        field[0:8] = jnp.zeros((8, NY), jnp.float32)
        field[8 + WIDE * REALS * REACH :] = jnp.zeros((8, NY), jnp.float32)
    for z in range(REACH):
        for j in range(4):
            for r, value in zip((j, 4 + j), divide(cof, z, j, spec_of(z, j), spec_of(z, 4 + j))):
                part_of(field_a, z, r)[...] = value

    def finish(z, r, value):
        out[z - FIRST, r] = value[4 : 4 + NARROW]

    sweeps(cof, spec_of, field_a, field_b, [(1, 9), (2, 8), (3, 7)], 0, finish)


def second_kernel(chip, above, below, cof, own, high, low, mine, theirs, field_a, field_b):
    core = lax.axis_index("space") % 2
    spec_of = spectrum_reader(chip, above, below)
    for field in (field_a, field_b):
        field[0:8] = jnp.zeros((8, NY), jnp.float32)
        field[8 + WIDE * REALS * 3 * CHIP :] = jnp.zeros((8, NY), jnp.float32)
    edge = jnp.zeros((8, NY), jnp.float32)
    for third, source in enumerate((low, own, high)):
        for plane in range(CHIP):
            for r in range(REALS):
                spot = part_of(field_a, CHIP * third + plane, r)
                spot[0:8] = edge
                spot[WIDE - 8 : WIDE] = edge
                spot[4 : 4 + NARROW] = source[plane, r]
    held = {}

    def finish(z, r, value):
        plane = z - FIRST
        value = value[8 : 8 + OWN]
        if plane < SLAB:
            held[plane, r] = value
        else:
            low_value = held.pop((plane - SLAB, r))
            mine[plane - SLAB, r] = jnp.where(core == 0, low_value, value)
            theirs[plane - SLAB, r] = jnp.where(core == 0, value, low_value)

    sweeps(cof, spec_of, field_a, field_b, [(0, 10), (1, 9), (2, 8), (3, 7)], 1, finish)


def call(kernel, shapes, args, scratch=(), anywhere=False, mib=32):
    vmem = pl.BlockSpec(memory_space=pltpu.VMEM)
    several = isinstance(shapes, list)
    out_shape = [jax.ShapeDtypeStruct(shape, jnp.float32) for shape in (shapes if several else [shapes])]
    return pl.pallas_call(
        kernel,
        out_shape=out_shape if several else out_shape[0],
        in_specs=[pl.BlockSpec(memory_space=pl.ANY) if anywhere else vmem] * len(args),
        out_specs=[vmem] * len(shapes) if several else vmem,
        scratch_shapes=[pltpu.VMEM(dims, jnp.float32) if isinstance(dims, tuple) else dims for dims in scratch],
        compiler_params=pltpu.CompilerParams(vmem_limit_bytes=mib * 1024 * 1024),
    )(*args)


def shards(forcing, iterate, kappa, velocity):
    block = (SLAB, NY, NX)
    previous = lax.ppermute(iterate, "tm", [(i, (i + 1) % WINDOW) for i in range(WINDOW)])
    cores = [(i, i ^ 1) for i in range(2 * CHIPS)]
    upward = [(i, (i + 2) % (2 * CHIPS)) for i in range(2 * CHIPS)]
    downward = [(j, i) for i, j in upward]
    outer, inner = call(
        entry_kernel, [block, block], (iterate, kappa), [pltpu.SemaphoreType.DMA((4,))], anywhere=True, mib=56
    )
    facing = [(i, (i + 1) % (2 * CHIPS)) for i in range(1, 2 * CHIPS, 2)]
    outer = lax.ppermute(outer, "space", facing + [(j, i) for i, j in facing])
    inner = lax.ppermute(inner, "space", cores)
    fields = call(
        fields_kernel,
        (4, SLAB, WIDE, NY),
        (kappa, velocity),
        [(4, SLAB, NY, NX), (8, NX + 16, NY), pltpu.SemaphoreType.DMA((4,))],
        anywhere=True,
    )
    fields_below = lax.ppermute(fields, "space", upward)
    fields_above = lax.ppermute(fields, "space", downward)
    base, rim, value = call(inside_kernel, [block] * 3, (forcing, iterate, kappa, velocity))
    sent = call(
        resid_kernel,
        (WINDOW, SLAB, WIDE, NY),
        (base, rim, value, previous, outer, inner),
        [(SLAB, NX + 16, NY)],
    )
    times = lax.all_to_all(sent, "tm", 0, 0)
    keep, sent = call(
        ahead_kernel,
        [(SLAB, REALS, WIDE, NY), (SLAB * REALS + 24, WIDE, NY)],
        (times, fields, fields_above, fields_below),
    )
    got = lax.ppermute(sent, "space", cores)
    part = (FIRST, REALS, WIDE, NY)
    chip, up, down = call(gather_kernel, [(CHIP, REALS, WIDE, NY), part, part], (keep, got))
    below = lax.ppermute(up, "space", upward)
    above = lax.ppermute(down, "space", downward)
    cof = call(
        prepare_kernel,
        (REACH, 15, WIDE, NY),
        (fields, fields_above, fields_below, got),
        [(4, 3 * CHIP, WIDE, NY)],
    )
    own = call(
        first_kernel,
        (CHIP, REALS, NARROW, NY),
        (chip, above, below, cof),
        [(16 + WIDE * REALS * REACH, NY)] * 2,
    )
    low = lax.ppermute(own, "space", upward)
    high = lax.ppermute(own, "space", downward)
    mine, theirs = call(
        second_kernel,
        [(SLAB, REALS, OWN, NY)] * 2,
        (chip, above, below, cof, own, high, low),
        [(16 + WIDE * REALS * 3 * CHIP, NY)] * 2,
    )
    theirs = lax.ppermute(theirs, "space", cores)
    correction = call(back_kernel, (WINDOW, SLAB, OWN, NY), (mine, theirs))
    correction = lax.all_to_all(correction, "tm", 0, 0)
    return call(update_kernel, (1, SLAB, NY, NX), (correction, iterate))


def solution(mesh):
    in_specs = (
        P("tm", "space", None, None),
        P("tm", "space", None, None),
        P("space", None, None),
        P(None, "space", None, None),
    )
    out_specs = P("tm", "space", None, None)
    return jax.shard_map(shards, mesh=mesh, in_specs=in_specs, out_specs=out_specs, check_vma=False)
```

time: 281 us -> 102 us (0.36); the launches traced: 277 us -> 102 us
  waiting for transfers between devices: 166 us -> 49.1 us
  starting transfers between devices: 90.4 us -> 21.2 us
  other arithmetic: 18.6 us -> 0 us
  blocking collectives: 0 us -> 17.9 us
  Pallas kernels: 0 us -> 9.33 us
  local copies, waits for them, and re-layouts: 0.67 us -> 3.99 us
    ppermute x25 -> x11, waiting for transfers between devices: 166 us -> 44.1 us  [the longest x1 11.6 us: shards(): lax.ppermute(iterate, 'tm', [(i, (i + 1) % WINDOW) for i in range(WINDOW)])]
    ppermute x25 -> x11, starting transfers between devices: 90.4 us -> 15.5 us  [the longest x1 4.12 us: shards(): below = lax.ppermute(up, 'space', upward)]
    all_to_all x0 -> x1, blocking collectives: none -> 17.9 us  [shards(): correction = lax.all_to_all(correction, 'tm', 0, 0)]
    pallas_call x0 -> x11, Pallas kernels: none -> 9.33 us  [call(): pl.pallas_call(kernel, out_shape=out_shape if several else out_shape[0],...]
    all_to_all x0 -> x1, starting transfers between devices: none -> 5.63 us  [shards(): times = lax.all_to_all(sent, 'tm', 0, 0)]
    all_to_all x0 -> x1, waiting for transfers between devices: none -> 5.07 us  [shards(): times = lax.all_to_all(sent, 'tm', 0, 0)]
    add x8 -> x0, other arithmetic: 4.74 us -> none  [the longest x7 3.95 us: shards(): solved = divide(spectrum + neighbour_sum(coeffs, padded))]
    concatenate x8 -> x0, other arithmetic: 3.89 us -> none  [extended(): block = jnp.concatenate([low, block, high], axis=dim)]
  transfers between devices with their start and end apart: 25 -> 12, of which waited for: 19 -> 8; matrix products, arithmetic and copies ran while one was open for 1% -> 0% of each run, Pallas kernels for 0% -> 4%
where the time goes in v2:
time: 102 us
  waiting for transfers between devices  49.1 us (48%)
  starting transfers between devices  21.2 us (21%)
  blocking collectives  17.9 us (18%)
  Pallas kernels  9.33 us (9%)
  local copies, waits for them, and re-layouts  3.99 us (4%)
    all_to_all x1, blocking collectives, shards(): correction = lax.all_to_all(correction, 'tm', 0, 0)  17.9 us
    ppermute x1, waiting for transfers between devices, shards(): lax.ppermute(iterate, 'tm', [(i, (i + 1) % WINDOW) for i in range(WINDOW)])  11.6 us
    pallas_call x11, Pallas kernels, call(): pl.pallas_call(kernel, out_shape=out_shape if several else out_shape[0],...  9.33 us
    ppermute x1, waiting for transfers between devices, shards(): above = lax.ppermute(down, 'space', downward)  8.68 us
    ppermute x1, waiting for transfers between devices, shards(): fields_below = lax.ppermute(fields, 'space', upward)  8.49 us
    ppermute x1, waiting for transfers between devices, shards(): low = lax.ppermute(own, 'space', upward)  7.51 us
    all_to_all x1, starting transfers between devices, shards(): times = lax.all_to_all(sent, 'tm', 0, 0)  5.63 us
    all_to_all x1, waiting for transfers between devices, shards(): times = lax.all_to_all(sent, 'tm', 0, 0)  5.07 us
  transfers between devices with their start and end apart: 12, of which 8 were waited for; matrix products, arithmetic and copies ran while one was open for 0% of the time, Pallas kernels for 4%

profile of v2, /device:TPU:24, one launch (start us, length us, event | category | flops | bytes accessed | tf_op | source)
XLA Modules:
  0.0 101.6 jit_solution(551228816896245047)
XLA Ops:
  0.0 1.5 %collective-permute-start = (f32[1,2,128,256]{3,2,1,0:T(8,128)}, f32[1,2,128,256]{3,2,1,0:T(8,128)S(1)}, u32[]{:S(2)}, u32[]{:S(2)}) collective-permute-start(f32[1,2,128,256]{3,2,1,0:T(8,128)} %iterate.5), channel_id=1, source_target_pairs={{0,16},{16,32},{32,48},{48,64},{64,80},{80,96},{96,112},{112,128},... | collective-permute-start | bytes 786440 | tf_op jit(solution)/shard_map/ppermute | solution.py:380
  1.5 2.0 %shard_map.47 = (f32[2,128,256]{2,1,0:T(8,128)}, f32[2,128,256]{2,1,0:T(8,128)}) custom-call(f32[1,2,128,256]{3,2,1,0:T(8,128)} %iterate.5, f32[2,128,256]{2,1,0:T(8,128)} %kappa.5), custom_call_target="tpu_custom_call" | custom-call | tf_op jit(solution)/shard_map/pallas_call | solution.py:368
  3.6 1.7 %collective-permute-start.2 = (f32[2,128,256]{2,1,0:T(8,128)}, f32[2,128,256]{2,1,0:T(8,128)S(1)}, u32[]{:S(2)}, u32[]{:S(2)}) collective-permute-start(f32[2,128,256]{2,1,0:T(8,128)} %get-tuple-element.21), channel_id=1, source_target_pairs={{0,1},{1,0},{2,3},{3,2},{4,5},{5,4},{6,7},{7,6},{8,9},{9,8},{10,11... | collective-permute-start | bytes 786440 | tf_op jit(solution)/shard_map/ppermute | solution.py:389
  5.3 1.1 %copy-done = f32[3,2,128,256]{3,2,1,0:T(8,128)S(1)} copy-done((f32[3,2,128,256]{3,2,1,0:T(8,128)S(1)}, f32[3,2,128,256]{3,2,1,0:T(8,128)}, u32[]{:S(2)}) %copy-start) | copy-done | bytes 786456
  6.4 0.9 copy-done.2
  7.3 0.9 copy-done.4
  8.3 0.9 copy-done.6
  9.8 11.6 %collective-permute-done.previous = f32[1,2,128,256]{3,2,1,0:T(8,128)S(1)} collective-permute-done((f32[1,2,128,256]{3,2,1,0:T(8,128)}, f32[1,2,128,256]{3,2,1,0:T(8,128)S(1)}, u32[]{:S(2)}, u32[]{:S(2)}) %collective-permute-start) | collective-permute-done | bytes 262176 | tf_op jit(solution)/shard_map/ppermute | solution.py:380
  21.5 1.0 shard_map.48
  22.5 5.6 %all-to-all-start = ((f32[16,2,32,128]{3,2,1,0:T(8,128)}), f32[16,2,32,128]{3,2,1,0:T(8,128)S(1)}, u32[]{:S(2)}, u32[]{:S(2)}) async-start(f32[16,2,32,128]{3,2,1,0:T(8,128)} %shard_map.48), calls=%async_computation | async-start | bytes 1048576 | tf_op jit(solution)/shard_map/all_to_all | solution.py:406
  28.8 3.9 %collective-permute-start.4 = (f32[4,2,32,128]{3,2,1,0:T(8,128)S(1)}, f32[4,2,32,128]{3,2,1,0:T(8,128)S(1)}, u32[]{:S(2)}, u32[]{:S(2)}) collective-permute-start(f32[4,2,32,128]{3,2,1,0:T(8,128)S(1)} %shard_map.49.fields), channel_id=1, source_target_pairs={{0,2},{1,3},{2,4},{3,5},{4,6},{5,7},{6,8},{7,9},{8,10},{9,11},{10,... | collective-permute-start | bytes 393224 | tf_op jit(solution)/shard_map/ppermute | solution.py:397
  32.8 8.5 %collective-permute-done.4.below = f32[4,2,32,128]{3,2,1,0:T(8,128)S(1)} collective-permute-done((f32[4,2,32,128]{3,2,1,0:T(8,128)S(1)}, f32[4,2,32,128]{3,2,1,0:T(8,128)S(1)}, u32[]{:S(2)}, u32[]{:S(2)}) %collective-permute-start.4) | collective-permute-done | bytes 131104 | tf_op jit(solution)/shard_map/ppermute | solution.py:397
  41.3 5.1 %all-to-all-done.times = f32[16,2,32,128]{3,2,1,0:T(8,128)S(1)} async-done(((f32[16,2,32,128]{3,2,1,0:T(8,128)}), f32[16,2,32,128]{3,2,1,0:T(8,128)S(1)}, u32[]{:S(2)}, u32[]{:S(2)}) %all-to-all-start) | async-done | bytes 524320 | tf_op jit(solution)/shard_map/all_to_all | solution.py:406
  46.6 2.1 %collective-permute-done.5.got = f32[40,32,128]{2,1,0:T(8,128)S(1)} collective-permute-done((f32[40,32,128]{2,1,0:T(8,128)S(1)}, f32[40,32,128]{2,1,0:T(8,128)S(1)}, u32[]{:S(2)}, u32[]{:S(2)}) %collective-permute-start.5) | collective-permute-done | bytes 655392 | tf_op jit(solution)/shard_map/ppermute | solution.py:412
  48.9 4.1 %collective-permute-start.7 = (f32[3,8,32,128]{3,2,1,0:T(8,128)S(1)}, f32[3,8,32,128]{3,2,1,0:T(8,128)S(1)}, u32[]{:S(2)}, u32[]{:S(2)}) collective-permute-start(f32[3,8,32,128]{3,2,1,0:T(8,128)S(1)} %get-tuple-element.26), channel_id=1, source_target_pairs={{0,2},{1,3},{2,4},{3,5},{4,6},{5,7},{6,8},{7,9},{8,10},{9,11},{10,... | collective-permute-start | bytes 1179656 | tf_op jit(solution)/shard_map/ppermute | solution.py:415
  53.4 8.7 %collective-permute-done.6.above = f32[3,8,32,128]{3,2,1,0:T(8,128)S(1)} collective-permute-done((f32[3,8,32,128]{3,2,1,0:T(8,128)S(1)}, f32[3,8,32,128]{3,2,1,0:T(8,128)S(1)}, u32[]{:S(2)}, u32[]{:S(2)}) %collective-permute-start.6) | collective-permute-done | bytes 393248 | tf_op jit(solution)/shard_map/ppermute | solution.py:416
  62.1 1.5 %shard_map.53.own = f32[4,8,24,128]{3,2,1,0:T(8,128)S(1)} custom-call(f32[4,8,32,128]{3,2,1,0:T(8,128)S(1)} %get-tuple-element.24.chip, f32[3,8,32,128]{3,2,1,0:T(8,128)S(1)} %collective-permute-done.6.above, f32[3,8,32,128]{3,2,1,0:T(8,128)S(1)} %collective-permute-done.7.below, f32[10,15,32,128]{3,2,1,0:T(8,128)S(1)} %shard_map.52.cof), custom_call_target="tpu_custom_call" | custom-call | tf_op jit(solution)/shard_map/pallas_call | solution.py:368
  63.6 3.9 %collective-permute-start.9 = (f32[4,8,24,128]{3,2,1,0:T(8,128)S(1)}, f32[4,8,24,128]{3,2,1,0:T(8,128)S(1)}, u32[]{:S(2)}, u32[]{:S(2)}) collective-permute-start(f32[4,8,24,128]{3,2,1,0:T(8,128)S(1)} %shard_map.53.own), channel_id=1, source_target_pairs={{0,2},{1,3},{2,4},{3,5},{4,6},{5,7},{6,8},{7,9},{8,10},{9,11},{10,... | collective-permute-start | bytes 1179656 | tf_op jit(solution)/shard_map/ppermute | solution.py:429
  67.5 7.5 %collective-permute-done.9.low = f32[4,8,24,128]{3,2,1,0:T(8,128)S(1)} collective-permute-done((f32[4,8,24,128]{3,2,1,0:T(8,128)S(1)}, f32[4,8,24,128]{3,2,1,0:T(8,128)S(1)}, u32[]{:S(2)}, u32[]{:S(2)}) %collective-permute-start.9) | collective-permute-done | bytes 393248 | tf_op jit(solution)/shard_map/ppermute | solution.py:429
  75.0 4.3 %collective-permute-done.8.high = f32[4,8,24,128]{3,2,1,0:T(8,128)S(1)} collective-permute-done((f32[4,8,24,128]{3,2,1,0:T(8,128)S(1)}, f32[4,8,24,128]{3,2,1,0:T(8,128)S(1)}, u32[]{:S(2)}, u32[]{:S(2)}) %collective-permute-start.8) | collective-permute-done | bytes 393248 | tf_op jit(solution)/shard_map/ppermute | solution.py:430
  79.3 2.0 %shard_map.54 = (f32[2,8,16,128]{3,2,1,0:T(8,128)S(1)}, f32[2,8,16,128]{3,2,1,0:T(8,128)S(1)}) custom-call(f32[4,8,32,128]{3,2,1,0:T(8,128)S(1)} %get-tuple-element.24.chip, f32[3,8,32,128]{3,2,1,0:T(8,128)S(1)} %collective-permute-done.6.above, f32[3,8,32,128]{3,2,1,0:T(8,128)S(1)} %collective-permute-done.7.below, f32[10,15,32,128]{3,2,1,0:T(8,128)S(1)} %shard_map.52.cof, ...), custom_call_target="tpu_custom_call" | custom-call | tf_op jit(solution)/shard_map/pallas_call | solution.py:368
  81.5 1.3 %collective-permute-done.10.theirs = f32[2,8,16,128]{3,2,1,0:T(8,128)S(1)} collective-permute-done((f32[2,8,16,128]{3,2,1,0:T(8,128)S(1)}, f32[2,8,16,128]{3,2,1,0:T(8,128)S(1)}, u32[]{:S(2)}, u32[]{:S(2)}) %collective-permute-start.10) | collective-permute-done | bytes 131104 | tf_op jit(solution)/shard_map/ppermute | solution.py:437
  82.9 17.9 %all_to_all.10.correction = f32[16,2,16,128]{3,2,1,0:T(8,128)S(1)} all-to-all(f32[16,2,16,128]{3,2,1,0:T(8,128)S(1)} %shard_map.55), channel_id=1, replica_groups=mesh['tm'=16,'space'=16] {'tm'}, dimensions={0} | all-to-all | bytes 524288 | tf_op jit(solution)/shard_map/all_to_all | solution.py:439
  100.8 0.8 shard_map.56
  (26 shorter events, 2.4 us)
Async XLA Ops:
  0.0 21.5 %collective-permute-start = (f32[1,2,128,256]{3,2,1,0:T(8,128)}, f32[1,2,128,256]{3,2,1,0:T(8,128)S(1)}, u32[]{:S(2)}, u32[]{:S(2)}) collective-permute-start(f32[1,2,128,256]{3,2,1,0:T(8,128)} %iterate.5), channel_id=1, source_target_pairs={{0,16},{16,32},{32,48},{48,64},{64,80},{80,96},{96,112},{112,128},... | collective-permute-start | bytes 786440 | tf_op jit(solution)/shard_map/ppermute | solution.py:380
  1.5 26.7 %copy-start.5 = (f32[2,128,256]{2,1,0:T(8,128)S(1)}, f32[2,128,256]{2,1,0:T(8,128)}, u32[]{:S(2)}) copy-start(f32[2,128,256]{2,1,0:T(8,128)} %kappa.5) | copy-start | bytes 786436
  3.5 18.0 %collective-permute-start.1 = (f32[2,128,256]{2,1,0:T(8,128)}, f32[2,128,256]{2,1,0:T(8,128)S(1)}, u32[]{:S(2)}, u32[]{:S(2)}) collective-permute-start(f32[2,128,256]{2,1,0:T(8,128)} %get-tuple-element.20), channel_id=1, source_target_pairs={{1,2},{3,4},{5,6},{7,8},{9,10},{11,12},{13,14},{15,0},{2,1},{4,3},... | collective-permute-start | bytes 786440 | tf_op jit(solution)/shard_map/ppermute | solution.py:388
  3.6 17.9 %collective-permute-start.2 = (f32[2,128,256]{2,1,0:T(8,128)}, f32[2,128,256]{2,1,0:T(8,128)S(1)}, u32[]{:S(2)}, u32[]{:S(2)}) collective-permute-start(f32[2,128,256]{2,1,0:T(8,128)} %get-tuple-element.21), channel_id=1, source_target_pairs={{0,1},{1,0},{2,3},{3,2},{4,5},{5,4},{6,7},{7,6},{8,9},{9,8},{10,11... | collective-permute-start | bytes 786440 | tf_op jit(solution)/shard_map/ppermute | solution.py:389
  5.3 1.1 %copy-start = (f32[3,2,128,256]{3,2,1,0:T(8,128)S(1)}, f32[3,2,128,256]{3,2,1,0:T(8,128)}, u32[]{:S(2)}) copy-start(f32[3,2,128,256]{3,2,1,0:T(8,128)} %velocity.3) | copy-start | bytes 2359300
  6.4 0.9 copy-start.2
  7.3 0.9 copy-start.4
  8.3 0.9 copy-start.6
  9.2 18.9 %copy-start.1 = (f32[3,2,128,256]{3,2,1,0:T(8,128)S(1)}, f32[3,2,128,256]{3,2,1,0:T(8,128)}, u32[]{:S(2)}) copy-start(f32[3,2,128,256]{3,2,1,0:T(8,128)} %velocity.3) | copy-start | bytes 2359300
  22.5 23.8 %all-to-all-start = ((f32[16,2,32,128]{3,2,1,0:T(8,128)}), f32[16,2,32,128]{3,2,1,0:T(8,128)S(1)}, u32[]{:S(2)}, u32[]{:S(2)}) async-start(f32[16,2,32,128]{3,2,1,0:T(8,128)} %shard_map.48), calls=%async_computation | async-start | bytes 1048576 | tf_op jit(solution)/shard_map/all_to_all | solution.py:406
  28.8 12.4 %collective-permute-start.4 = (f32[4,2,32,128]{3,2,1,0:T(8,128)S(1)}, f32[4,2,32,128]{3,2,1,0:T(8,128)S(1)}, u32[]{:S(2)}, u32[]{:S(2)}) collective-permute-start(f32[4,2,32,128]{3,2,1,0:T(8,128)S(1)} %shard_map.49.fields), channel_id=1, source_target_pairs={{0,2},{1,3},{2,4},{3,5},{4,6},{5,7},{6,8},{7,9},{8,10},{9,11},{10,... | collective-permute-start | bytes 393224 | tf_op jit(solution)/shard_map/ppermute | solution.py:397
  32.8 8.5 %collective-permute-start.3 = (f32[4,2,32,128]{3,2,1,0:T(8,128)S(1)}, f32[4,2,32,128]{3,2,1,0:T(8,128)S(1)}, u32[]{:S(2)}, u32[]{:S(2)}) collective-permute-start(f32[4,2,32,128]{3,2,1,0:T(8,128)S(1)} %shard_map.49.fields), channel_id=1, source_target_pairs={{2,0},{3,1},{4,2},{5,3},{6,4},{7,5},{8,6},{9,7},{10,8},{11,9},{12,... | collective-permute-start | bytes 393224 | tf_op jit(solution)/shard_map/ppermute | solution.py:398
  46.5 2.2 %collective-permute-start.5 = (f32[40,32,128]{2,1,0:T(8,128)S(1)}, f32[40,32,128]{2,1,0:T(8,128)S(1)}, u32[]{:S(2)}, u32[]{:S(2)}) collective-permute-start(f32[40,32,128]{2,1,0:T(8,128)S(1)} %get-tuple-element.23), channel_id=1, source_target_pairs={{0,1},{1,0},{2,3},{3,2},{4,5},{5,4},{6,7},{7,6},{8,9},{9,8},{10,11... | collective-permute-start | bytes 1966088 | tf_op jit(solution)/shard_map/ppermute | solution.py:412
  48.8 13.3 %collective-permute-start.6 = (f32[3,8,32,128]{3,2,1,0:T(8,128)S(1)}, f32[3,8,32,128]{3,2,1,0:T(8,128)S(1)}, u32[]{:S(2)}, u32[]{:S(2)}) collective-permute-start(f32[3,8,32,128]{3,2,1,0:T(8,128)S(1)} %get-tuple-element.25), channel_id=1, source_target_pairs={{2,0},{3,1},{4,2},{5,3},{6,4},{7,5},{8,6},{9,7},{10,8},{11,9},{12,... | collective-permute-start | bytes 1179656 | tf_op jit(solution)/shard_map/ppermute | solution.py:416
  48.9 13.2 %collective-permute-start.7 = (f32[3,8,32,128]{3,2,1,0:T(8,128)S(1)}, f32[3,8,32,128]{3,2,1,0:T(8,128)S(1)}, u32[]{:S(2)}, u32[]{:S(2)}) collective-permute-start(f32[3,8,32,128]{3,2,1,0:T(8,128)S(1)} %get-tuple-element.26), channel_id=1, source_target_pairs={{0,2},{1,3},{2,4},{3,5},{4,6},{5,7},{6,8},{7,9},{8,10},{9,11},{10,... | collective-permute-start | bytes 1179656 | tf_op jit(solution)/shard_map/ppermute | solution.py:415
  63.6 37.2 %copy-start.3 = (f32[1,2,128,256]{3,2,1,0:T(8,128)S(1)}, f32[1,2,128,256]{3,2,1,0:T(8,128)}, u32[]{:S(2)}) copy-start(f32[1,2,128,256]{3,2,1,0:T(8,128)} %iterate.5) | copy-start | bytes 786436
  63.6 11.4 %collective-permute-start.9 = (f32[4,8,24,128]{3,2,1,0:T(8,128)S(1)}, f32[4,8,24,128]{3,2,1,0:T(8,128)S(1)}, u32[]{:S(2)}, u32[]{:S(2)}) collective-permute-start(f32[4,8,24,128]{3,2,1,0:T(8,128)S(1)} %shard_map.53.own), channel_id=1, source_target_pairs={{0,2},{1,3},{2,4},{3,5},{4,6},{5,7},{6,8},{7,9},{8,10},{9,11},{10,... | collective-permute-start | bytes 1179656 | tf_op jit(solution)/shard_map/ppermute | solution.py:429
  67.5 11.8 %collective-permute-start.8 = (f32[4,8,24,128]{3,2,1,0:T(8,128)S(1)}, f32[4,8,24,128]{3,2,1,0:T(8,128)S(1)}, u32[]{:S(2)}, u32[]{:S(2)}) collective-permute-start(f32[4,8,24,128]{3,2,1,0:T(8,128)S(1)} %shard_map.53.own), channel_id=1, source_target_pairs={{2,0},{3,1},{4,2},{5,3},{6,4},{7,5},{8,6},{9,7},{10,8},{11,9},{12,... | collective-permute-start | bytes 1179656 | tf_op jit(solution)/shard_map/ppermute | solution.py:430
  81.4 1.4 %collective-permute-start.10 = (f32[2,8,16,128]{3,2,1,0:T(8,128)S(1)}, f32[2,8,16,128]{3,2,1,0:T(8,128)S(1)}, u32[]{:S(2)}, u32[]{:S(2)}) collective-permute-start(f32[2,8,16,128]{3,2,1,0:T(8,128)S(1)} %get-tuple-element.28), channel_id=1, source_target_pairs={{0,1},{1,0},{2,3},{3,2},{4,5},{5,4},{6,7},{7,6},{8,9},{9,8},{10,11... | collective-permute-start | bytes 393224 | tf_op jit(solution)/shard_map/ppermute | solution.py:437

commit v3 on v2

--- a/solution.py
+++ b/solution.py
@@ -1,3 +1,4 @@
+import functools
 import math
 
 import jax
@@ -19,9 +20,12 @@
 CHIP = 4
 CHIPS = NZ // CHIP
 FIRST = 3
+EXTRA = 16
 REACH = 10
 NARROW = OWN + 8
-REALS = 8
+GROUPS = 2
+EACH = 2
+REALS = 4
 
 
 def time_scale(n):
@@ -88,38 +92,41 @@
     return [even[n] + odd[n] for n in range(8)] + [even[n] - odd[n] for n in range(8)]
 
 
-def entry_kernel(iterate, kappa, outer, inner, sems):
-    parity = lax.axis_index("space") % 2
-    copies = [
-        pltpu.make_async_copy(iterate.at[0, parity], outer.at[0], sems.at[0]),
-        pltpu.make_async_copy(kappa.at[parity], outer.at[1], sems.at[1]),
-        pltpu.make_async_copy(iterate.at[0, 1 - parity], inner.at[0], sems.at[2]),
-        pltpu.make_async_copy(kappa.at[1 - parity], inner.at[1], sems.at[3]),
-    ]
+def run_copies(pairs, sems):
+    copies = [pltpu.make_async_copy(source, target, sems.at[i]) for i, (source, target) in enumerate(pairs)]
     for copy in copies:
         copy.start()
-    for copy in copies:
-        copy.wait()
-
-
-def fields_kernel(kappa, velocity, out, held, turned, sems):
+    return copies
+
+
+def entry_kernel(iterate, kappa, velocity, first, second, outer, inner, out, held, turned, sems):
     step = lax.axis_index("tm")
-    copies = [pltpu.make_async_copy(kappa, held.at[0], sems.at[0])]
-    copies += [pltpu.make_async_copy(velocity.at[d], held.at[1 + d], sems.at[1 + d]) for d in range(3)]
-    for copy in copies:
-        copy.start()
+    parity = lax.axis_index("space") % 2
+    pairs = [(kappa, held.at[0])]
+    pairs += [(velocity.at[d], held.at[1 + d]) for d in range(3)]
+    pairs += [
+        (iterate.at[0, 0], first),
+        (iterate.at[0, 1], second),
+        (iterate.at[0, parity], outer.at[0]),
+        (kappa.at[parity], outer.at[1]),
+        (iterate.at[0, 1 - parity], inner.at[0]),
+        (kappa.at[1 - parity], inner.at[1]),
+    ]
+    copies = run_copies(pairs, sems)
     edge = jnp.zeros((8, NY), jnp.float32)
     for field in range(4):
         copies[field].wait()
-        for plane in range(2):
-            spot = turned.at[2 * field + plane]
+        for plane in range(SLAB):
+            spot = turned.at[SLAB * field + plane]
             spot[0:8] = edge
             spot[8 : 8 + NX] = held[field, plane].T
             spot[8 + NX : 16 + NX] = edge
             out[field, plane] = spot[pl.ds(pl.multiple_of(step * OWN, OWN), WIDE), :]
-
-
-def inside_kernel(forcing, iterate, kappa, velocity, base, rim, value):
+    for copy in copies[4:]:
+        copy.wait()
+
+
+def inside_kernel(forcing, iterate, kappa, velocity, base, rim):
     row = lax.broadcasted_iota(jnp.int32, (NY, NX), 0)
     lane = lax.broadcasted_iota(jnp.int32, (NY, NX), 1)
 
@@ -129,7 +136,7 @@
         inside = index < extent - 1 if up else index > 0
         return jnp.where(inside, pltpu.roll(array, extent - 1 if up else 1, dim), 0.0)
 
-    for plane in range(2):
+    for plane in range(SLAB):
         centre, here = kappa[plane], iterate[0, plane]
         towards = -1.0 if plane == 0 else 1.0
         half = 0.5 * velocity[0, plane]
@@ -144,73 +151,95 @@
                 diagonal += face
                 total += (face + sign * half) * shifted(here, dim, up)
         base[plane] = forcing[0, plane] - here * (1.0 / TIME_STEP) - (diagonal * here - total)
-        value[plane] = here
-
-
-def resid_kernel(base, rim, value, previous, outer, inner, out, turned):
+
+
+def resid_kernel(base, rim, iterate, first, second, outer, inner, out, turned):
     step = lax.axis_index("tm")
     place = lax.axis_index("space")
     even = place % 2 == 0
+    leads = step % 4 == 0
     growth = jnp.exp(jnp.full((1, 1), step.astype(jnp.float32) / WINDOW * math.log(ALPHA), jnp.float32))
-    carried = jnp.where(step == 0, 0.0, 1.0 / TIME_STEP)
     edge = jnp.zeros((8, NY), jnp.float32)
-    for plane in range(2):
+
+    def turn(spot, array):
+        spot[0:8] = edge
+        spot[8 : 8 + NX] = array.T
+        spot[8 + NX : 16 + NX] = edge
+
+    before = (first, second)
+    for plane in range(SLAB):
         side, other = (outer, inner) if plane == 0 else (inner, outer)
         ends = place == 0 if plane == 0 else place == 2 * CHIPS - 1
-        here = value[plane]
+        here = iterate[0, plane]
         near = jnp.where(ends, 0.0, jnp.where(even, side[0], other[0]))
         far = jnp.where(ends, 0.0, 0.5 * jnp.where(even, side[1], other[1]))
-        resid = base[plane] + previous[0, plane] * carried + (rim[plane] + far) * near - far * here
-        turned[plane, 0:8] = edge
-        turned[plane, 8 : 8 + NX] = (resid * growth).T
-        turned[plane, 8 + NX : 16 + NX] = edge
+        carried = jnp.where(step == 0 if plane == 0 else leads, 0.0, 1.0 / TIME_STEP)
+        resid = base[plane] + before[plane][...] * carried + (rim[plane] + far) * near - far * here
+        turn(turned.at[plane], resid * growth)
         for c in range(WINDOW):
-            out[c, plane] = turned[plane, OWN * c : OWN * c + WIDE]
-
-
-def ahead_kernel(times, fields, above, below, keep, send):
+            out[c, WIDE * plane : WIDE * (plane + 1)] = turned[plane, OWN * c : OWN * c + WIDE]
+    turn(turned.at[SLAB], jnp.where(leads, second[...], iterate[0, 1]))
+    skip = jnp.where(leads, 0, 8)
+    for c in range(WINDOW):
+        for number in range(2):
+            start = pl.multiple_of(OWN * c + OWN * number + skip, 8)
+            spot = SLAB * WIDE + 8 * number
+            out[c, spot : spot + 8] = turned[SLAB, pl.ds(start, 8)]
+
+
+def ahead_kernel(times, fields, above, below, *outs):
+    keeps, sends = outs[:GROUPS], outs[GROUPS:]
     core = lax.axis_index("space") % 2
     for plane in range(SLAB):
         for tile in range(WIDE // 8):
             rows = slice(8 * tile, 8 * tile + 8)
-            parts = spectrum_of([times[n, plane, rows] for n in range(WINDOW)])
-            for j in range(REALS):
-                p, part = j % 4, j // 4
-                low, high = parts[8 * part + p], parts[8 * part + 4 + p]
-                keep[plane, j, rows] = jnp.where(core == 0, low, high)
-                send[REALS * plane + j, rows] = jnp.where(core == 0, high, low)
+            values = [times[n, WIDE * plane + 8 * tile : WIDE * plane + 8 * tile + 8] for n in range(WINDOW)]
+            if plane == 1:
+                for n in (4, 8, 12):
+                    spot = SLAB * WIDE + 8 * (tile // 2)
+                    source = n - 1 if tile % 2 else n - 4
+                    values[n] += times[source, spot : spot + 8] * (time_scale(n) / TIME_STEP)
+            parts = spectrum_of(values)
+            for group, (keep, send) in enumerate(zip(keeps, sends)):
+                for r in range(REALS):
+                    index = 8 * (r // EACH) + EACH * group + r % EACH
+                    low, high = parts[index], parts[index + 4]
+                    keep[plane, r, rows] = jnp.where(core == 0, low, high)
+                    send[REALS * plane + r, rows] = jnp.where(core == 0, high, low)
     spot = SLAB * REALS
     for source in (below, fields, above):
         for field in range(4):
             for plane in range(SLAB):
-                send[spot] = source[field, plane]
+                sends[-1][spot] = source[field, plane]
                 spot += 1
 
 
 def gather_kernel(keep, got, chip, up, down):
     core = lax.axis_index("space") % 2
-    for j in range(REALS):
+    for r in range(REALS):
         for plane in range(CHIP):
-            mine, theirs = keep[plane % SLAB, j], got[REALS * (plane % SLAB) + j]
+            mine, theirs = keep[plane % SLAB, r], got[REALS * (plane % SLAB) + r]
             value = jnp.where(core == plane // SLAB, mine, theirs)
-            chip[plane, j] = value
+            chip[plane, r] = value
             if plane >= CHIP - FIRST:
-                up[plane - (CHIP - FIRST), j] = value
+                up[plane - (CHIP - FIRST), r] = value
             if plane < FIRST:
-                down[plane, j] = value
-
-
-def back_kernel(mine, theirs, out):
+                down[plane, r] = value
+
+
+def back_kernel(*refs):
+    mines, theirs, out = refs[:GROUPS], refs[GROUPS:-1], refs[-1]
     core = lax.axis_index("space") % 2
     for plane in range(SLAB):
         for tile in range(OWN // 8):
             rows = slice(8 * tile, 8 * tile + 8)
             parts = [None] * 16
-            for j in range(REALS):
-                p, part = j % 4, j // 4
-                one, two = mine[plane, j, rows], theirs[plane, j, rows]
-                parts[8 * part + p] = jnp.where(core == 0, one, two)
-                parts[8 * part + 4 + p] = jnp.where(core == 0, two, one)
+            for group in range(GROUPS):
+                for r in range(REALS):
+                    index = 8 * (r // EACH) + EACH * group + r % EACH
+                    one, two = mines[group][plane, r, rows], theirs[group][plane, r, rows]
+                    parts[index] = jnp.where(core == 0, one, two)
+                    parts[index + 4] = jnp.where(core == 0, two, one)
             values = times_of(parts)
             for n in range(WINDOW):
                 out[n, plane, rows] = values[n] * (time_scale(-n) / WINDOW)
@@ -287,19 +316,19 @@
     return field.at[start : start + WIDE]
 
 
-def sweeps(cof, spec_of, src, dst, planes, shift, finish):
+def sweeps(group, cof, spec_of, src, dst, planes, shift, finish):
     for number, (first, end) in enumerate(planes):
         for z in range(first, end):
             here = z + shift
-            for j in range(4):
+            for j in range(EACH):
                 totals = []
-                for r in (j, 4 + j):
+                for r in (j, EACH + j):
                     centre = part_of(src, here, r)[...]
                     total = cof[z, 0] * part_of(src, here + 1, r)[...] + cof[z, 1] * part_of(src, here - 1, r)[...]
                     total += cof[z, 2] * pltpu.roll(centre, NY - 1, 1) + cof[z, 3] * pltpu.roll(centre, 1, 1)
                     total += cof[z, 4] * part_of(src, here, r, 1)[...] + cof[z, 5] * part_of(src, here, r, -1)[...]
                     totals.append(total + spec_of(z, r))
-                for r, value in zip((j, 4 + j), divide(cof, z, j, *totals)):
+                for r, value in zip((j, EACH + j), divide(cof, z, EACH * group + j, *totals)):
                     if number == len(planes) - 1:
                         finish(z, r, value)
                     else:
@@ -316,23 +345,24 @@
     return spec_of
 
 
-def first_kernel(chip, above, below, cof, out, field_a, field_b):
+def first_kernel(group, chip, above, below, cof, out, field_a, field_b):
     spec_of = spectrum_reader(chip, above, below)
     for field in (field_a, field_b):
         field[0:8] = jnp.zeros((8, NY), jnp.float32)
         field[8 + WIDE * REALS * REACH :] = jnp.zeros((8, NY), jnp.float32)
     for z in range(REACH):
-        for j in range(4):
-            for r, value in zip((j, 4 + j), divide(cof, z, j, spec_of(z, j), spec_of(z, 4 + j))):
+        for j in range(EACH):
+            values = divide(cof, z, EACH * group + j, spec_of(z, j), spec_of(z, EACH + j))
+            for r, value in zip((j, EACH + j), values):
                 part_of(field_a, z, r)[...] = value
 
     def finish(z, r, value):
         out[z - FIRST, r] = value[4 : 4 + NARROW]
 
-    sweeps(cof, spec_of, field_a, field_b, [(1, 9), (2, 8), (3, 7)], 0, finish)
-
-
-def second_kernel(chip, above, below, cof, own, high, low, mine, theirs, field_a, field_b):
+    sweeps(group, cof, spec_of, field_a, field_b, [(1, 9), (2, 8), (3, 7)], 0, finish)
+
+
+def second_kernel(group, chip, above, below, cof, own, high, low, mine, theirs, field_a, field_b):
     core = lax.axis_index("space") % 2
     spec_of = spectrum_reader(chip, above, below)
     for field in (field_a, field_b):
@@ -358,7 +388,7 @@
             mine[plane - SLAB, r] = jnp.where(core == 0, low_value, value)
             theirs[plane - SLAB, r] = jnp.where(core == 0, value, low_value)
 
-    sweeps(cof, spec_of, field_a, field_b, [(0, 10), (1, 9), (2, 8), (3, 7)], 1, finish)
+    sweeps(group, cof, spec_of, field_a, field_b, [(0, 10), (1, 9), (2, 8), (3, 7)], 1, finish)
 
 
 def call(kernel, shapes, args, scratch=(), anywhere=False, mib=32):
@@ -376,66 +406,77 @@
 
 
 def shards(forcing, iterate, kappa, velocity):
-    block = (SLAB, NY, NX)
-    previous = lax.ppermute(iterate, "tm", [(i, (i + 1) % WINDOW) for i in range(WINDOW)])
+    single, block = (NY, NX), (SLAB, NY, NX)
     cores = [(i, i ^ 1) for i in range(2 * CHIPS)]
     upward = [(i, (i + 2) % (2 * CHIPS)) for i in range(2 * CHIPS)]
     downward = [(j, i) for i, j in upward]
-    outer, inner = call(
-        entry_kernel, [block, block], (iterate, kappa), [pltpu.SemaphoreType.DMA((4,))], anywhere=True, mib=56
-    )
     facing = [(i, (i + 1) % (2 * CHIPS)) for i in range(1, 2 * CHIPS, 2)]
-    outer = lax.ppermute(outer, "space", facing + [(j, i) for i, j in facing])
+    facing += [(j, i) for i, j in facing]
+    first, second, outer, inner, fields = call(
+        entry_kernel,
+        [single, single, block, block, (4, SLAB, WIDE, NY)],
+        (iterate, kappa, velocity),
+        [(4, *block), (8, NX + 16, NY), pltpu.SemaphoreType.DMA((10,))],
+        anywhere=True,
+        mib=56,
+    )
+    first = lax.ppermute(first, "tm", [(i, (i + 1) % WINDOW) for i in range(WINDOW)])
+    second = lax.ppermute(second, "tm", [(i, i // 4 * 4 + (i + 1) % 4) for i in range(WINDOW)])
+    outer = lax.ppermute(outer, "space", facing)
     inner = lax.ppermute(inner, "space", cores)
-    fields = call(
-        fields_kernel,
-        (4, SLAB, WIDE, NY),
-        (kappa, velocity),
-        [(4, SLAB, NY, NX), (8, NX + 16, NY), pltpu.SemaphoreType.DMA((4,))],
-        anywhere=True,
-    )
     fields_below = lax.ppermute(fields, "space", upward)
     fields_above = lax.ppermute(fields, "space", downward)
-    base, rim, value = call(inside_kernel, [block] * 3, (forcing, iterate, kappa, velocity))
+    base, rim = call(inside_kernel, [block, block], (forcing, iterate, kappa, velocity))
+    first, fields_below, fields_above = lax.optimization_barrier((first, fields_below, fields_above))
     sent = call(
         resid_kernel,
-        (WINDOW, SLAB, WIDE, NY),
-        (base, rim, value, previous, outer, inner),
-        [(SLAB, NX + 16, NY)],
+        (WINDOW, SLAB * WIDE + EXTRA, NY),
+        (base, rim, iterate, first, second, outer, inner),
+        [(SLAB + 1, NX + 16, NY)],
     )
     times = lax.all_to_all(sent, "tm", 0, 0)
-    keep, sent = call(
+    parts = call(
         ahead_kernel,
-        [(SLAB, REALS, WIDE, NY), (SLAB * REALS + 24, WIDE, NY)],
+        [(SLAB, REALS, WIDE, NY)] * GROUPS
+        + [(SLAB * REALS + (24 if group == GROUPS - 1 else 0), WIDE, NY) for group in range(GROUPS)],
         (times, fields, fields_above, fields_below),
     )
-    got = lax.ppermute(sent, "space", cores)
-    part = (FIRST, REALS, WIDE, NY)
-    chip, up, down = call(gather_kernel, [(CHIP, REALS, WIDE, NY), part, part], (keep, got))
-    below = lax.ppermute(up, "space", upward)
-    above = lax.ppermute(down, "space", downward)
+    got = [lax.ppermute(sent, "space", cores) for sent in parts[GROUPS:]]
+    chips, aboves, belows = [], [], []
+    for group in range(GROUPS):
+        shape = (FIRST, REALS, WIDE, NY)
+        chip, up, down = call(gather_kernel, [(CHIP, REALS, WIDE, NY), shape, shape], (parts[group], got[group]))
+        chips.append(chip)
+        belows.append(lax.ppermute(up, "space", upward))
+        aboves.append(lax.ppermute(down, "space", downward))
     cof = call(
         prepare_kernel,
         (REACH, 15, WIDE, NY),
-        (fields, fields_above, fields_below, got),
+        (fields, fields_above, fields_below, got[-1]),
         [(4, 3 * CHIP, WIDE, NY)],
     )
-    own = call(
-        first_kernel,
-        (CHIP, REALS, NARROW, NY),
-        (chip, above, below, cof),
-        [(16 + WIDE * REALS * REACH, NY)] * 2,
-    )
-    low = lax.ppermute(own, "space", upward)
-    high = lax.ppermute(own, "space", downward)
-    mine, theirs = call(
-        second_kernel,
-        [(SLAB, REALS, OWN, NY)] * 2,
-        (chip, above, below, cof, own, high, low),
-        [(16 + WIDE * REALS * 3 * CHIP, NY)] * 2,
-    )
-    theirs = lax.ppermute(theirs, "space", cores)
-    correction = call(back_kernel, (WINDOW, SLAB, OWN, NY), (mine, theirs))
+    owns, lows, highs = [], [], []
+    for group in range(GROUPS):
+        own = call(
+            functools.partial(first_kernel, group),
+            (CHIP, REALS, NARROW, NY),
+            (chips[group], aboves[group], belows[group], cof),
+            [(16 + WIDE * REALS * REACH, NY)] * 2,
+        )
+        owns.append(own)
+        lows.append(lax.ppermute(own, "space", upward))
+        highs.append(lax.ppermute(own, "space", downward))
+    mines, theirs = [], []
+    for group in range(GROUPS):
+        mine, other = call(
+            functools.partial(second_kernel, group),
+            [(SLAB, REALS, OWN, NY)] * 2,
+            (chips[group], aboves[group], belows[group], cof, owns[group], highs[group], lows[group]),
+            [(16 + WIDE * REALS * 3 * CHIP, NY)] * 2,
+        )
+        mines.append(mine)
+        theirs.append(lax.ppermute(other, "space", cores))
+    correction = call(back_kernel, (WINDOW, SLAB, OWN, NY), (*mines, *theirs))
     correction = lax.all_to_all(correction, "tm", 0, 0)
     return call(update_kernel, (1, SLAB, NY, NX), (correction, iterate))
 

time: 102 us -> 95.9 us (0.940)
  the two profiles are of different devices: /device:TPU:24 before, /device:TPU:32 now
where the time goes in v3:
time: 95.9 us; the launch traced here: 95.6 us
  blocking collectives  40.7 us (42%)
  starting transfers between devices  23.5 us (25%)
  waiting for transfers between devices  18.8 us (20%)
  Pallas kernels  8.45 us (9%)
  local copies, waits for them, and re-layouts  3.99 us (4%)
    all_to_all x1, blocking collectives, shards(): times = lax.all_to_all(sent, 'tm', 0, 0)  23.6 us
    all_to_all x1, blocking collectives, shards(): correction = lax.all_to_all(correction, 'tm', 0, 0)  17.1 us
    ppermute x2, starting transfers between devices, shards(): aboves.append(lax.ppermute(down, 'space', downward))  9.61 us
    pallas_call x13, Pallas kernels, call(): pl.pallas_call(kernel, out_shape=out_shape if several else out_shape[0],...  8.45 us
    ppermute x2, waiting for transfers between devices, shards(): belows.append(lax.ppermute(up, 'space', upward))  5.25 us
    ppermute x2, waiting for transfers between devices, shards(): lows.append(lax.ppermute(own, 'space', upward))  5.19 us
    unnamed x12, local copies, waits for them, and re-layouts  3.99 us
    ppermute x1, waiting for transfers between devices, shards(): lax.ppermute(first, 'tm', [(i, (i + 1) % WINDOW) for i in range(WINDOW)])  2.88 us
  transfers between devices with their start and end apart: 18, of which 12 were waited for; matrix products, arithmetic and copies ran while one was open for 0% of the time, Pallas kernels for 5%

profile of v3, /device:TPU:32, one launch (start us, length us, event | category | flops | bytes accessed | tf_op | source)
XLA Modules:
  0.0 95.6 jit_solution(3680923135197971023)
XLA Ops:
  0.0 2.5 %shard_map.47 = (f32[128,256]{1,0:T(8,128)}, f32[128,256]{1,0:T(8,128)}, f32[2,128,256]{2,1,0:T(8,128)}, f32[2,128,256]{2,1,0:T(8,128)}, f32[4,2,32,128]{3,2,1,0:T(8,128)}) custom-call(f32[1,2,128,256]{3,2,1,0:T(8,128)} %iterate.7, f32[2,128,256]{2,1,0:T(8,128)} %kappa.3, f32[3,2,128,256]{3,2,1,0:T(8,128)} %velocity.3), custom_call_target="tpu_custom_call" | custom-call | tf_op jit(solution)/shard_map/pallas_call | solution.py:398
  2.6 1.7 %collective-permute-start.1 = (f32[4,2,32,128]{3,2,1,0:T(8,128)}, f32[4,2,32,128]{3,2,1,0:T(8,128)S(1)}, u32[]{:S(2)}, u32[]{:S(2)}) collective-permute-start(f32[4,2,32,128]{3,2,1,0:T(8,128)} %get-tuple-element.32.fields), channel_id=1, source_target_pairs={{0,2},{1,3},{2,4},{3,5},{4,6},{5,7},{6,8},{7,9},{8,10},{9,11},{10,... | collective-permute-start | bytes 393224 | tf_op jit(solution)/shard_map/ppermute | solution.py:427
  4.2 1.7 %collective-permute-start.4 = (f32[2,128,256]{2,1,0:T(8,128)}, f32[2,128,256]{2,1,0:T(8,128)S(1)}, u32[]{:S(2)}, u32[]{:S(2)}) collective-permute-start(f32[2,128,256]{2,1,0:T(8,128)} %get-tuple-element.35), channel_id=1, source_target_pairs={{1,2},{3,4},{5,6},{7,8},{9,10},{11,12},{13,14},{15,0},{2,1},{4,3},... | collective-permute-start | bytes 786440 | tf_op jit(solution)/shard_map/ppermute | solution.py:425
  5.9 2.5 %collective-permute-start.2 = (f32[4,2,32,128]{3,2,1,0:T(8,128)}, f32[4,2,32,128]{3,2,1,0:T(8,128)S(1)}, u32[]{:S(2)}, u32[]{:S(2)}) collective-permute-start(f32[4,2,32,128]{3,2,1,0:T(8,128)} %get-tuple-element.32.fields), channel_id=1, source_target_pairs={{2,0},{3,1},{4,2},{5,3},{6,4},{7,5},{8,6},{9,7},{10,8},{11,9},{12,... | collective-permute-start | bytes 393224 | tf_op jit(solution)/shard_map/ppermute | solution.py:428
  8.5 1.5 %collective-permute-start = (f32[128,256]{1,0:T(8,128)}, f32[128,256]{1,0:T(8,128)S(1)}, u32[]{:S(2)}, u32[]{:S(2)}) collective-permute-start(f32[128,256]{1,0:T(8,128)} %get-tuple-element.31), channel_id=1, source_target_pairs={{0,16},{16,32},{32,48},{48,64},{64,80},{80,96},{96,112},{112,128},... | collective-permute-start | bytes 393224 | tf_op jit(solution)/shard_map/ppermute | solution.py:423
  10.9 1.5 %collective-permute-start.3 = (f32[128,256]{1,0:T(8,128)}, f32[128,256]{1,0:T(8,128)S(1)}, u32[]{:S(2)}, u32[]{:S(2)}) collective-permute-start(f32[128,256]{1,0:T(8,128)} %get-tuple-element.34), channel_id=1, source_target_pairs={{0,16},{16,32},{32,48},{48,0},{64,80},{80,96},{96,112},{112,64},{1... | collective-permute-start | bytes 393224 | tf_op jit(solution)/shard_map/ppermute | solution.py:424
  12.3 0.9 copy-done
  13.3 1.1 %copy-done.2 = f32[3,2,128,256]{3,2,1,0:T(8,128)S(1)} copy-done((f32[3,2,128,256]{3,2,1,0:T(8,128)S(1)}, f32[3,2,128,256]{3,2,1,0:T(8,128)}, u32[]{:S(2)}) %copy-start.2) | copy-done | bytes 786456
  14.4 0.9 copy-done.3
  15.4 0.9 copy-done.5
  17.0 2.9 %collective-permute-done.first = f32[128,256]{1,0:T(8,128)S(1)} collective-permute-done((f32[128,256]{1,0:T(8,128)}, f32[128,256]{1,0:T(8,128)S(1)}, u32[]{:S(2)}, u32[]{:S(2)}) %collective-permute-start) | collective-permute-done | bytes 131104 | tf_op jit(solution)/shard_map/ppermute | solution.py:423
  20.8 23.6 %all_to_all.10.times = f32[16,80,128]{2,1,0:T(8,128)S(1)} all-to-all(f32[16,80,128]{2,1,0:T(8,128)S(1)} %shard_map.48), channel_id=1, replica_groups=mesh['tm'=16,'space'=16] {'tm'}, dimensions={0} | all-to-all | bytes 1310720 | tf_op jit(solution)/shard_map/all_to_all | solution.py:437
  45.1 1.6 %collective-permute-done.6.got = f32[8,32,128]{2,1,0:T(8,128)S(1)} collective-permute-done((f32[8,32,128]{2,1,0:T(8,128)S(1)}, f32[8,32,128]{2,1,0:T(8,128)S(1)}, u32[]{:S(2)}, u32[]{:S(2)}) %collective-permute-start.6) | collective-permute-done | bytes 131104 | tf_op jit(solution)/shard_map/ppermute | solution.py:444
  46.8 5.4 %collective-permute-start.7 = (f32[3,4,32,128]{3,2,1,0:T(8,128)S(1)}, f32[3,4,32,128]{3,2,1,0:T(8,128)S(1)}, u32[]{:S(2)}, u32[]{:S(2)}) collective-permute-start(f32[3,4,32,128]{3,2,1,0:T(8,128)S(1)} %get-tuple-element.42), channel_id=1, source_target_pairs={{2,0},{3,1},{4,2},{5,3},{6,4},{7,5},{8,6},{9,7},{10,8},{11,9},{12,... | collective-permute-start | bytes 589832 | tf_op jit(solution)/shard_map/ppermute | solution.py:451
  52.2 4.2 %collective-permute-start.12 = (f32[3,4,32,128]{3,2,1,0:T(8,128)S(1)}, f32[3,4,32,128]{3,2,1,0:T(8,128)S(1)}, u32[]{:S(2)}, u32[]{:S(2)}) collective-permute-start(f32[3,4,32,128]{3,2,1,0:T(8,128)S(1)} %get-tuple-element.48), channel_id=1, source_target_pairs={{2,0},{3,1},{4,2},{5,3},{6,4},{7,5},{8,6},{9,7},{10,8},{11,9},{12,... | collective-permute-start | bytes 589832 | tf_op jit(solution)/shard_map/ppermute | solution.py:451
  57.0 4.3 %collective-permute-done.8.below = f32[3,4,32,128]{3,2,1,0:T(8,128)S(1)} collective-permute-done((f32[3,4,32,128]{3,2,1,0:T(8,128)S(1)}, f32[3,4,32,128]{3,2,1,0:T(8,128)S(1)}, u32[]{:S(2)}, u32[]{:S(2)}) %collective-permute-start.8) | collective-permute-done | bytes 196640 | tf_op jit(solution)/shard_map/ppermute | solution.py:450
  62.5 1.7 %collective-permute-start.11 = (f32[4,4,24,128]{3,2,1,0:T(8,128)S(1)}, f32[4,4,24,128]{3,2,1,0:T(8,128)S(1)}, u32[]{:S(2)}, u32[]{:S(2)}) collective-permute-start(f32[4,4,24,128]{3,2,1,0:T(8,128)S(1)} %shard_map.52.own), channel_id=1, source_target_pairs={{0,2},{1,3},{2,4},{3,5},{4,6},{5,7},{6,8},{7,9},{8,10},{9,11},{10,... | collective-permute-start | bytes 589832 | tf_op jit(solution)/shard_map/ppermute | solution.py:467
  65.9 1.5 %collective-permute-start.14 = (f32[4,4,24,128]{3,2,1,0:T(8,128)S(1)}, f32[4,4,24,128]{3,2,1,0:T(8,128)S(1)}, u32[]{:S(2)}, u32[]{:S(2)}) collective-permute-start(f32[4,4,24,128]{3,2,1,0:T(8,128)S(1)} %shard_map.55.own), channel_id=1, source_target_pairs={{2,0},{3,1},{4,2},{5,3},{6,4},{7,5},{8,6},{9,7},{10,8},{11,9},{12,... | collective-permute-start | bytes 589832 | tf_op jit(solution)/shard_map/ppermute | solution.py:468
  68.2 2.0 %collective-permute-done.11.low = f32[4,4,24,128]{3,2,1,0:T(8,128)S(1)} collective-permute-done((f32[4,4,24,128]{3,2,1,0:T(8,128)S(1)}, f32[4,4,24,128]{3,2,1,0:T(8,128)S(1)}, u32[]{:S(2)}, u32[]{:S(2)}) %collective-permute-start.11) | collective-permute-done | bytes 196640 | tf_op jit(solution)/shard_map/ppermute | solution.py:467
  70.3 1.0 %shard_map.53 = (f32[2,4,16,128]{3,2,1,0:T(8,128)S(1)}, f32[2,4,16,128]{3,2,1,0:T(8,128)S(1)}) custom-call(f32[4,4,32,128]{3,2,1,0:T(8,128)S(1)} %get-tuple-element.41.chip, f32[3,4,32,128]{3,2,1,0:T(8,128)S(1)} %collective-permute-done.7.above, f32[3,4,32,128]{3,2,1,0:T(8,128)S(1)} %collective-permute-done.8.below, f32[10,15,32,128]{3,2,1,0:T(8,128)S(1)} %shard_map.51.cof, ...), custom_call_target="tpu_custom_call" | custom-call | tf_op jit(solution)/shard_map/pallas_call | solution.py:398
  72.1 3.1 %collective-permute-done.15.low = f32[4,4,24,128]{3,2,1,0:T(8,128)S(1)} collective-permute-done((f32[4,4,24,128]{3,2,1,0:T(8,128)S(1)}, f32[4,4,24,128]{3,2,1,0:T(8,128)S(1)}, u32[]{:S(2)}, u32[]{:S(2)}) %collective-permute-start.15) | collective-permute-done | bytes 196640 | tf_op jit(solution)/shard_map/ppermute | solution.py:467
  75.2 1.0 %shard_map.56 = (f32[2,4,16,128]{3,2,1,0:T(8,128)S(1)}, f32[2,4,16,128]{3,2,1,0:T(8,128)S(1)}) custom-call(f32[4,4,32,128]{3,2,1,0:T(8,128)S(1)} %get-tuple-element.47.chip, f32[3,4,32,128]{3,2,1,0:T(8,128)S(1)} %collective-permute-done.12.above, f32[3,4,32,128]{3,2,1,0:T(8,128)S(1)} %collective-permute-done.13.below, ...), custom_call_target="tpu_custom_call" | custom-call | tf_op jit(solution)/shard_map/pallas_call | solution.py:398
  76.3 1.2 %collective-permute-done.17.refs_3_ = f32[2,4,16,128]{3,2,1,0:T(8,128)S(1)} collective-permute-done((f32[2,4,16,128]{3,2,1,0:T(8,128)S(1)}, f32[2,4,16,128]{3,2,1,0:T(8,128)S(1)}, u32[]{:S(2)}, u32[]{:S(2)}) %collective-permute-start.17) | collective-permute-done | bytes 65568 | tf_op jit(solution)/shard_map/ppermute | solution.py:478
  77.6 17.1 %all_to_all.11.correction = f32[16,2,16,128]{3,2,1,0:T(8,128)S(1)} all-to-all(f32[16,2,16,128]{3,2,1,0:T(8,128)S(1)} %shard_map.57), channel_id=1, replica_groups=mesh['tm'=16,'space'=16] {'tm'}, dimensions={0} | all-to-all | bytes 524288 | tf_op jit(solution)/shard_map/all_to_all | solution.py:480
  (39 shorter events, 9.3 us)
Async XLA Ops:
  0.0 20.5 %copy-start.1 = (f32[1,2,128,256]{3,2,1,0:T(8,128)S(1)}, f32[1,2,128,256]{3,2,1,0:T(8,128)}, u32[]{:S(2)}) copy-start(f32[1,2,128,256]{3,2,1,0:T(8,128)} %iterate.7) | copy-start | bytes 786436
  2.6 8.3 %collective-permute-start.1 = (f32[4,2,32,128]{3,2,1,0:T(8,128)}, f32[4,2,32,128]{3,2,1,0:T(8,128)S(1)}, u32[]{:S(2)}, u32[]{:S(2)}) collective-permute-start(f32[4,2,32,128]{3,2,1,0:T(8,128)} %get-tuple-element.32.fields), channel_id=1, source_target_pairs={{0,2},{1,3},{2,4},{3,5},{4,6},{5,7},{6,8},{7,9},{8,10},{9,11},{10,... | collective-permute-start | bytes 393224 | tf_op jit(solution)/shard_map/ppermute | solution.py:427
  4.2 16.3 %collective-permute-start.4 = (f32[2,128,256]{2,1,0:T(8,128)}, f32[2,128,256]{2,1,0:T(8,128)S(1)}, u32[]{:S(2)}, u32[]{:S(2)}) collective-permute-start(f32[2,128,256]{2,1,0:T(8,128)} %get-tuple-element.35), channel_id=1, source_target_pairs={{1,2},{3,4},{5,6},{7,8},{9,10},{11,12},{13,14},{15,0},{2,1},{4,3},... | collective-permute-start | bytes 786440 | tf_op jit(solution)/shard_map/ppermute | solution.py:425
  5.9 14.6 %collective-permute-start.5 = (f32[2,128,256]{2,1,0:T(8,128)}, f32[2,128,256]{2,1,0:T(8,128)S(1)}, u32[]{:S(2)}, u32[]{:S(2)}) collective-permute-start(f32[2,128,256]{2,1,0:T(8,128)} %get-tuple-element.36), channel_id=1, source_target_pairs={{0,1},{1,0},{2,3},{3,2},{4,5},{5,4},{6,7},{7,6},{8,9},{9,8},{10,11... | collective-permute-start | bytes 786440 | tf_op jit(solution)/shard_map/ppermute | solution.py:426
  5.9 11.0 %collective-permute-start.2 = (f32[4,2,32,128]{3,2,1,0:T(8,128)}, f32[4,2,32,128]{3,2,1,0:T(8,128)S(1)}, u32[]{:S(2)}, u32[]{:S(2)}) collective-permute-start(f32[4,2,32,128]{3,2,1,0:T(8,128)} %get-tuple-element.32.fields), channel_id=1, source_target_pairs={{2,0},{3,1},{4,2},{5,3},{6,4},{7,5},{8,6},{9,7},{10,8},{11,9},{12,... | collective-permute-start | bytes 393224 | tf_op jit(solution)/shard_map/ppermute | solution.py:428
  8.5 11.4 %collective-permute-start = (f32[128,256]{1,0:T(8,128)}, f32[128,256]{1,0:T(8,128)S(1)}, u32[]{:S(2)}, u32[]{:S(2)}) collective-permute-start(f32[128,256]{1,0:T(8,128)} %get-tuple-element.31), channel_id=1, source_target_pairs={{0,16},{16,32},{32,48},{48,64},{64,80},{80,96},{96,112},{112,128},... | collective-permute-start | bytes 393224 | tf_op jit(solution)/shard_map/ppermute | solution.py:423
  10.9 9.7 %collective-permute-start.3 = (f32[128,256]{1,0:T(8,128)}, f32[128,256]{1,0:T(8,128)S(1)}, u32[]{:S(2)}, u32[]{:S(2)}) collective-permute-start(f32[128,256]{1,0:T(8,128)} %get-tuple-element.34), channel_id=1, source_target_pairs={{0,16},{16,32},{32,48},{48,0},{64,80},{80,96},{96,112},{112,64},{1... | collective-permute-start | bytes 393224 | tf_op jit(solution)/shard_map/ppermute | solution.py:424
  12.3 0.9 copy-start
  13.3 1.1 %copy-start.2 = (f32[3,2,128,256]{3,2,1,0:T(8,128)S(1)}, f32[3,2,128,256]{3,2,1,0:T(8,128)}, u32[]{:S(2)}) copy-start(f32[3,2,128,256]{3,2,1,0:T(8,128)} %velocity.3) | copy-start | bytes 2359300
  14.4 0.9 copy-start.3
  15.4 0.9 copy-start.5
  16.3 28.1 %copy-start.4 = (f32[4,2,32,128]{3,2,1,0:T(8,128)S(1)}, f32[4,2,32,128]{3,2,1,0:T(8,128)}, u32[]{:S(2)}) copy-start(f32[4,2,32,128]{3,2,1,0:T(8,128)} %get-tuple-element.32.fields) | copy-start | bytes 393220
  44.5 7.6 %collective-permute-start.9 = (f32[32,32,128]{2,1,0:T(8,128)S(1)}, f32[32,32,128]{2,1,0:T(8,128)S(1)}, u32[]{:S(2)}, u32[]{:S(2)}) collective-permute-start(f32[32,32,128]{2,1,0:T(8,128)S(1)} %get-tuple-element.44), channel_id=1, source_target_pairs={{0,1},{1,0},{2,3},{3,2},{4,5},{5,4},{6,7},{7,6},{8,9},{9,8},{10,11... | collective-permute-start | bytes 1572872 | tf_op jit(solution)/shard_map/ppermute | solution.py:444
  44.6 2.1 %collective-permute-start.6 = (f32[8,32,128]{2,1,0:T(8,128)S(1)}, f32[8,32,128]{2,1,0:T(8,128)S(1)}, u32[]{:S(2)}, u32[]{:S(2)}) collective-permute-start(f32[8,32,128]{2,1,0:T(8,128)S(1)} %get-tuple-element.40), channel_id=1, source_target_pairs={{0,1},{1,0},{2,3},{3,2},{4,5},{5,4},{6,7},{7,6},{8,9},{9,8},{10,11... | collective-permute-start | bytes 393224 | tf_op jit(solution)/shard_map/ppermute | solution.py:444
  46.8 10.3 %collective-permute-start.7 = (f32[3,4,32,128]{3,2,1,0:T(8,128)S(1)}, f32[3,4,32,128]{3,2,1,0:T(8,128)S(1)}, u32[]{:S(2)}, u32[]{:S(2)}) collective-permute-start(f32[3,4,32,128]{3,2,1,0:T(8,128)S(1)} %get-tuple-element.42), channel_id=1, source_target_pairs={{2,0},{3,1},{4,2},{5,3},{6,4},{7,5},{8,6},{9,7},{10,8},{11,9},{12,... | collective-permute-start | bytes 589832 | tf_op jit(solution)/shard_map/ppermute | solution.py:451
  52.2 9.2 %collective-permute-start.8 = (f32[3,4,32,128]{3,2,1,0:T(8,128)S(1)}, f32[3,4,32,128]{3,2,1,0:T(8,128)S(1)}, u32[]{:S(2)}, u32[]{:S(2)}) collective-permute-start(f32[3,4,32,128]{3,2,1,0:T(8,128)S(1)} %get-tuple-element.43), channel_id=1, source_target_pairs={{0,2},{1,3},{2,4},{3,5},{4,6},{5,7},{6,8},{7,9},{8,10},{9,11},{10,... | collective-permute-start | bytes 589832 | tf_op jit(solution)/shard_map/ppermute | solution.py:450
  52.2 12.0 %collective-permute-start.12 = (f32[3,4,32,128]{3,2,1,0:T(8,128)S(1)}, f32[3,4,32,128]{3,2,1,0:T(8,128)S(1)}, u32[]{:S(2)}, u32[]{:S(2)}) collective-permute-start(f32[3,4,32,128]{3,2,1,0:T(8,128)S(1)} %get-tuple-element.48), channel_id=1, source_target_pairs={{2,0},{3,1},{4,2},{5,3},{6,4},{7,5},{8,6},{9,7},{10,8},{11,9},{12,... | collective-permute-start | bytes 589832 | tf_op jit(solution)/shard_map/ppermute | solution.py:451
  56.4 8.7 %collective-permute-start.13 = (f32[3,4,32,128]{3,2,1,0:T(8,128)S(1)}, f32[3,4,32,128]{3,2,1,0:T(8,128)S(1)}, u32[]{:S(2)}, u32[]{:S(2)}) collective-permute-start(f32[3,4,32,128]{3,2,1,0:T(8,128)S(1)} %get-tuple-element.49), channel_id=1, source_target_pairs={{0,2},{1,3},{2,4},{3,5},{4,6},{5,7},{6,8},{7,9},{8,10},{9,11},{10,... | collective-permute-start | bytes 589832 | tf_op jit(solution)/shard_map/ppermute | solution.py:450
  62.1 6.1 %collective-permute-start.10 = (f32[4,4,24,128]{3,2,1,0:T(8,128)S(1)}, f32[4,4,24,128]{3,2,1,0:T(8,128)S(1)}, u32[]{:S(2)}, u32[]{:S(2)}) collective-permute-start(f32[4,4,24,128]{3,2,1,0:T(8,128)S(1)} %shard_map.52.own), channel_id=1, source_target_pairs={{2,0},{3,1},{4,2},{5,3},{6,4},{7,5},{8,6},{9,7},{10,8},{11,9},{12,... | collective-permute-start | bytes 589832 | tf_op jit(solution)/shard_map/ppermute | solution.py:468
  62.5 7.8 %collective-permute-start.11 = (f32[4,4,24,128]{3,2,1,0:T(8,128)S(1)}, f32[4,4,24,128]{3,2,1,0:T(8,128)S(1)}, u32[]{:S(2)}, u32[]{:S(2)}) collective-permute-start(f32[4,4,24,128]{3,2,1,0:T(8,128)S(1)} %shard_map.52.own), channel_id=1, source_target_pairs={{0,2},{1,3},{2,4},{3,5},{4,6},{5,7},{6,8},{7,9},{8,10},{9,11},{10,... | collective-permute-start | bytes 589832 | tf_op jit(solution)/shard_map/ppermute | solution.py:467
  65.9 6.2 %collective-permute-start.14 = (f32[4,4,24,128]{3,2,1,0:T(8,128)S(1)}, f32[4,4,24,128]{3,2,1,0:T(8,128)S(1)}, u32[]{:S(2)}, u32[]{:S(2)}) collective-permute-start(f32[4,4,24,128]{3,2,1,0:T(8,128)S(1)} %shard_map.55.own), channel_id=1, source_target_pairs={{2,0},{3,1},{4,2},{5,3},{6,4},{7,5},{8,6},{9,7},{10,8},{11,9},{12,... | collective-permute-start | bytes 589832 | tf_op jit(solution)/shard_map/ppermute | solution.py:468
  67.4 7.8 %collective-permute-start.15 = (f32[4,4,24,128]{3,2,1,0:T(8,128)S(1)}, f32[4,4,24,128]{3,2,1,0:T(8,128)S(1)}, u32[]{:S(2)}, u32[]{:S(2)}) collective-permute-start(f32[4,4,24,128]{3,2,1,0:T(8,128)S(1)} %shard_map.55.own), channel_id=1, source_target_pairs={{0,2},{1,3},{2,4},{3,5},{4,6},{5,7},{6,8},{7,9},{8,10},{9,11},{10,... | collective-permute-start | bytes 589832 | tf_op jit(solution)/shard_map/ppermute | solution.py:467
  71.3 5.1 %collective-permute-start.16 = (f32[2,4,16,128]{3,2,1,0:T(8,128)S(1)}, f32[2,4,16,128]{3,2,1,0:T(8,128)S(1)}, u32[]{:S(2)}, u32[]{:S(2)}) collective-permute-start(f32[2,4,16,128]{3,2,1,0:T(8,128)S(1)} %get-tuple-element.51), channel_id=1, source_target_pairs={{0,1},{1,0},{2,3},{3,2},{4,5},{5,4},{6,7},{7,6},{8,9},{9,8},{10,11... | collective-permute-start | bytes 196616 | tf_op jit(solution)/shard_map/ppermute | solution.py:478
  76.2 1.3 %collective-permute-start.17 = (f32[2,4,16,128]{3,2,1,0:T(8,128)S(1)}, f32[2,4,16,128]{3,2,1,0:T(8,128)S(1)}, u32[]{:S(2)}, u32[]{:S(2)}) collective-permute-start(f32[2,4,16,128]{3,2,1,0:T(8,128)S(1)} %get-tuple-element.52), channel_id=1, source_target_pairs={{0,1},{1,0},{2,3},{3,2},{4,5},{5,4},{6,7},{7,6},{8,9},{9,8},{10,11... | collective-permute-start | bytes 196616 | tf_op jit(solution)/shard_map/ppermute | solution.py:478

commit v4 on v3

--- a/solution.py
+++ b/solution.py
@@ -99,14 +99,12 @@
     return copies
 
 
-def entry_kernel(iterate, kappa, velocity, first, second, outer, inner, out, held, turned, sems):
+def entry_kernel(iterate, kappa, velocity, outer, inner, out, held, turned, sems):
     step = lax.axis_index("tm")
     parity = lax.axis_index("space") % 2
     pairs = [(kappa, held.at[0])]
     pairs += [(velocity.at[d], held.at[1 + d]) for d in range(3)]
     pairs += [
-        (iterate.at[0, 0], first),
-        (iterate.at[0, 1], second),
         (iterate.at[0, parity], outer.at[0]),
         (kappa.at[parity], outer.at[1]),
         (iterate.at[0, 1 - parity], inner.at[0]),
@@ -126,7 +124,11 @@
         copy.wait()
 
 
-def inside_kernel(forcing, iterate, kappa, velocity, base, rim):
+def inside_kernel(forcing_hbm, iterate_hbm, kappa_hbm, velocity_hbm, base, rim, *scratch):
+    forcing, iterate, kappa, velocity, sems = scratch
+    pairs = [(kappa_hbm, kappa), (iterate_hbm, iterate), (velocity_hbm, velocity), (forcing_hbm, forcing)]
+    for copy in run_copies(pairs, sems):
+        copy.wait()
     row = lax.broadcasted_iota(jnp.int32, (NY, NX), 0)
     lane = lax.broadcasted_iota(jnp.int32, (NY, NX), 1)
 
@@ -153,7 +155,7 @@
         base[plane] = forcing[0, plane] - here * (1.0 / TIME_STEP) - (diagonal * here - total)
 
 
-def resid_kernel(base, rim, iterate, first, second, outer, inner, out, turned):
+def resid_kernel(base, rim, iterate, previous, outer, inner, out, turned):
     step = lax.axis_index("tm")
     place = lax.axis_index("space")
     even = place % 2 == 0
@@ -166,39 +168,37 @@
         spot[8 : 8 + NX] = array.T
         spot[8 + NX : 16 + NX] = edge
 
-    before = (first, second)
+    carried = jnp.where(leads, 0.0, 1.0 / TIME_STEP)
+    skip = jnp.where(leads, 0, 8)
     for plane in range(SLAB):
         side, other = (outer, inner) if plane == 0 else (inner, outer)
         ends = place == 0 if plane == 0 else place == 2 * CHIPS - 1
         here = iterate[0, plane]
         near = jnp.where(ends, 0.0, jnp.where(even, side[0], other[0]))
         far = jnp.where(ends, 0.0, 0.5 * jnp.where(even, side[1], other[1]))
-        carried = jnp.where(step == 0 if plane == 0 else leads, 0.0, 1.0 / TIME_STEP)
-        resid = base[plane] + before[plane][...] * carried + (rim[plane] + far) * near - far * here
+        resid = base[plane] + previous[0, plane] * carried + (rim[plane] + far) * near - far * here
         turn(turned.at[plane], resid * growth)
         for c in range(WINDOW):
             out[c, WIDE * plane : WIDE * (plane + 1)] = turned[plane, OWN * c : OWN * c + WIDE]
-    turn(turned.at[SLAB], jnp.where(leads, second[...], iterate[0, 1]))
-    skip = jnp.where(leads, 0, 8)
-    for c in range(WINDOW):
-        for number in range(2):
-            start = pl.multiple_of(OWN * c + OWN * number + skip, 8)
-            spot = SLAB * WIDE + 8 * number
-            out[c, spot : spot + 8] = turned[SLAB, pl.ds(start, 8)]
-
-
-def ahead_kernel(times, fields, above, below, *outs):
+        turn(turned.at[SLAB + plane], jnp.where(leads, previous[0, plane], here))
+        for c in range(WINDOW):
+            for number in range(2):
+                start = pl.multiple_of(OWN * c + OWN * number + skip, 8)
+                spot = SLAB * WIDE + EXTRA * plane + 8 * number
+                out[c, spot : spot + 8] = turned[SLAB + plane, pl.ds(start, 8)]
+
+
+def ahead_kernel(times, *outs):
     keeps, sends = outs[:GROUPS], outs[GROUPS:]
     core = lax.axis_index("space") % 2
     for plane in range(SLAB):
         for tile in range(WIDE // 8):
             rows = slice(8 * tile, 8 * tile + 8)
             values = [times[n, WIDE * plane + 8 * tile : WIDE * plane + 8 * tile + 8] for n in range(WINDOW)]
-            if plane == 1:
-                for n in (4, 8, 12):
-                    spot = SLAB * WIDE + 8 * (tile // 2)
-                    source = n - 1 if tile % 2 else n - 4
-                    values[n] += times[source, spot : spot + 8] * (time_scale(n) / TIME_STEP)
+            spot = SLAB * WIDE + EXTRA * plane + 8 * (tile // 2)
+            for n in (4, 8, 12):
+                source = n - 1 if tile % 2 else n - 4
+                values[n] += times[source, spot : spot + 8] * (time_scale(n) / TIME_STEP)
             parts = spectrum_of(values)
             for group, (keep, send) in enumerate(zip(keeps, sends)):
                 for r in range(REALS):
@@ -206,25 +206,30 @@
                     low, high = parts[index], parts[index + 4]
                     keep[plane, r, rows] = jnp.where(core == 0, low, high)
                     send[REALS * plane + r, rows] = jnp.where(core == 0, high, low)
-    spot = SLAB * REALS
-    for source in (below, fields, above):
+
+
+def pick(even, odd):
+    return jnp.where(lax.axis_index("space") // 2 % 2 == 0, even, odd)
+
+
+def gather_kernel(keep, got, chip, pair, other):
+    core = lax.axis_index("space") % 2
+    for r in range(REALS):
+        values = []
+        for plane in range(CHIP):
+            mine, theirs = keep[plane % SLAB, r], got[REALS * (plane % SLAB) + r]
+            values.append(jnp.where(core == plane // SLAB, mine, theirs))
+            chip[plane, r] = values[plane]
+        for plane in range(FIRST):
+            pair[plane, r] = pick(values[plane + 1], values[plane])
+            other[plane, r] = pick(values[plane], values[plane + 1])
+
+
+def pack_kernel(pair, fields, other, out):
+    for third, source in enumerate((pair, fields, other)):
         for field in range(4):
             for plane in range(SLAB):
-                sends[-1][spot] = source[field, plane]
-                spot += 1
-
-
-def gather_kernel(keep, got, chip, up, down):
-    core = lax.axis_index("space") % 2
-    for r in range(REALS):
-        for plane in range(CHIP):
-            mine, theirs = keep[plane % SLAB, r], got[REALS * (plane % SLAB) + r]
-            value = jnp.where(core == plane // SLAB, mine, theirs)
-            chip[plane, r] = value
-            if plane >= CHIP - FIRST:
-                up[plane - (CHIP - FIRST), r] = value
-            if plane < FIRST:
-                down[plane, r] = value
+                out[third, field, plane] = source[field, plane]
 
 
 def back_kernel(*refs):
@@ -251,7 +256,7 @@
         out[0, plane] = iterate[0, plane] + turned
 
 
-def prepare_kernel(fields, above, below, got, cof, held):
+def prepare_kernel(pair, fields, other, got, cof, held):
     place = lax.axis_index("space")
     core, chip = place % 2, place // 2
     start = lax.axis_index("tm") * OWN - 8
@@ -259,17 +264,21 @@
     lane = lax.broadcasted_iota(jnp.int32, (WIDE, NY), 1)
     rows = shift_rows()
     shifts = [[jnp.where(core == 0, rows[j][i], rows[4 + j][i]) for i in range(3)] for j in range(4)]
-    spot = SLAB * REALS
-    for third, source in enumerate((below, fields, above)):
+    for third in range(3):
         for field in range(4):
             for plane in range(SLAB):
-                value, other = source[field, plane], got[spot]
-                spot += 1
-                if field == 0 and third != 1:
-                    outside = chip == (0 if third == 0 else CHIPS - 1)
-                    value, other = jnp.where(outside, 0.0, value), jnp.where(outside, 0.0, other)
-                held[field, CHIP * third + plane] = jnp.where(core == 0, value, other)
-                held[field, CHIP * third + SLAB + plane] = jnp.where(core == 0, other, value)
+                if third == 1:
+                    value, partner = fields[field, plane], got[1, field, plane]
+                else:
+                    sources = [(pair[field, plane], got[0, field, plane]), (other[field, plane], got[2, field, plane])]
+                    below, above = sources[::-1], sources
+                    even, odd = below if third == 0 else above
+                    value, partner = pick(even[0], odd[0]), pick(even[1], odd[1])
+                    if field == 0:
+                        outside = chip == (0 if third == 0 else CHIPS - 1)
+                        value, partner = jnp.where(outside, 0.0, value), jnp.where(outside, 0.0, partner)
+                held[field, CHIP * third + plane] = jnp.where(core == 0, value, partner)
+                held[field, CHIP * third + SLAB + plane] = jnp.where(core == 0, partner, value)
     for z in range(REACH):
         spot = z + 1
         centre = held[0, spot]
@@ -336,17 +345,19 @@
         src, dst = dst, src
 
 
-def spectrum_reader(chip, above, below):
+def spectrum_reader(chip, pair, other):
     def spec_of(z, r):
         if z < FIRST:
-            return below[z, r]
-        return chip[z - FIRST, r] if z < FIRST + CHIP else above[z - FIRST - CHIP, r]
+            return pick(other[z, r], pair[z, r])
+        if z < FIRST + CHIP:
+            return chip[z - FIRST, r]
+        return pick(pair[z - FIRST - CHIP, r], other[z - FIRST - CHIP, r])
 
     return spec_of
 
 
-def first_kernel(group, chip, above, below, cof, out, field_a, field_b):
-    spec_of = spectrum_reader(chip, above, below)
+def first_kernel(group, chip, pair, other, cof, out, field_a, field_b):
+    spec_of = spectrum_reader(chip, pair, other)
     for field in (field_a, field_b):
         field[0:8] = jnp.zeros((8, NY), jnp.float32)
         field[8 + WIDE * REALS * REACH :] = jnp.zeros((8, NY), jnp.float32)
@@ -362,20 +373,21 @@
     sweeps(group, cof, spec_of, field_a, field_b, [(1, 9), (2, 8), (3, 7)], 0, finish)
 
 
-def second_kernel(group, chip, above, below, cof, own, high, low, mine, theirs, field_a, field_b):
+def second_kernel(group, chip, pair, other, cof, own, pair_own, other_own, mine, theirs, field_a, field_b):
     core = lax.axis_index("space") % 2
-    spec_of = spectrum_reader(chip, above, below)
+    spec_of = spectrum_reader(chip, pair, other)
     for field in (field_a, field_b):
         field[0:8] = jnp.zeros((8, NY), jnp.float32)
         field[8 + WIDE * REALS * 3 * CHIP :] = jnp.zeros((8, NY), jnp.float32)
     edge = jnp.zeros((8, NY), jnp.float32)
-    for third, source in enumerate((low, own, high)):
+    sources = ((other_own, pair_own), (own, own), (pair_own, other_own))
+    for third, (even, odd) in enumerate(sources):
         for plane in range(CHIP):
             for r in range(REALS):
                 spot = part_of(field_a, CHIP * third + plane, r)
                 spot[0:8] = edge
                 spot[WIDE - 8 : WIDE] = edge
-                spot[4 : 4 + NARROW] = source[plane, r]
+                spot[4 : 4 + NARROW] = own[plane, r] if third == 1 else pick(even[plane, r], odd[plane, r])
     held = {}
 
     def finish(z, r, value):
@@ -389,6 +401,9 @@
             theirs[plane - SLAB, r] = jnp.where(core == 0, value, low_value)
 
     sweeps(group, cof, spec_of, field_a, field_b, [(0, 10), (1, 9), (2, 8), (3, 7)], 1, finish)
+
+
+INSIDE_MIB = 53.25
 
 
 def call(kernel, shapes, args, scratch=(), anywhere=False, mib=32):
@@ -401,77 +416,91 @@
         in_specs=[pl.BlockSpec(memory_space=pl.ANY) if anywhere else vmem] * len(args),
         out_specs=[vmem] * len(shapes) if several else vmem,
         scratch_shapes=[pltpu.VMEM(dims, jnp.float32) if isinstance(dims, tuple) else dims for dims in scratch],
-        compiler_params=pltpu.CompilerParams(vmem_limit_bytes=mib * 1024 * 1024),
+        compiler_params=pltpu.CompilerParams(vmem_limit_bytes=int(mib * 1024 * 1024)),
     )(*args)
 
 
 def shards(forcing, iterate, kappa, velocity):
-    single, block = (NY, NX), (SLAB, NY, NX)
+    block = (SLAB, NY, NX)
     cores = [(i, i ^ 1) for i in range(2 * CHIPS)]
-    upward = [(i, (i + 2) % (2 * CHIPS)) for i in range(2 * CHIPS)]
-    downward = [(j, i) for i, j in upward]
+    pairs = [(i, i ^ 2) for i in range(2 * CHIPS)]
+    others = [(i, (i + 2) % (2 * CHIPS)) for i in range(2 * CHIPS) if i // 2 % 2]
+    others += [(j, i) for i, j in others]
     facing = [(i, (i + 1) % (2 * CHIPS)) for i in range(1, 2 * CHIPS, 2)]
     facing += [(j, i) for i, j in facing]
-    first, second, outer, inner, fields = call(
+    previous = lax.ppermute(iterate, "tm", [(i, i // 4 * 4 + (i + 1) % 4) for i in range(WINDOW)])
+    outer, inner, fields = call(
         entry_kernel,
-        [single, single, block, block, (4, SLAB, WIDE, NY)],
+        [block, block, (4, SLAB, WIDE, NY)],
         (iterate, kappa, velocity),
-        [(4, *block), (8, NX + 16, NY), pltpu.SemaphoreType.DMA((10,))],
+        [(4, *block), (8, NX + 16, NY), pltpu.SemaphoreType.DMA((8,))],
         anywhere=True,
-        mib=56,
-    )
-    first = lax.ppermute(first, "tm", [(i, (i + 1) % WINDOW) for i in range(WINDOW)])
-    second = lax.ppermute(second, "tm", [(i, i // 4 * 4 + (i + 1) % 4) for i in range(WINDOW)])
+        mib=53.25,
+    )
     outer = lax.ppermute(outer, "space", facing)
     inner = lax.ppermute(inner, "space", cores)
-    fields_below = lax.ppermute(fields, "space", upward)
-    fields_above = lax.ppermute(fields, "space", downward)
-    base, rim = call(inside_kernel, [block, block], (forcing, iterate, kappa, velocity))
-    first, fields_below, fields_above = lax.optimization_barrier((first, fields_below, fields_above))
+    fields, inner = lax.optimization_barrier((fields, inner))
+    fields_pair = lax.ppermute(fields, "space", pairs)
+    fields_other = lax.ppermute(fields, "space", others)
+    base, rim = call(
+        inside_kernel,
+        [block, block],
+        (forcing, iterate, kappa, velocity),
+        [(1, *block), (1, *block), block, (3, *block), pltpu.SemaphoreType.DMA((4,))],
+        anywhere=True,
+        mib=INSIDE_MIB,
+    )
+    outer, fields_pair, fields_other = lax.optimization_barrier((outer, fields_pair, fields_other))
     sent = call(
         resid_kernel,
-        (WINDOW, SLAB * WIDE + EXTRA, NY),
-        (base, rim, iterate, first, second, outer, inner),
-        [(SLAB + 1, NX + 16, NY)],
+        (WINDOW, SLAB * (WIDE + EXTRA), NY),
+        (base, rim, iterate, previous, outer, inner),
+        [(2 * SLAB, NX + 16, NY)],
     )
     times = lax.all_to_all(sent, "tm", 0, 0)
     parts = call(
         ahead_kernel,
         [(SLAB, REALS, WIDE, NY)] * GROUPS
-        + [(SLAB * REALS + (24 if group == GROUPS - 1 else 0), WIDE, NY) for group in range(GROUPS)],
-        (times, fields, fields_above, fields_below),
+        + [(SLAB * REALS, WIDE, NY)] * GROUPS,
+        (times,),
     )
     got = [lax.ppermute(sent, "space", cores) for sent in parts[GROUPS:]]
-    chips, aboves, belows = [], [], []
+    chips, pair_specs, other_specs = [], [], []
     for group in range(GROUPS):
         shape = (FIRST, REALS, WIDE, NY)
-        chip, up, down = call(gather_kernel, [(CHIP, REALS, WIDE, NY), shape, shape], (parts[group], got[group]))
+        chip, pair, other = call(gather_kernel, [(CHIP, REALS, WIDE, NY), shape, shape], (parts[group], got[group]))
         chips.append(chip)
-        belows.append(lax.ppermute(up, "space", upward))
-        aboves.append(lax.ppermute(down, "space", downward))
+        pair_specs.append(lax.ppermute(pair, "space", pairs))
+        other_specs.append(lax.ppermute(other, "space", others))
+    fields, chips[-1] = lax.optimization_barrier((fields, chips[-1]))
+    held = call(pack_kernel, (3, 4, SLAB, WIDE, NY), (fields_pair, fields, fields_other))
+    held = lax.ppermute(held, "space", cores)
     cof = call(
         prepare_kernel,
         (REACH, 15, WIDE, NY),
-        (fields, fields_above, fields_below, got[-1]),
+        (fields_pair, fields, fields_other, held),
         [(4, 3 * CHIP, WIDE, NY)],
     )
-    owns, lows, highs = [], [], []
+    owns, pair_owns, other_owns = [], [], []
     for group in range(GROUPS):
         own = call(
             functools.partial(first_kernel, group),
             (CHIP, REALS, NARROW, NY),
-            (chips[group], aboves[group], belows[group], cof),
+            (chips[group], pair_specs[group], other_specs[group], cof),
             [(16 + WIDE * REALS * REACH, NY)] * 2,
         )
         owns.append(own)
-        lows.append(lax.ppermute(own, "space", upward))
-        highs.append(lax.ppermute(own, "space", downward))
+        pair_owns.append(lax.ppermute(own, "space", pairs))
+        other_owns.append(lax.ppermute(own, "space", others))
     mines, theirs = [], []
     for group in range(GROUPS):
         mine, other = call(
             functools.partial(second_kernel, group),
             [(SLAB, REALS, OWN, NY)] * 2,
-            (chips[group], aboves[group], belows[group], cof, owns[group], highs[group], lows[group]),
+            (
+                *(chips[group], pair_specs[group], other_specs[group], cof),
+                *(owns[group], pair_owns[group], other_owns[group]),
+            ),
             [(16 + WIDE * REALS * 3 * CHIP, NY)] * 2,
         )
         mines.append(mine)

time: 95.9 us -> 93 us (0.970)
  the two profiles are of different devices: /device:TPU:32 before, /device:TPU:24 now
where the time goes in v4:
time: 93 us; the launch traced here: 92.7 us
  blocking collectives  50.2 us (54%)
  waiting for transfers between devices  17.7 us (19%)
  starting transfers between devices  15.4 us (17%)
  Pallas kernels  9.19 us (10%)
    all_to_all x1, blocking collectives, shards(): times = lax.all_to_all(sent, 'tm', 0, 0)  33.6 us
    all_to_all x1, blocking collectives, shards(): correction = lax.all_to_all(correction, 'tm', 0, 0)  16.6 us
    pallas_call x14, Pallas kernels, call(): pl.pallas_call(kernel, out_shape=out_shape if several else out_shape[0],...  9.19 us
    ppermute x2, waiting for transfers between devices, shards(): other_owns.append(lax.ppermute(own, 'space', others))  4.42 us
    ppermute x2, waiting for transfers between devices, shards(): other_specs.append(lax.ppermute(other, 'space', others))  4.21 us
    ppermute x2, starting transfers between devices, shards(): other_specs.append(lax.ppermute(other, 'space', others))  3.8 us
    ppermute x2, starting transfers between devices, shards(): other_owns.append(lax.ppermute(own, 'space', others))  3.26 us
    ppermute x1, starting transfers between devices, shards(): fields_other = lax.ppermute(fields, 'space', others)  2.95 us
  transfers between devices with their start and end apart: 18, of which 11 were waited for; matrix products, arithmetic and copies ran while one was open for 0% of the time, Pallas kernels for 7%

profile of v4, /device:TPU:24, one launch (start us, length us, event | category | flops | bytes accessed | tf_op | source)
XLA Modules:
  0.0 92.7 jit_solution(3052680315680728793)
XLA Ops:
  0.0 1.6 %shard_map.47 = (f32[2,128,256]{2,1,0:T(8,128)S(1)}, f32[2,128,256]{2,1,0:T(8,128)S(1)}, f32[4,2,32,128]{3,2,1,0:T(8,128)S(1)}) custom-call(f32[1,2,128,256]{3,2,1,0:T(8,128)} %iterate.5, f32[2,128,256]{2,1,0:T(8,128)} %kappa.1, f32[3,2,128,256]{3,2,1,0:T(8,128)} %velocity.1), custom_call_target="tpu_custom_call" | custom-call | tf_op jit(solution)/shard_map/pallas_call | solution.py:413
  1.7 0.8 collective-permute-start.1
  2.6 1.5 %collective-permute-start = (f32[1,2,128,256]{3,2,1,0:T(8,128)}, f32[1,2,128,256]{3,2,1,0:T(8,128)S(1)}, u32[]{:S(2)}, u32[]{:S(2)}) collective-permute-start(f32[1,2,128,256]{3,2,1,0:T(8,128)} %iterate.5), channel_id=1, source_target_pairs={{0,16},{16,32},{32,48},{48,0},{64,80},{80,96},{96,112},{112,64},{1... | collective-permute-start | bytes 786440 | tf_op jit(solution)/shard_map/ppermute | solution.py:431
  4.5 2.9 %collective-permute-start.4 = (f32[4,2,32,128]{3,2,1,0:T(8,128)S(1)}, f32[4,2,32,128]{3,2,1,0:T(8,128)S(1)}, u32[]{:S(2)}, u32[]{:S(2)}) collective-permute-start(f32[4,2,32,128]{3,2,1,0:T(8,128)S(1)} %get-tuple-element.48.fields), channel_id=1, source_target_pairs={{2,4},{3,5},{6,8},{7,9},{10,12},{11,13},{14,0},{15,1},{4,2},{5,3},... | collective-permute-start | bytes 393224 | tf_op jit(solution)/shard_map/ppermute | solution.py:444
  7.5 1.9 %shard_map.46 = (f32[2,128,256]{2,1,0:T(8,128)S(1)}, f32[2,128,256]{2,1,0:T(8,128)S(1)}) custom-call(f32[1,2,128,256]{3,2,1,0:T(8,128)} %forcing_hbm.1, f32[1,2,128,256]{3,2,1,0:T(8,128)} %iterate.5, f32[2,128,256]{2,1,0:T(8,128)} %kappa.1, f32[3,2,128,256]{3,2,1,0:T(8,128)} %velocity.1), custom_call_target="tpu_custom_call" | custom-call | tf_op jit(solution)/shard_map/pallas_call | solution.py:413
  9.4 1.0 %collective-permute-done.3.pair = f32[4,2,32,128]{3,2,1,0:T(8,128)S(1)} collective-permute-done((f32[4,2,32,128]{3,2,1,0:T(8,128)S(1)}, f32[4,2,32,128]{3,2,1,0:T(8,128)S(1)}, u32[]{:S(2)}, u32[]{:S(2)}) %collective-permute-start.3) | collective-permute-done | bytes 131104 | tf_op jit(solution)/shard_map/ppermute | solution.py:443
  10.4 2.7 %collective-permute-done.4.other = f32[4,2,32,128]{3,2,1,0:T(8,128)S(1)} collective-permute-done((f32[4,2,32,128]{3,2,1,0:T(8,128)S(1)}, f32[4,2,32,128]{3,2,1,0:T(8,128)S(1)}, u32[]{:S(2)}, u32[]{:S(2)}) %collective-permute-start.4) | collective-permute-done | bytes 131104 | tf_op jit(solution)/shard_map/ppermute | solution.py:444
  13.4 33.6 %all_to_all.10.times = f32[16,96,128]{2,1,0:T(8,128)S(1)} all-to-all(f32[16,96,128]{2,1,0:T(8,128)S(1)} %shard_map.48), channel_id=1, replica_groups=mesh['tm'=16,'space'=16] {'tm'}, dimensions={0} | all-to-all | bytes 1572864 | tf_op jit(solution)/shard_map/all_to_all | solution.py:460
  47.3 1.3 %collective-permute-done.8.got = f32[8,32,128]{2,1,0:T(8,128)S(1)} collective-permute-done((f32[8,32,128]{2,1,0:T(8,128)S(1)}, f32[8,32,128]{2,1,0:T(8,128)S(1)}, u32[]{:S(2)}, u32[]{:S(2)}) %collective-permute-start.8) | collective-permute-done | bytes 131104 | tf_op jit(solution)/shard_map/ppermute | solution.py:467
  49.9 0.9 collective-permute-start.13
  51.5 3.0 %collective-permute-start.7 = (f32[3,4,32,128]{3,2,1,0:T(8,128)S(1)}, f32[3,4,32,128]{3,2,1,0:T(8,128)S(1)}, u32[]{:S(2)}, u32[]{:S(2)}) collective-permute-start(f32[3,4,32,128]{3,2,1,0:T(8,128)S(1)} %get-tuple-element.43), channel_id=1, source_target_pairs={{2,4},{3,5},{6,8},{7,9},{10,12},{11,13},{14,0},{15,1},{4,2},{5,3},... | collective-permute-start | bytes 589832 | tf_op jit(solution)/shard_map/ppermute | solution.py:474
  54.9 2.1 %collective-permute-done.12.pair = f32[3,4,32,128]{3,2,1,0:T(8,128)S(1)} collective-permute-done((f32[3,4,32,128]{3,2,1,0:T(8,128)S(1)}, f32[3,4,32,128]{3,2,1,0:T(8,128)S(1)}, u32[]{:S(2)}, u32[]{:S(2)}) %collective-permute-start.12) | collective-permute-done | bytes 196640 | tf_op jit(solution)/shard_map/ppermute | solution.py:473
  57.0 2.7 %collective-permute-done.13.other = f32[3,4,32,128]{3,2,1,0:T(8,128)S(1)} collective-permute-done((f32[3,4,32,128]{3,2,1,0:T(8,128)S(1)}, f32[3,4,32,128]{3,2,1,0:T(8,128)S(1)}, u32[]{:S(2)}, u32[]{:S(2)}) %collective-permute-start.13) | collective-permute-done | bytes 196640 | tf_op jit(solution)/shard_map/ppermute | solution.py:474
  59.8 0.8 shard_map.56.own
  61.4 1.5 %collective-permute-done.7.other = f32[3,4,32,128]{3,2,1,0:T(8,128)S(1)} collective-permute-done((f32[3,4,32,128]{3,2,1,0:T(8,128)S(1)}, f32[3,4,32,128]{3,2,1,0:T(8,128)S(1)}, u32[]{:S(2)}, u32[]{:S(2)}) %collective-permute-start.7) | collective-permute-done | bytes 196640 | tf_op jit(solution)/shard_map/ppermute | solution.py:474
  62.9 0.8 shard_map.54.own
  64.0 2.6 %collective-permute-start.11 = (f32[4,4,24,128]{3,2,1,0:T(8,128)S(1)}, f32[4,4,24,128]{3,2,1,0:T(8,128)S(1)}, u32[]{:S(2)}, u32[]{:S(2)}) collective-permute-start(f32[4,4,24,128]{3,2,1,0:T(8,128)S(1)} %shard_map.54.own), channel_id=1, source_target_pairs={{2,4},{3,5},{6,8},{7,9},{10,12},{11,13},{14,0},{15,1},{4,2},{5,3},... | collective-permute-start | bytes 589832 | tf_op jit(solution)/shard_map/ppermute | solution.py:494
  67.1 2.2 %collective-permute-done.15.other_own = f32[4,4,24,128]{3,2,1,0:T(8,128)S(1)} collective-permute-done((f32[4,4,24,128]{3,2,1,0:T(8,128)S(1)}, f32[4,4,24,128]{3,2,1,0:T(8,128)S(1)}, u32[]{:S(2)}, u32[]{:S(2)}) %collective-permute-start.15) | collective-permute-done | bytes 196640 | tf_op jit(solution)/shard_map/ppermute | solution.py:494
  69.3 1.1 %shard_map.57 = (f32[2,4,16,128]{3,2,1,0:T(8,128)S(1)}, f32[2,4,16,128]{3,2,1,0:T(8,128)S(1)}) custom-call(f32[4,4,32,128]{3,2,1,0:T(8,128)S(1)} %get-tuple-element.51.chip, f32[3,4,32,128]{3,2,1,0:T(8,128)S(1)} %collective-permute-done.12.pair, f32[3,4,32,128]{3,2,1,0:T(8,128)S(1)} %collective-permute-done.13.other, f32[10,15,32,128]{3,2,1,0:T(8,128)S(1)} %shard_map.53.cof, ...), custom_call_target="tpu_custom_call" | custom-call | tf_op jit(solution)/shard_map/pallas_call | solution.py:413
  70.5 2.2 %collective-permute-done.11.other_own = f32[4,4,24,128]{3,2,1,0:T(8,128)S(1)} collective-permute-done((f32[4,4,24,128]{3,2,1,0:T(8,128)S(1)}, f32[4,4,24,128]{3,2,1,0:T(8,128)S(1)}, u32[]{:S(2)}, u32[]{:S(2)}) %collective-permute-start.11) | collective-permute-done | bytes 196640 | tf_op jit(solution)/shard_map/ppermute | solution.py:494
  72.8 1.1 %shard_map.55 = (f32[2,4,16,128]{3,2,1,0:T(8,128)S(1)}, f32[2,4,16,128]{3,2,1,0:T(8,128)S(1)}) custom-call(f32[4,4,32,128]{3,2,1,0:T(8,128)S(1)} %get-tuple-element.41.chip, f32[3,4,32,128]{3,2,1,0:T(8,128)S(1)} %collective-permute-done.6.pair, f32[3,4,32,128]{3,2,1,0:T(8,128)S(1)} %collective-permute-done.7.other, f32[10,15,32,128]{3,2,1,0:T(8,128)S(1)} %shard_map.53.cof, ...), custom_call_target="tpu_custom_call" | custom-call | tf_op jit(solution)/shard_map/pallas_call | solution.py:413
  73.9 1.2 %collective-permute-done.16.refs_2_ = f32[2,4,16,128]{3,2,1,0:T(8,128)S(1)} collective-permute-done((f32[2,4,16,128]{3,2,1,0:T(8,128)S(1)}, f32[2,4,16,128]{3,2,1,0:T(8,128)S(1)}, u32[]{:S(2)}, u32[]{:S(2)}) %collective-permute-start.16) | collective-permute-done | bytes 65568 | tf_op jit(solution)/shard_map/ppermute | solution.py:507
  75.2 16.6 %all_to_all.11.correction = f32[16,2,16,128]{3,2,1,0:T(8,128)S(1)} all-to-all(f32[16,2,16,128]{3,2,1,0:T(8,128)S(1)} %shard_map.58), channel_id=1, replica_groups=mesh['tm'=16,'space'=16] {'tm'}, dimensions={0} | all-to-all | bytes 524288 | tf_op jit(solution)/shard_map/all_to_all | solution.py:509
  91.8 0.8 shard_map.59
  (30 shorter events, 5.5 us)
Async XLA Ops:
  0.0 13.1 %copy-start = (f32[1,2,128,256]{3,2,1,0:T(8,128)S(1)}, f32[1,2,128,256]{3,2,1,0:T(8,128)}, u32[]{:S(2)}) copy-start(f32[1,2,128,256]{3,2,1,0:T(8,128)} %iterate.5) | copy-start | bytes 786436
  1.6 2.4 %collective-permute-start.2 = (f32[2,128,256]{2,1,0:T(8,128)S(1)}, f32[2,128,256]{2,1,0:T(8,128)S(1)}, u32[]{:S(2)}, u32[]{:S(2)}) collective-permute-start(f32[2,128,256]{2,1,0:T(8,128)S(1)} %get-tuple-element.35), channel_id=1, source_target_pairs={{0,1},{1,0},{2,3},{3,2},{4,5},{5,4},{6,7},{7,6},{8,9},{9,8},{10,11... | collective-permute-start | bytes 786440 | tf_op jit(solution)/shard_map/ppermute | solution.py:441
  1.7 7.7 %collective-permute-start.1 = (f32[2,128,256]{2,1,0:T(8,128)S(1)}, f32[2,128,256]{2,1,0:T(8,128)S(1)}, u32[]{:S(2)}, u32[]{:S(2)}) collective-permute-start(f32[2,128,256]{2,1,0:T(8,128)S(1)} %get-tuple-element.33), channel_id=1, source_target_pairs={{1,2},{3,4},{5,6},{7,8},{9,10},{11,12},{13,14},{15,0},{2,1},{4,3},... | collective-permute-start | bytes 786440 | tf_op jit(solution)/shard_map/ppermute | solution.py:440
  2.6 10.6 %collective-permute-start = (f32[1,2,128,256]{3,2,1,0:T(8,128)}, f32[1,2,128,256]{3,2,1,0:T(8,128)S(1)}, u32[]{:S(2)}, u32[]{:S(2)}) collective-permute-start(f32[1,2,128,256]{3,2,1,0:T(8,128)} %iterate.5), channel_id=1, source_target_pairs={{0,16},{16,32},{32,48},{48,0},{64,80},{80,96},{96,112},{112,64},{1... | collective-permute-start | bytes 786440 | tf_op jit(solution)/shard_map/ppermute | solution.py:431
  4.1 6.4 %collective-permute-start.3 = (f32[4,2,32,128]{3,2,1,0:T(8,128)S(1)}, f32[4,2,32,128]{3,2,1,0:T(8,128)S(1)}, u32[]{:S(2)}, u32[]{:S(2)}) collective-permute-start(f32[4,2,32,128]{3,2,1,0:T(8,128)S(1)} %get-tuple-element.48.fields), channel_id=1, source_target_pairs={{0,2},{1,3},{2,0},{3,1},{4,6},{5,7},{6,4},{7,5},{8,10},{9,11},{10,... | collective-permute-start | bytes 393224 | tf_op jit(solution)/shard_map/ppermute | solution.py:443
  4.5 8.6 %collective-permute-start.4 = (f32[4,2,32,128]{3,2,1,0:T(8,128)S(1)}, f32[4,2,32,128]{3,2,1,0:T(8,128)S(1)}, u32[]{:S(2)}, u32[]{:S(2)}) collective-permute-start(f32[4,2,32,128]{3,2,1,0:T(8,128)S(1)} %get-tuple-element.48.fields), channel_id=1, source_target_pairs={{2,4},{3,5},{6,8},{7,9},{10,12},{11,13},{14,0},{15,1},{4,2},{5,3},... | collective-permute-start | bytes 393224 | tf_op jit(solution)/shard_map/ppermute | solution.py:444
  47.1 1.4 %collective-permute-start.8 = (f32[8,32,128]{2,1,0:T(8,128)S(1)}, f32[8,32,128]{2,1,0:T(8,128)S(1)}, u32[]{:S(2)}, u32[]{:S(2)}) collective-permute-start(f32[8,32,128]{2,1,0:T(8,128)S(1)} %get-tuple-element.46), channel_id=1, source_target_pairs={{0,1},{1,0},{2,3},{3,2},{4,5},{5,4},{6,7},{7,6},{8,9},{9,8},{10,11... | collective-permute-start | bytes 393224 | tf_op jit(solution)/shard_map/ppermute | solution.py:467
  48.7 5.7 %collective-permute-start.9 = (f32[3,4,2,32,128]{4,3,2,1,0:T(8,128)S(1)}, f32[3,4,2,32,128]{4,3,2,1,0:T(8,128)S(1)}, u32[]{:S(2)}, u32[]{:S(2)}) collective-permute-start(f32[3,4,2,32,128]{4,3,2,1,0:T(8,128)S(1)} %shard_map.52), channel_id=1, source_target_pairs={{0,1},{1,0},{2,3},{3,2},{4,5},{5,4},{6,7},{7,6},{8,9},{9,8},{10,11... | collective-permute-start | bytes 1179656 | tf_op jit(solution)/shard_map/ppermute | solution.py:477
  48.9 1.8 %collective-permute-start.5 = (f32[8,32,128]{2,1,0:T(8,128)S(1)}, f32[8,32,128]{2,1,0:T(8,128)S(1)}, u32[]{:S(2)}, u32[]{:S(2)}) collective-permute-start(f32[8,32,128]{2,1,0:T(8,128)S(1)} %get-tuple-element.40), channel_id=1, source_target_pairs={{0,1},{1,0},{2,3},{3,2},{4,5},{5,4},{6,7},{7,6},{8,9},{9,8},{10,11... | collective-permute-start | bytes 393224 | tf_op jit(solution)/shard_map/ppermute | solution.py:467
  49.3 7.7 %collective-permute-start.12 = (f32[3,4,32,128]{3,2,1,0:T(8,128)S(1)}, f32[3,4,32,128]{3,2,1,0:T(8,128)S(1)}, u32[]{:S(2)}, u32[]{:S(2)}) collective-permute-start(f32[3,4,32,128]{3,2,1,0:T(8,128)S(1)} %get-tuple-element.52), channel_id=1, source_target_pairs={{0,2},{1,3},{2,0},{3,1},{4,6},{5,7},{6,4},{7,5},{8,10},{9,11},{10,... | collective-permute-start | bytes 589832 | tf_op jit(solution)/shard_map/ppermute | solution.py:473
  49.9 9.9 %collective-permute-start.13 = (f32[3,4,32,128]{3,2,1,0:T(8,128)S(1)}, f32[3,4,32,128]{3,2,1,0:T(8,128)S(1)}, u32[]{:S(2)}, u32[]{:S(2)}) collective-permute-start(f32[3,4,32,128]{3,2,1,0:T(8,128)S(1)} %get-tuple-element.53), channel_id=1, source_target_pairs={{2,4},{3,5},{6,8},{7,9},{10,12},{11,13},{14,0},{15,1},{4,2},{5,3},... | collective-permute-start | bytes 589832 | tf_op jit(solution)/shard_map/ppermute | solution.py:474
  50.8 10.6 %collective-permute-start.6 = (f32[3,4,32,128]{3,2,1,0:T(8,128)S(1)}, f32[3,4,32,128]{3,2,1,0:T(8,128)S(1)}, u32[]{:S(2)}, u32[]{:S(2)}) collective-permute-start(f32[3,4,32,128]{3,2,1,0:T(8,128)S(1)} %get-tuple-element.42), channel_id=1, source_target_pairs={{0,2},{1,3},{2,0},{3,1},{4,6},{5,7},{6,4},{7,5},{8,10},{9,11},{10,... | collective-permute-start | bytes 589832 | tf_op jit(solution)/shard_map/ppermute | solution.py:473
  51.5 11.4 %collective-permute-start.7 = (f32[3,4,32,128]{3,2,1,0:T(8,128)S(1)}, f32[3,4,32,128]{3,2,1,0:T(8,128)S(1)}, u32[]{:S(2)}, u32[]{:S(2)}) collective-permute-start(f32[3,4,32,128]{3,2,1,0:T(8,128)S(1)} %get-tuple-element.43), channel_id=1, source_target_pairs={{2,4},{3,5},{6,8},{7,9},{10,12},{11,13},{14,0},{15,1},{4,2},{5,3},... | collective-permute-start | bytes 589832 | tf_op jit(solution)/shard_map/ppermute | solution.py:474
  60.6 6.5 %collective-permute-start.14 = (f32[4,4,24,128]{3,2,1,0:T(8,128)S(1)}, f32[4,4,24,128]{3,2,1,0:T(8,128)S(1)}, u32[]{:S(2)}, u32[]{:S(2)}) collective-permute-start(f32[4,4,24,128]{3,2,1,0:T(8,128)S(1)} %shard_map.56.own), channel_id=1, source_target_pairs={{0,2},{1,3},{2,0},{3,1},{4,6},{5,7},{6,4},{7,5},{8,10},{9,11},{10,... | collective-permute-start | bytes 589832 | tf_op jit(solution)/shard_map/ppermute | solution.py:493
  60.7 8.6 %collective-permute-start.15 = (f32[4,4,24,128]{3,2,1,0:T(8,128)S(1)}, f32[4,4,24,128]{3,2,1,0:T(8,128)S(1)}, u32[]{:S(2)}, u32[]{:S(2)}) collective-permute-start(f32[4,4,24,128]{3,2,1,0:T(8,128)S(1)} %shard_map.56.own), channel_id=1, source_target_pairs={{2,4},{3,5},{6,8},{7,9},{10,12},{11,13},{14,0},{15,1},{4,2},{5,3},... | collective-permute-start | bytes 589832 | tf_op jit(solution)/shard_map/ppermute | solution.py:494
  63.7 6.9 %collective-permute-start.10 = (f32[4,4,24,128]{3,2,1,0:T(8,128)S(1)}, f32[4,4,24,128]{3,2,1,0:T(8,128)S(1)}, u32[]{:S(2)}, u32[]{:S(2)}) collective-permute-start(f32[4,4,24,128]{3,2,1,0:T(8,128)S(1)} %shard_map.54.own), channel_id=1, source_target_pairs={{0,2},{1,3},{2,0},{3,1},{4,6},{5,7},{6,4},{7,5},{8,10},{9,11},{10,... | collective-permute-start | bytes 589832 | tf_op jit(solution)/shard_map/ppermute | solution.py:493
  64.0 8.8 %collective-permute-start.11 = (f32[4,4,24,128]{3,2,1,0:T(8,128)S(1)}, f32[4,4,24,128]{3,2,1,0:T(8,128)S(1)}, u32[]{:S(2)}, u32[]{:S(2)}) collective-permute-start(f32[4,4,24,128]{3,2,1,0:T(8,128)S(1)} %shard_map.54.own), channel_id=1, source_target_pairs={{2,4},{3,5},{6,8},{7,9},{10,12},{11,13},{14,0},{15,1},{4,2},{5,3},... | collective-permute-start | bytes 589832 | tf_op jit(solution)/shard_map/ppermute | solution.py:494
  70.4 3.6 %collective-permute-start.17 = (f32[2,4,16,128]{3,2,1,0:T(8,128)S(1)}, f32[2,4,16,128]{3,2,1,0:T(8,128)S(1)}, u32[]{:S(2)}, u32[]{:S(2)}) collective-permute-start(f32[2,4,16,128]{3,2,1,0:T(8,128)S(1)} %get-tuple-element.56), channel_id=1, source_target_pairs={{0,1},{1,0},{2,3},{3,2},{4,5},{5,4},{6,7},{7,6},{8,9},{9,8},{10,11... | collective-permute-start | bytes 196616 | tf_op jit(solution)/shard_map/ppermute | solution.py:507
  73.8 1.3 %collective-permute-start.16 = (f32[2,4,16,128]{3,2,1,0:T(8,128)S(1)}, f32[2,4,16,128]{3,2,1,0:T(8,128)S(1)}, u32[]{:S(2)}, u32[]{:S(2)}) collective-permute-start(f32[2,4,16,128]{3,2,1,0:T(8,128)S(1)} %get-tuple-element.55), channel_id=1, source_target_pairs={{0,1},{1,0},{2,3},{3,2},{4,5},{5,4},{6,7},{7,6},{8,9},{9,8},{10,11... | collective-permute-start | bytes 196616 | tf_op jit(solution)/shard_map/ppermute | solution.py:507

commit v5 on v4

--- a/solution.py
+++ b/solution.py
@@ -356,7 +356,7 @@
     return spec_of
 
 
-def first_kernel(group, chip, pair, other, cof, out, field_a, field_b):
+def first_kernel(group, chip, other, pair, cof, out, field_a, field_b):
     spec_of = spectrum_reader(chip, pair, other)
     for field in (field_a, field_b):
         field[0:8] = jnp.zeros((8, NY), jnp.float32)
@@ -373,7 +373,7 @@
     sweeps(group, cof, spec_of, field_a, field_b, [(1, 9), (2, 8), (3, 7)], 0, finish)
 
 
-def second_kernel(group, chip, pair, other, cof, own, pair_own, other_own, mine, theirs, field_a, field_b):
+def second_kernel(group, chip, other, pair, cof, own, other_own, pair_own, mine, theirs, field_a, field_b):
     core = lax.axis_index("space") % 2
     spec_of = spectrum_reader(chip, pair, other)
     for field in (field_a, field_b):
@@ -424,8 +424,9 @@
     block = (SLAB, NY, NX)
     cores = [(i, i ^ 1) for i in range(2 * CHIPS)]
     pairs = [(i, i ^ 2) for i in range(2 * CHIPS)]
-    others = [(i, (i + 2) % (2 * CHIPS)) for i in range(2 * CHIPS) if i // 2 % 2]
+    others = [(i, i + 2) for i in range(2 * CHIPS - 2) if i // 2 % 2]
     others += [(j, i) for i, j in others]
+    others += [(i, i ^ 1) for i in (0, 1, 2 * CHIPS - 2, 2 * CHIPS - 1)]
     facing = [(i, (i + 1) % (2 * CHIPS)) for i in range(1, 2 * CHIPS, 2)]
     facing += [(j, i) for i, j in facing]
     previous = lax.ppermute(iterate, "tm", [(i, i // 4 * 4 + (i + 1) % 4) for i in range(WINDOW)])
@@ -470,8 +471,8 @@
         shape = (FIRST, REALS, WIDE, NY)
         chip, pair, other = call(gather_kernel, [(CHIP, REALS, WIDE, NY), shape, shape], (parts[group], got[group]))
         chips.append(chip)
+        other_specs.append(lax.ppermute(other, "space", others))
         pair_specs.append(lax.ppermute(pair, "space", pairs))
-        other_specs.append(lax.ppermute(other, "space", others))
     fields, chips[-1] = lax.optimization_barrier((fields, chips[-1]))
     held = call(pack_kernel, (3, 4, SLAB, WIDE, NY), (fields_pair, fields, fields_other))
     held = lax.ppermute(held, "space", cores)
@@ -486,20 +487,20 @@
         own = call(
             functools.partial(first_kernel, group),
             (CHIP, REALS, NARROW, NY),
-            (chips[group], pair_specs[group], other_specs[group], cof),
+            (chips[group], other_specs[group], pair_specs[group], cof),
             [(16 + WIDE * REALS * REACH, NY)] * 2,
         )
         owns.append(own)
+        other_owns.append(lax.ppermute(own, "space", others))
         pair_owns.append(lax.ppermute(own, "space", pairs))
-        other_owns.append(lax.ppermute(own, "space", others))
     mines, theirs = [], []
     for group in range(GROUPS):
         mine, other = call(
             functools.partial(second_kernel, group),
             [(SLAB, REALS, OWN, NY)] * 2,
             (
-                *(chips[group], pair_specs[group], other_specs[group], cof),
-                *(owns[group], pair_owns[group], other_owns[group]),
+                *(chips[group], other_specs[group], pair_specs[group], cof),
+                *(owns[group], other_owns[group], pair_owns[group]),
             ),
             [(16 + WIDE * REALS * 3 * CHIP, NY)] * 2,
         )

time: 93 us -> 91.8 us (0.987)
    ppermute x2, waiting for transfers between devices: 2.13 us -> 0.01 us  [shards(): pair_specs.append(lax.ppermute(pair, 'space', pairs))]
    ppermute x2, waiting for transfers between devices: 4.21 us -> 5.53 us  [shards(): other_specs.append(lax.ppermute(other, 'space', others))]
    ppermute x2, starting transfers between devices: 3.8 us -> 2.83 us  [shards(): other_specs.append(lax.ppermute(other, 'space', others))]
  transfers between devices with their start and end apart: 18 -> 18, of which waited for: 11 -> 10; matrix products, arithmetic and copies ran while one was open for 0% -> 0% of each run, Pallas kernels for 7% -> 7%
where the time goes in v5:
time: 91.8 us; the launch traced here: 91.2 us
  blocking collectives  49.5 us (54%)
  waiting for transfers between devices  17.9 us (19%)
  starting transfers between devices  14.5 us (16%)
  Pallas kernels  9.19 us (10%)
    all_to_all x1, blocking collectives, shards(): times = lax.all_to_all(sent, 'tm', 0, 0)  33.4 us
    all_to_all x1, blocking collectives, shards(): correction = lax.all_to_all(correction, 'tm', 0, 0)  16.1 us
    pallas_call x14, Pallas kernels, call(): pl.pallas_call(kernel, out_shape=out_shape if several else out_shape[0],...  9.19 us
    ppermute x2, waiting for transfers between devices, shards(): other_specs.append(lax.ppermute(other, 'space', others))  5.53 us
    ppermute x2, waiting for transfers between devices, shards(): other_owns.append(lax.ppermute(own, 'space', others))  4.55 us
    ppermute x2, starting transfers between devices, shards(): other_owns.append(lax.ppermute(own, 'space', others))  4.16 us
    ppermute x1, starting transfers between devices, shards(): fields_other = lax.ppermute(fields, 'space', others)  2.95 us
    ppermute x2, starting transfers between devices, shards(): other_specs.append(lax.ppermute(other, 'space', others))  2.83 us
  transfers between devices with their start and end apart: 18, of which 10 were waited for; matrix products, arithmetic and copies ran while one was open for 0% of the time, Pallas kernels for 7%

profile of v5, /device:TPU:24, one launch (start us, length us, event | category | flops | bytes accessed | tf_op | source)
XLA Modules:
  0.0 91.2 jit_solution(15350011475940344134)
XLA Ops:
  0.0 1.6 %shard_map.47 = (f32[2,128,256]{2,1,0:T(8,128)S(1)}, f32[2,128,256]{2,1,0:T(8,128)S(1)}, f32[4,2,32,128]{3,2,1,0:T(8,128)S(1)}) custom-call(f32[1,2,128,256]{3,2,1,0:T(8,128)} %iterate.5, f32[2,128,256]{2,1,0:T(8,128)} %kappa.1, f32[3,2,128,256]{3,2,1,0:T(8,128)} %velocity.1), custom_call_target="tpu_custom_call" | custom-call | tf_op jit(solution)/shard_map/pallas_call | solution.py:413
  1.7 0.8 collective-permute-start.1
  2.6 1.5 %collective-permute-start = (f32[1,2,128,256]{3,2,1,0:T(8,128)}, f32[1,2,128,256]{3,2,1,0:T(8,128)S(1)}, u32[]{:S(2)}, u32[]{:S(2)}) collective-permute-start(f32[1,2,128,256]{3,2,1,0:T(8,128)} %iterate.5), channel_id=1, source_target_pairs={{0,16},{16,32},{32,48},{48,0},{64,80},{80,96},{96,112},{112,64},{1... | collective-permute-start | bytes 786440 | tf_op jit(solution)/shard_map/ppermute | solution.py:432
  4.5 2.9 %collective-permute-start.4 = (f32[4,2,32,128]{3,2,1,0:T(8,128)S(1)}, f32[4,2,32,128]{3,2,1,0:T(8,128)S(1)}, u32[]{:S(2)}, u32[]{:S(2)}) collective-permute-start(f32[4,2,32,128]{3,2,1,0:T(8,128)S(1)} %get-tuple-element.48.fields), channel_id=1, source_target_pairs={{2,4},{3,5},{6,8},{7,9},{10,12},{11,13},{4,2},{5,3},{8,6},{9,7},{1... | collective-permute-start | bytes 393224 | tf_op jit(solution)/shard_map/ppermute | solution.py:445
  7.5 1.9 %shard_map.46 = (f32[2,128,256]{2,1,0:T(8,128)S(1)}, f32[2,128,256]{2,1,0:T(8,128)S(1)}) custom-call(f32[1,2,128,256]{3,2,1,0:T(8,128)} %forcing_hbm.1, f32[1,2,128,256]{3,2,1,0:T(8,128)} %iterate.5, f32[2,128,256]{2,1,0:T(8,128)} %kappa.1, f32[3,2,128,256]{3,2,1,0:T(8,128)} %velocity.1), custom_call_target="tpu_custom_call" | custom-call | tf_op jit(solution)/shard_map/pallas_call | solution.py:413
  9.4 1.0 %collective-permute-done.3.pair = f32[4,2,32,128]{3,2,1,0:T(8,128)S(1)} collective-permute-done((f32[4,2,32,128]{3,2,1,0:T(8,128)S(1)}, f32[4,2,32,128]{3,2,1,0:T(8,128)S(1)}, u32[]{:S(2)}, u32[]{:S(2)}) %collective-permute-start.3) | collective-permute-done | bytes 131104 | tf_op jit(solution)/shard_map/ppermute | solution.py:444
  10.4 2.7 %collective-permute-done.4.other = f32[4,2,32,128]{3,2,1,0:T(8,128)S(1)} collective-permute-done((f32[4,2,32,128]{3,2,1,0:T(8,128)S(1)}, f32[4,2,32,128]{3,2,1,0:T(8,128)S(1)}, u32[]{:S(2)}, u32[]{:S(2)}) %collective-permute-start.4) | collective-permute-done | bytes 131104 | tf_op jit(solution)/shard_map/ppermute | solution.py:445
  13.4 33.4 %all_to_all.10.times = f32[16,96,128]{2,1,0:T(8,128)S(1)} all-to-all(f32[16,96,128]{2,1,0:T(8,128)S(1)} %shard_map.48), channel_id=1, replica_groups=mesh['tm'=16,'space'=16] {'tm'}, dimensions={0} | all-to-all | bytes 1572864 | tf_op jit(solution)/shard_map/all_to_all | solution.py:461
  47.0 1.3 %collective-permute-done.8.got = f32[8,32,128]{2,1,0:T(8,128)S(1)} collective-permute-done((f32[8,32,128]{2,1,0:T(8,128)S(1)}, f32[8,32,128]{2,1,0:T(8,128)S(1)}, u32[]{:S(2)}, u32[]{:S(2)}) %collective-permute-start.8) | collective-permute-done | bytes 131104 | tf_op jit(solution)/shard_map/ppermute | solution.py:468
  49.1 0.8 collective-permute-start.13
  50.5 2.8 %collective-permute-start.6 = (f32[3,4,32,128]{3,2,1,0:T(8,128)S(1)}, f32[3,4,32,128]{3,2,1,0:T(8,128)S(1)}, u32[]{:S(2)}, u32[]{:S(2)}) collective-permute-start(f32[3,4,32,128]{3,2,1,0:T(8,128)S(1)} %get-tuple-element.42), channel_id=1, source_target_pairs={{2,4},{3,5},{6,8},{7,9},{10,12},{11,13},{4,2},{5,3},{8,6},{9,7},{1... | collective-permute-start | bytes 589832 | tf_op jit(solution)/shard_map/ppermute | solution.py:474
  53.8 5.1 %collective-permute-done.12.other = f32[3,4,32,128]{3,2,1,0:T(8,128)S(1)} collective-permute-done((f32[3,4,32,128]{3,2,1,0:T(8,128)S(1)}, f32[3,4,32,128]{3,2,1,0:T(8,128)S(1)}, u32[]{:S(2)}, u32[]{:S(2)}) %collective-permute-start.12) | collective-permute-done | bytes 196640 | tf_op jit(solution)/shard_map/ppermute | solution.py:474
  58.9 0.8 shard_map.56.own
  59.7 2.1 %collective-permute-start.14 = (f32[4,4,24,128]{3,2,1,0:T(8,128)S(1)}, f32[4,4,24,128]{3,2,1,0:T(8,128)S(1)}, u32[]{:S(2)}, u32[]{:S(2)}) collective-permute-start(f32[4,4,24,128]{3,2,1,0:T(8,128)S(1)} %shard_map.56.own), channel_id=1, source_target_pairs={{2,4},{3,5},{6,8},{7,9},{10,12},{11,13},{4,2},{5,3},{8,6},{9,7},{1... | collective-permute-start | bytes 589832 | tf_op jit(solution)/shard_map/ppermute | solution.py:494
  62.3 0.8 shard_map.54.own
  63.2 2.0 %collective-permute-start.10 = (f32[4,4,24,128]{3,2,1,0:T(8,128)S(1)}, f32[4,4,24,128]{3,2,1,0:T(8,128)S(1)}, u32[]{:S(2)}, u32[]{:S(2)}) collective-permute-start(f32[4,4,24,128]{3,2,1,0:T(8,128)S(1)} %shard_map.54.own), channel_id=1, source_target_pairs={{2,4},{3,5},{6,8},{7,9},{10,12},{11,13},{4,2},{5,3},{8,6},{9,7},{1... | collective-permute-start | bytes 589832 | tf_op jit(solution)/shard_map/ppermute | solution.py:494
  65.2 2.5 %collective-permute-done.14.other_own = f32[4,4,24,128]{3,2,1,0:T(8,128)S(1)} collective-permute-done((f32[4,4,24,128]{3,2,1,0:T(8,128)S(1)}, f32[4,4,24,128]{3,2,1,0:T(8,128)S(1)}, u32[]{:S(2)}, u32[]{:S(2)}) %collective-permute-start.14) | collective-permute-done | bytes 196640 | tf_op jit(solution)/shard_map/ppermute | solution.py:494
  67.7 0.9 %collective-permute-done.15.pair_own = f32[4,4,24,128]{3,2,1,0:T(8,128)S(1)} collective-permute-done((f32[4,4,24,128]{3,2,1,0:T(8,128)S(1)}, f32[4,4,24,128]{3,2,1,0:T(8,128)S(1)}, u32[]{:S(2)}, u32[]{:S(2)}) %collective-permute-start.15) | collective-permute-done | bytes 196640 | tf_op jit(solution)/shard_map/ppermute | solution.py:495
  68.6 1.1 %shard_map.57 = (f32[2,4,16,128]{3,2,1,0:T(8,128)S(1)}, f32[2,4,16,128]{3,2,1,0:T(8,128)S(1)}) custom-call(f32[4,4,32,128]{3,2,1,0:T(8,128)S(1)} %get-tuple-element.51.chip, f32[3,4,32,128]{3,2,1,0:T(8,128)S(1)} %collective-permute-done.12.other, f32[3,4,32,128]{3,2,1,0:T(8,128)S(1)} %collective-permute-done.13.pair, f32[10,15,32,128]{3,2,1,0:T(8,128)S(1)} %shard_map.53.cof, ...), custom_call_target="tpu_custom_call" | custom-call | tf_op jit(solution)/shard_map/pallas_call | solution.py:413
  69.8 2.0 %collective-permute-done.10.other_own = f32[4,4,24,128]{3,2,1,0:T(8,128)S(1)} collective-permute-done((f32[4,4,24,128]{3,2,1,0:T(8,128)S(1)}, f32[4,4,24,128]{3,2,1,0:T(8,128)S(1)}, u32[]{:S(2)}, u32[]{:S(2)}) %collective-permute-start.10) | collective-permute-done | bytes 196640 | tf_op jit(solution)/shard_map/ppermute | solution.py:494
  71.8 1.1 %shard_map.55 = (f32[2,4,16,128]{3,2,1,0:T(8,128)S(1)}, f32[2,4,16,128]{3,2,1,0:T(8,128)S(1)}) custom-call(f32[4,4,32,128]{3,2,1,0:T(8,128)S(1)} %get-tuple-element.41.chip, f32[3,4,32,128]{3,2,1,0:T(8,128)S(1)} %collective-permute-done.6.other, f32[3,4,32,128]{3,2,1,0:T(8,128)S(1)} %collective-permute-done.7.pair, f32[10,15,32,128]{3,2,1,0:T(8,128)S(1)} %shard_map.53.cof, ...), custom_call_target="tpu_custom_call" | custom-call | tf_op jit(solution)/shard_map/pallas_call | solution.py:413
  73.0 1.2 %collective-permute-done.16.refs_2_ = f32[2,4,16,128]{3,2,1,0:T(8,128)S(1)} collective-permute-done((f32[2,4,16,128]{3,2,1,0:T(8,128)S(1)}, f32[2,4,16,128]{3,2,1,0:T(8,128)S(1)}, u32[]{:S(2)}, u32[]{:S(2)}) %collective-permute-start.16) | collective-permute-done | bytes 65568 | tf_op jit(solution)/shard_map/ppermute | solution.py:508
  74.3 16.1 %all_to_all.11.correction = f32[16,2,16,128]{3,2,1,0:T(8,128)S(1)} all-to-all(f32[16,2,16,128]{3,2,1,0:T(8,128)S(1)} %shard_map.58), channel_id=1, replica_groups=mesh['tm'=16,'space'=16] {'tm'}, dimensions={0} | all-to-all | bytes 524288 | tf_op jit(solution)/shard_map/all_to_all | solution.py:510
  90.4 0.8 shard_map.59
  (30 shorter events, 3.6 us)
Async XLA Ops:
  0.0 13.1 %copy-start = (f32[1,2,128,256]{3,2,1,0:T(8,128)S(1)}, f32[1,2,128,256]{3,2,1,0:T(8,128)}, u32[]{:S(2)}) copy-start(f32[1,2,128,256]{3,2,1,0:T(8,128)} %iterate.5) | copy-start | bytes 786436
  1.6 2.4 %collective-permute-start.2 = (f32[2,128,256]{2,1,0:T(8,128)S(1)}, f32[2,128,256]{2,1,0:T(8,128)S(1)}, u32[]{:S(2)}, u32[]{:S(2)}) collective-permute-start(f32[2,128,256]{2,1,0:T(8,128)S(1)} %get-tuple-element.35), channel_id=1, source_target_pairs={{0,1},{1,0},{2,3},{3,2},{4,5},{5,4},{6,7},{7,6},{8,9},{9,8},{10,11... | collective-permute-start | bytes 786440 | tf_op jit(solution)/shard_map/ppermute | solution.py:442
  1.7 7.7 %collective-permute-start.1 = (f32[2,128,256]{2,1,0:T(8,128)S(1)}, f32[2,128,256]{2,1,0:T(8,128)S(1)}, u32[]{:S(2)}, u32[]{:S(2)}) collective-permute-start(f32[2,128,256]{2,1,0:T(8,128)S(1)} %get-tuple-element.33), channel_id=1, source_target_pairs={{1,2},{3,4},{5,6},{7,8},{9,10},{11,12},{13,14},{15,0},{2,1},{4,3},... | collective-permute-start | bytes 786440 | tf_op jit(solution)/shard_map/ppermute | solution.py:441
  2.6 10.6 %collective-permute-start = (f32[1,2,128,256]{3,2,1,0:T(8,128)}, f32[1,2,128,256]{3,2,1,0:T(8,128)S(1)}, u32[]{:S(2)}, u32[]{:S(2)}) collective-permute-start(f32[1,2,128,256]{3,2,1,0:T(8,128)} %iterate.5), channel_id=1, source_target_pairs={{0,16},{16,32},{32,48},{48,0},{64,80},{80,96},{96,112},{112,64},{1... | collective-permute-start | bytes 786440 | tf_op jit(solution)/shard_map/ppermute | solution.py:432
  4.1 6.4 %collective-permute-start.3 = (f32[4,2,32,128]{3,2,1,0:T(8,128)S(1)}, f32[4,2,32,128]{3,2,1,0:T(8,128)S(1)}, u32[]{:S(2)}, u32[]{:S(2)}) collective-permute-start(f32[4,2,32,128]{3,2,1,0:T(8,128)S(1)} %get-tuple-element.48.fields), channel_id=1, source_target_pairs={{0,2},{1,3},{2,0},{3,1},{4,6},{5,7},{6,4},{7,5},{8,10},{9,11},{10,... | collective-permute-start | bytes 393224 | tf_op jit(solution)/shard_map/ppermute | solution.py:444
  4.5 8.6 %collective-permute-start.4 = (f32[4,2,32,128]{3,2,1,0:T(8,128)S(1)}, f32[4,2,32,128]{3,2,1,0:T(8,128)S(1)}, u32[]{:S(2)}, u32[]{:S(2)}) collective-permute-start(f32[4,2,32,128]{3,2,1,0:T(8,128)S(1)} %get-tuple-element.48.fields), channel_id=1, source_target_pairs={{2,4},{3,5},{6,8},{7,9},{10,12},{11,13},{4,2},{5,3},{8,6},{9,7},{1... | collective-permute-start | bytes 393224 | tf_op jit(solution)/shard_map/ppermute | solution.py:445
  46.9 1.4 %collective-permute-start.8 = (f32[8,32,128]{2,1,0:T(8,128)S(1)}, f32[8,32,128]{2,1,0:T(8,128)S(1)}, u32[]{:S(2)}, u32[]{:S(2)}) collective-permute-start(f32[8,32,128]{2,1,0:T(8,128)S(1)} %get-tuple-element.46), channel_id=1, source_target_pairs={{0,1},{1,0},{2,3},{3,2},{4,5},{5,4},{6,7},{7,6},{8,9},{9,8},{10,11... | collective-permute-start | bytes 393224 | tf_op jit(solution)/shard_map/ppermute | solution.py:468
  48.5 4.9 %collective-permute-start.9 = (f32[3,4,2,32,128]{4,3,2,1,0:T(8,128)S(1)}, f32[3,4,2,32,128]{4,3,2,1,0:T(8,128)S(1)}, u32[]{:S(2)}, u32[]{:S(2)}) collective-permute-start(f32[3,4,2,32,128]{4,3,2,1,0:T(8,128)S(1)} %shard_map.52), channel_id=1, source_target_pairs={{0,1},{1,0},{2,3},{3,2},{4,5},{5,4},{6,7},{7,6},{8,9},{9,8},{10,11... | collective-permute-start | bytes 1179656 | tf_op jit(solution)/shard_map/ppermute | solution.py:478
  48.7 1.8 %collective-permute-start.5 = (f32[8,32,128]{2,1,0:T(8,128)S(1)}, f32[8,32,128]{2,1,0:T(8,128)S(1)}, u32[]{:S(2)}, u32[]{:S(2)}) collective-permute-start(f32[8,32,128]{2,1,0:T(8,128)S(1)} %get-tuple-element.40), channel_id=1, source_target_pairs={{0,1},{1,0},{2,3},{3,2},{4,5},{5,4},{6,7},{7,6},{8,9},{9,8},{10,11... | collective-permute-start | bytes 393224 | tf_op jit(solution)/shard_map/ppermute | solution.py:468
  49.1 9.9 %collective-permute-start.12 = (f32[3,4,32,128]{3,2,1,0:T(8,128)S(1)}, f32[3,4,32,128]{3,2,1,0:T(8,128)S(1)}, u32[]{:S(2)}, u32[]{:S(2)}) collective-permute-start(f32[3,4,32,128]{3,2,1,0:T(8,128)S(1)} %get-tuple-element.52), channel_id=1, source_target_pairs={{2,4},{3,5},{6,8},{7,9},{10,12},{11,13},{4,2},{5,3},{8,6},{9,7},{1... | collective-permute-start | bytes 589832 | tf_op jit(solution)/shard_map/ppermute | solution.py:474
  49.1 9.9 %collective-permute-start.13 = (f32[3,4,32,128]{3,2,1,0:T(8,128)S(1)}, f32[3,4,32,128]{3,2,1,0:T(8,128)S(1)}, u32[]{:S(2)}, u32[]{:S(2)}) collective-permute-start(f32[3,4,32,128]{3,2,1,0:T(8,128)S(1)} %get-tuple-element.53), channel_id=1, source_target_pairs={{0,2},{1,3},{2,0},{3,1},{4,6},{5,7},{6,4},{7,5},{8,10},{9,11},{10,... | collective-permute-start | bytes 589832 | tf_op jit(solution)/shard_map/ppermute | solution.py:475
  50.5 11.8 %collective-permute-start.6 = (f32[3,4,32,128]{3,2,1,0:T(8,128)S(1)}, f32[3,4,32,128]{3,2,1,0:T(8,128)S(1)}, u32[]{:S(2)}, u32[]{:S(2)}) collective-permute-start(f32[3,4,32,128]{3,2,1,0:T(8,128)S(1)} %get-tuple-element.42), channel_id=1, source_target_pairs={{2,4},{3,5},{6,8},{7,9},{10,12},{11,13},{4,2},{5,3},{8,6},{9,7},{1... | collective-permute-start | bytes 589832 | tf_op jit(solution)/shard_map/ppermute | solution.py:474
  53.4 9.0 %collective-permute-start.7 = (f32[3,4,32,128]{3,2,1,0:T(8,128)S(1)}, f32[3,4,32,128]{3,2,1,0:T(8,128)S(1)}, u32[]{:S(2)}, u32[]{:S(2)}) collective-permute-start(f32[3,4,32,128]{3,2,1,0:T(8,128)S(1)} %get-tuple-element.43), channel_id=1, source_target_pairs={{0,2},{1,3},{2,0},{3,1},{4,6},{5,7},{6,4},{7,5},{8,10},{9,11},{10,... | collective-permute-start | bytes 589832 | tf_op jit(solution)/shard_map/ppermute | solution.py:475
  59.7 8.0 %collective-permute-start.14 = (f32[4,4,24,128]{3,2,1,0:T(8,128)S(1)}, f32[4,4,24,128]{3,2,1,0:T(8,128)S(1)}, u32[]{:S(2)}, u32[]{:S(2)}) collective-permute-start(f32[4,4,24,128]{3,2,1,0:T(8,128)S(1)} %shard_map.56.own), channel_id=1, source_target_pairs={{2,4},{3,5},{6,8},{7,9},{10,12},{11,13},{4,2},{5,3},{8,6},{9,7},{1... | collective-permute-start | bytes 589832 | tf_op jit(solution)/shard_map/ppermute | solution.py:494
  61.9 6.7 %collective-permute-start.15 = (f32[4,4,24,128]{3,2,1,0:T(8,128)S(1)}, f32[4,4,24,128]{3,2,1,0:T(8,128)S(1)}, u32[]{:S(2)}, u32[]{:S(2)}) collective-permute-start(f32[4,4,24,128]{3,2,1,0:T(8,128)S(1)} %shard_map.56.own), channel_id=1, source_target_pairs={{0,2},{1,3},{2,0},{3,1},{4,6},{5,7},{6,4},{7,5},{8,10},{9,11},{10,... | collective-permute-start | bytes 589832 | tf_op jit(solution)/shard_map/ppermute | solution.py:495
  63.2 8.7 %collective-permute-start.10 = (f32[4,4,24,128]{3,2,1,0:T(8,128)S(1)}, f32[4,4,24,128]{3,2,1,0:T(8,128)S(1)}, u32[]{:S(2)}, u32[]{:S(2)}) collective-permute-start(f32[4,4,24,128]{3,2,1,0:T(8,128)S(1)} %shard_map.54.own), channel_id=1, source_target_pairs={{2,4},{3,5},{6,8},{7,9},{10,12},{11,13},{4,2},{5,3},{8,6},{9,7},{1... | collective-permute-start | bytes 589832 | tf_op jit(solution)/shard_map/ppermute | solution.py:494
  65.2 6.7 %collective-permute-start.11 = (f32[4,4,24,128]{3,2,1,0:T(8,128)S(1)}, f32[4,4,24,128]{3,2,1,0:T(8,128)S(1)}, u32[]{:S(2)}, u32[]{:S(2)}) collective-permute-start(f32[4,4,24,128]{3,2,1,0:T(8,128)S(1)} %shard_map.54.own), channel_id=1, source_target_pairs={{0,2},{1,3},{2,0},{3,1},{4,6},{5,7},{6,4},{7,5},{8,10},{9,11},{10,... | collective-permute-start | bytes 589832 | tf_op jit(solution)/shard_map/ppermute | solution.py:495
  69.7 3.3 %collective-permute-start.17 = (f32[2,4,16,128]{3,2,1,0:T(8,128)S(1)}, f32[2,4,16,128]{3,2,1,0:T(8,128)S(1)}, u32[]{:S(2)}, u32[]{:S(2)}) collective-permute-start(f32[2,4,16,128]{3,2,1,0:T(8,128)S(1)} %get-tuple-element.56), channel_id=1, source_target_pairs={{0,1},{1,0},{2,3},{3,2},{4,5},{5,4},{6,7},{7,6},{8,9},{9,8},{10,11... | collective-permute-start | bytes 196616 | tf_op jit(solution)/shard_map/ppermute | solution.py:508
  72.9 1.3 %collective-permute-start.16 = (f32[2,4,16,128]{3,2,1,0:T(8,128)S(1)}, f32[2,4,16,128]{3,2,1,0:T(8,128)S(1)}, u32[]{:S(2)}, u32[]{:S(2)}) collective-permute-start(f32[2,4,16,128]{3,2,1,0:T(8,128)S(1)} %get-tuple-element.55), channel_id=1, source_target_pairs={{0,1},{1,0},{2,3},{3,2},{4,5},{5,4},{6,7},{7,6},{8,9},{9,8},{10,11... | collective-permute-start | bytes 196616 | tf_op jit(solution)/shard_map/ppermute | solution.py:508

commit v6 on v5

--- a/solution.py
+++ b/solution.py
@@ -99,12 +99,14 @@
     return copies
 
 
-def entry_kernel(iterate, kappa, velocity, outer, inner, out, held, turned, sems):
+def entry_kernel(iterate, kappa, velocity, first, second, outer, inner, out, held, turned, sems):
     step = lax.axis_index("tm")
     parity = lax.axis_index("space") % 2
     pairs = [(kappa, held.at[0])]
     pairs += [(velocity.at[d], held.at[1 + d]) for d in range(3)]
     pairs += [
+        (iterate.at[0, 0], first),
+        (iterate.at[0, 1], second),
         (iterate.at[0, parity], outer.at[0]),
         (kappa.at[parity], outer.at[1]),
         (iterate.at[0, 1 - parity], inner.at[0]),
@@ -155,7 +157,7 @@
         base[plane] = forcing[0, plane] - here * (1.0 / TIME_STEP) - (diagonal * here - total)
 
 
-def resid_kernel(base, rim, iterate, previous, outer, inner, out, turned):
+def resid_kernel(base, rim, iterate, first, second, outer, inner, out, turned):
     step = lax.axis_index("tm")
     place = lax.axis_index("space")
     even = place % 2 == 0
@@ -168,7 +170,7 @@
         spot[8 : 8 + NX] = array.T
         spot[8 + NX : 16 + NX] = edge
 
-    carried = jnp.where(leads, 0.0, 1.0 / TIME_STEP)
+    before = (first, second)
     skip = jnp.where(leads, 0, 8)
     for plane in range(SLAB):
         side, other = (outer, inner) if plane == 0 else (inner, outer)
@@ -176,16 +178,17 @@
         here = iterate[0, plane]
         near = jnp.where(ends, 0.0, jnp.where(even, side[0], other[0]))
         far = jnp.where(ends, 0.0, 0.5 * jnp.where(even, side[1], other[1]))
-        resid = base[plane] + previous[0, plane] * carried + (rim[plane] + far) * near - far * here
+        carried = jnp.where(step == 0 if plane == 0 else leads, 0.0, 1.0 / TIME_STEP)
+        resid = base[plane] + before[plane][...] * carried + (rim[plane] + far) * near - far * here
         turn(turned.at[plane], resid * growth)
         for c in range(WINDOW):
             out[c, WIDE * plane : WIDE * (plane + 1)] = turned[plane, OWN * c : OWN * c + WIDE]
-        turn(turned.at[SLAB + plane], jnp.where(leads, previous[0, plane], here))
-        for c in range(WINDOW):
-            for number in range(2):
-                start = pl.multiple_of(OWN * c + OWN * number + skip, 8)
-                spot = SLAB * WIDE + EXTRA * plane + 8 * number
-                out[c, spot : spot + 8] = turned[SLAB + plane, pl.ds(start, 8)]
+    turn(turned.at[SLAB], jnp.where(leads, second[...], iterate[0, 1]))
+    for c in range(WINDOW):
+        for number in range(2):
+            start = pl.multiple_of(OWN * c + OWN * number + skip, 8)
+            spot = SLAB * WIDE + 8 * number
+            out[c, spot : spot + 8] = turned[SLAB, pl.ds(start, 8)]
 
 
 def ahead_kernel(times, *outs):
@@ -195,8 +198,8 @@
         for tile in range(WIDE // 8):
             rows = slice(8 * tile, 8 * tile + 8)
             values = [times[n, WIDE * plane + 8 * tile : WIDE * plane + 8 * tile + 8] for n in range(WINDOW)]
-            spot = SLAB * WIDE + EXTRA * plane + 8 * (tile // 2)
-            for n in (4, 8, 12):
+            spot = SLAB * WIDE + 8 * (tile // 2)
+            for n in (4, 8, 12) if plane == 1 else ():
                 source = n - 1 if tile % 2 else n - 4
                 values[n] += times[source, spot : spot + 8] * (time_scale(n) / TIME_STEP)
             parts = spectrum_of(values)
@@ -429,15 +432,16 @@
     others += [(i, i ^ 1) for i in (0, 1, 2 * CHIPS - 2, 2 * CHIPS - 1)]
     facing = [(i, (i + 1) % (2 * CHIPS)) for i in range(1, 2 * CHIPS, 2)]
     facing += [(j, i) for i, j in facing]
-    previous = lax.ppermute(iterate, "tm", [(i, i // 4 * 4 + (i + 1) % 4) for i in range(WINDOW)])
-    outer, inner, fields = call(
+    first, second, outer, inner, fields = call(
         entry_kernel,
-        [block, block, (4, SLAB, WIDE, NY)],
+        [(NY, NX), (NY, NX), block, block, (4, SLAB, WIDE, NY)],
         (iterate, kappa, velocity),
-        [(4, *block), (8, NX + 16, NY), pltpu.SemaphoreType.DMA((8,))],
+        [(4, *block), (8, NX + 16, NY), pltpu.SemaphoreType.DMA((10,))],
         anywhere=True,
-        mib=53.25,
-    )
+        mib=53,
+    )
+    first = lax.ppermute(first, "tm", [(i, (i + 1) % WINDOW) for i in range(WINDOW)])
+    second = lax.ppermute(second, "tm", [(i, i // 4 * 4 + (i + 1) % 4) for i in range(WINDOW)])
     outer = lax.ppermute(outer, "space", facing)
     inner = lax.ppermute(inner, "space", cores)
     fields, inner = lax.optimization_barrier((fields, inner))
@@ -454,9 +458,9 @@
     outer, fields_pair, fields_other = lax.optimization_barrier((outer, fields_pair, fields_other))
     sent = call(
         resid_kernel,
-        (WINDOW, SLAB * (WIDE + EXTRA), NY),
-        (base, rim, iterate, previous, outer, inner),
-        [(2 * SLAB, NX + 16, NY)],
+        (WINDOW, SLAB * WIDE + EXTRA, NY),
+        (base, rim, iterate, first, second, outer, inner),
+        [(SLAB + 1, NX + 16, NY)],
     )
     times = lax.all_to_all(sent, "tm", 0, 0)
     parts = call(

time: 91.8 us -> 91.1 us (level)
  blocking collectives: 49.5 us -> 38.9 us
  waiting for transfers between devices: 17.9 us -> 26.3 us
  starting transfers between devices: 14.5 us -> 16.2 us
    all_to_all x1, blocking collectives: 33.4 us -> 22.4 us  [shards(): times = lax.all_to_all(sent, 'tm', 0, 0)]
    ppermute x1 -> x2, waiting for transfers between devices: 0.02 us -> 10.1 us  [the longest x1 10.1 us: shards(): lax.ppermute(first, 'tm', [(i, (i + 1) % WINDOW) for i in range(WINDOW)])]
    ppermute x1 -> x2, starting transfers between devices: 1.49 us -> 2.98 us  [the longest x1 1.49 us: shards(): lax.ppermute(first, 'tm', [(i, (i + 1) % WINDOW) for i in range(WINDOW)])]
    ppermute x1, waiting for transfers between devices: 0.99 us -> 0.01 us  [shards(): fields_pair = lax.ppermute(fields, 'space', pairs)]
    ppermute x1, waiting for transfers between devices: 2.7 us -> 1.76 us  [shards(): fields_other = lax.ppermute(fields, 'space', others)]
  transfers between devices with their start and end apart: 18 -> 19, of which waited for: 10 -> 10; matrix products, arithmetic and copies ran while one was open for 0% -> 0% of each run, Pallas kernels for 7% -> 7%
where the time goes in v6:
time: 91.1 us; the launch traced here: 90.8 us
  blocking collectives  38.9 us (43%)
  waiting for transfers between devices  26.3 us (29%)
  starting transfers between devices  16.2 us (18%)
  Pallas kernels  9.18 us (10%)
    all_to_all x1, blocking collectives, shards(): times = lax.all_to_all(sent, 'tm', 0, 0)  22.4 us
    all_to_all x1, blocking collectives, shards(): correction = lax.all_to_all(correction, 'tm', 0, 0)  16.5 us
    ppermute x1, waiting for transfers between devices, shards(): lax.ppermute(first, 'tm', [(i, (i + 1) % WINDOW) for i in range(WINDOW)])  10.1 us
    pallas_call x14, Pallas kernels, call(): pl.pallas_call(kernel, out_shape=out_shape if several else out_shape[0],...  9.18 us
    ppermute x2, waiting for transfers between devices, shards(): other_specs.append(lax.ppermute(other, 'space', others))  5.53 us
    ppermute x2, waiting for transfers between devices, shards(): other_owns.append(lax.ppermute(own, 'space', others))  4.71 us
    ppermute x2, starting transfers between devices, shards(): other_owns.append(lax.ppermute(own, 'space', others))  3.98 us
    ppermute x2, starting transfers between devices, shards(): other_specs.append(lax.ppermute(other, 'space', others))  3.03 us
  transfers between devices with their start and end apart: 19, of which 10 were waited for; matrix products, arithmetic and copies ran while one was open for 0% of the time, Pallas kernels for 7%

profile of v6, /device:TPU:24, one launch (start us, length us, event | category | flops | bytes accessed | tf_op | source)
XLA Modules:
  0.0 90.8 jit_solution(13087726824316537120)
XLA Ops:
  0.0 1.6 %shard_map.47 = (f32[128,256]{1,0:T(8,128)S(1)}, f32[128,256]{1,0:T(8,128)S(1)}, f32[2,128,256]{2,1,0:T(8,128)S(1)}, f32[2,128,256]{2,1,0:T(8,128)S(1)}, f32[4,2,32,128]{3,2,1,0:T(8,128)S(1)}) custom-call(f32[1,2,128,256]{3,2,1,0:T(8,128)} %iterate.5, f32[2,128,256]{2,1,0:T(8,128)} %kappa.1, f32[3,2,128,256]{3,2,1,0:T(8,128)} %velocity.1), custom_call_target="tpu_custom_call" | custom-call | tf_op jit(solution)/shard_map/pallas_call | solution.py:416
  1.7 0.8 collective-permute-start.2
  4.0 2.4 %collective-permute-start.5 = (f32[4,2,32,128]{3,2,1,0:T(8,128)S(1)}, f32[4,2,32,128]{3,2,1,0:T(8,128)S(1)}, u32[]{:S(2)}, u32[]{:S(2)}) collective-permute-start(f32[4,2,32,128]{3,2,1,0:T(8,128)S(1)} %get-tuple-element.52.fields), channel_id=1, source_target_pairs={{2,4},{3,5},{6,8},{7,9},{10,12},{11,13},{4,2},{5,3},{8,6},{9,7},{1... | collective-permute-start | bytes 393224 | tf_op jit(solution)/shard_map/ppermute | solution.py:449
  6.4 1.5 %collective-permute-start = (f32[128,256]{1,0:T(8,128)S(1)}, f32[128,256]{1,0:T(8,128)S(1)}, u32[]{:S(2)}, u32[]{:S(2)}) collective-permute-start(f32[128,256]{1,0:T(8,128)S(1)} %get-tuple-element.35), channel_id=1, source_target_pairs={{0,16},{16,32},{32,48},{48,64},{64,80},{80,96},{96,112},{112,128},... | collective-permute-start | bytes 393224 | tf_op jit(solution)/shard_map/ppermute | solution.py:443
  7.9 1.5 %collective-permute-start.1 = (f32[128,256]{1,0:T(8,128)S(1)}, f32[128,256]{1,0:T(8,128)S(1)}, u32[]{:S(2)}, u32[]{:S(2)}) collective-permute-start(f32[128,256]{1,0:T(8,128)S(1)} %get-tuple-element.36), channel_id=1, source_target_pairs={{0,16},{16,32},{32,48},{48,0},{64,80},{80,96},{96,112},{112,64},{1... | collective-permute-start | bytes 393224 | tf_op jit(solution)/shard_map/ppermute | solution.py:444
  9.4 1.9 %shard_map.46 = (f32[2,128,256]{2,1,0:T(8,128)S(1)}, f32[2,128,256]{2,1,0:T(8,128)S(1)}) custom-call(f32[1,2,128,256]{3,2,1,0:T(8,128)} %forcing_hbm.1, f32[1,2,128,256]{3,2,1,0:T(8,128)} %iterate.5, f32[2,128,256]{2,1,0:T(8,128)} %kappa.1, f32[3,2,128,256]{3,2,1,0:T(8,128)} %velocity.1), custom_call_target="tpu_custom_call" | custom-call | tf_op jit(solution)/shard_map/pallas_call | solution.py:416
  11.4 1.8 %collective-permute-done.5.other = f32[4,2,32,128]{3,2,1,0:T(8,128)S(1)} collective-permute-done((f32[4,2,32,128]{3,2,1,0:T(8,128)S(1)}, f32[4,2,32,128]{3,2,1,0:T(8,128)S(1)}, u32[]{:S(2)}, u32[]{:S(2)}) %collective-permute-start.5) | collective-permute-done | bytes 131104 | tf_op jit(solution)/shard_map/ppermute | solution.py:449
  13.1 10.1 %collective-permute-done.first = f32[128,256]{1,0:T(8,128)S(1)} collective-permute-done((f32[128,256]{1,0:T(8,128)S(1)}, f32[128,256]{1,0:T(8,128)S(1)}, u32[]{:S(2)}, u32[]{:S(2)}) %collective-permute-start) | collective-permute-done | bytes 131104 | tf_op jit(solution)/shard_map/ppermute | solution.py:443
  23.5 22.4 %all_to_all.10.times = f32[16,80,128]{2,1,0:T(8,128)S(1)} all-to-all(f32[16,80,128]{2,1,0:T(8,128)S(1)} %shard_map.48), channel_id=1, replica_groups=mesh['tm'=16,'space'=16] {'tm'}, dimensions={0} | all-to-all | bytes 1310720 | tf_op jit(solution)/shard_map/all_to_all | solution.py:465
  46.1 1.3 %collective-permute-done.9.got = f32[8,32,128]{2,1,0:T(8,128)S(1)} collective-permute-done((f32[8,32,128]{2,1,0:T(8,128)S(1)}, f32[8,32,128]{2,1,0:T(8,128)S(1)}, u32[]{:S(2)}, u32[]{:S(2)}) %collective-permute-start.9) | collective-permute-done | bytes 131104 | tf_op jit(solution)/shard_map/ppermute | solution.py:472
  48.9 1.2 %collective-permute-start.14 = (f32[3,4,32,128]{3,2,1,0:T(8,128)S(1)}, f32[3,4,32,128]{3,2,1,0:T(8,128)S(1)}, u32[]{:S(2)}, u32[]{:S(2)}) collective-permute-start(f32[3,4,32,128]{3,2,1,0:T(8,128)S(1)} %get-tuple-element.57), channel_id=1, source_target_pairs={{0,2},{1,3},{2,0},{3,1},{4,6},{5,7},{6,4},{7,5},{8,10},{9,11},{10,... | collective-permute-start | bytes 589832 | tf_op jit(solution)/shard_map/ppermute | solution.py:479
  50.2 2.3 %collective-permute-start.7 = (f32[3,4,32,128]{3,2,1,0:T(8,128)S(1)}, f32[3,4,32,128]{3,2,1,0:T(8,128)S(1)}, u32[]{:S(2)}, u32[]{:S(2)}) collective-permute-start(f32[3,4,32,128]{3,2,1,0:T(8,128)S(1)} %get-tuple-element.46), channel_id=1, source_target_pairs={{2,4},{3,5},{6,8},{7,9},{10,12},{11,13},{4,2},{5,3},{8,6},{9,7},{1... | collective-permute-start | bytes 589832 | tf_op jit(solution)/shard_map/ppermute | solution.py:478
  52.9 5.1 %collective-permute-done.13.other = f32[3,4,32,128]{3,2,1,0:T(8,128)S(1)} collective-permute-done((f32[3,4,32,128]{3,2,1,0:T(8,128)S(1)}, f32[3,4,32,128]{3,2,1,0:T(8,128)S(1)}, u32[]{:S(2)}, u32[]{:S(2)}) %collective-permute-start.13) | collective-permute-done | bytes 196640 | tf_op jit(solution)/shard_map/ppermute | solution.py:478
  58.8 2.1 %collective-permute-start.15 = (f32[4,4,24,128]{3,2,1,0:T(8,128)S(1)}, f32[4,4,24,128]{3,2,1,0:T(8,128)S(1)}, u32[]{:S(2)}, u32[]{:S(2)}) collective-permute-start(f32[4,4,24,128]{3,2,1,0:T(8,128)S(1)} %shard_map.56.own), channel_id=1, source_target_pairs={{2,4},{3,5},{6,8},{7,9},{10,12},{11,13},{4,2},{5,3},{8,6},{9,7},{1... | collective-permute-start | bytes 589832 | tf_op jit(solution)/shard_map/ppermute | solution.py:498
  61.4 0.8 shard_map.54.own
  62.2 1.8 %collective-permute-start.11 = (f32[4,4,24,128]{3,2,1,0:T(8,128)S(1)}, f32[4,4,24,128]{3,2,1,0:T(8,128)S(1)}, u32[]{:S(2)}, u32[]{:S(2)}) collective-permute-start(f32[4,4,24,128]{3,2,1,0:T(8,128)S(1)} %shard_map.54.own), channel_id=1, source_target_pairs={{2,4},{3,5},{6,8},{7,9},{10,12},{11,13},{4,2},{5,3},{8,6},{9,7},{1... | collective-permute-start | bytes 589832 | tf_op jit(solution)/shard_map/ppermute | solution.py:498
  64.1 2.9 %collective-permute-done.15.other_own = f32[4,4,24,128]{3,2,1,0:T(8,128)S(1)} collective-permute-done((f32[4,4,24,128]{3,2,1,0:T(8,128)S(1)}, f32[4,4,24,128]{3,2,1,0:T(8,128)S(1)}, u32[]{:S(2)}, u32[]{:S(2)}) %collective-permute-start.15) | collective-permute-done | bytes 196640 | tf_op jit(solution)/shard_map/ppermute | solution.py:498
  67.0 1.0 %collective-permute-done.16.pair_own = f32[4,4,24,128]{3,2,1,0:T(8,128)S(1)} collective-permute-done((f32[4,4,24,128]{3,2,1,0:T(8,128)S(1)}, f32[4,4,24,128]{3,2,1,0:T(8,128)S(1)}, u32[]{:S(2)}, u32[]{:S(2)}) %collective-permute-start.16) | collective-permute-done | bytes 196640 | tf_op jit(solution)/shard_map/ppermute | solution.py:499
  67.9 1.1 %shard_map.57 = (f32[2,4,16,128]{3,2,1,0:T(8,128)S(1)}, f32[2,4,16,128]{3,2,1,0:T(8,128)S(1)}) custom-call(f32[4,4,32,128]{3,2,1,0:T(8,128)S(1)} %get-tuple-element.55.chip, f32[3,4,32,128]{3,2,1,0:T(8,128)S(1)} %collective-permute-done.13.other, f32[3,4,32,128]{3,2,1,0:T(8,128)S(1)} %collective-permute-done.14.pair, f32[10,15,32,128]{3,2,1,0:T(8,128)S(1)} %shard_map.53.cof, ...), custom_call_target="tpu_custom_call" | custom-call | tf_op jit(solution)/shard_map/pallas_call | solution.py:416
  69.1 1.8 %collective-permute-done.11.other_own = f32[4,4,24,128]{3,2,1,0:T(8,128)S(1)} collective-permute-done((f32[4,4,24,128]{3,2,1,0:T(8,128)S(1)}, f32[4,4,24,128]{3,2,1,0:T(8,128)S(1)}, u32[]{:S(2)}, u32[]{:S(2)}) %collective-permute-start.11) | collective-permute-done | bytes 196640 | tf_op jit(solution)/shard_map/ppermute | solution.py:498
  70.9 1.1 %shard_map.55 = (f32[2,4,16,128]{3,2,1,0:T(8,128)S(1)}, f32[2,4,16,128]{3,2,1,0:T(8,128)S(1)}) custom-call(f32[4,4,32,128]{3,2,1,0:T(8,128)S(1)} %get-tuple-element.45.chip, f32[3,4,32,128]{3,2,1,0:T(8,128)S(1)} %collective-permute-done.7.other, f32[3,4,32,128]{3,2,1,0:T(8,128)S(1)} %collective-permute-done.8.pair, f32[10,15,32,128]{3,2,1,0:T(8,128)S(1)} %shard_map.53.cof, ...), custom_call_target="tpu_custom_call" | custom-call | tf_op jit(solution)/shard_map/pallas_call | solution.py:416
  72.1 1.2 %collective-permute-done.17.refs_2_ = f32[2,4,16,128]{3,2,1,0:T(8,128)S(1)} collective-permute-done((f32[2,4,16,128]{3,2,1,0:T(8,128)S(1)}, f32[2,4,16,128]{3,2,1,0:T(8,128)S(1)}, u32[]{:S(2)}, u32[]{:S(2)}) %collective-permute-start.17) | collective-permute-done | bytes 65568 | tf_op jit(solution)/shard_map/ppermute | solution.py:512
  73.4 16.5 %all_to_all.11.correction = f32[16,2,16,128]{3,2,1,0:T(8,128)S(1)} all-to-all(f32[16,2,16,128]{3,2,1,0:T(8,128)S(1)} %shard_map.58), channel_id=1, replica_groups=mesh['tm'=16,'space'=16] {'tm'}, dimensions={0} | all-to-all | bytes 524288 | tf_op jit(solution)/shard_map/all_to_all | solution.py:514
  89.9 0.8 shard_map.59
  (32 shorter events, 5.5 us)
Async XLA Ops:
  0.0 23.2 %copy-start = (f32[1,2,128,256]{3,2,1,0:T(8,128)S(1)}, f32[1,2,128,256]{3,2,1,0:T(8,128)}, u32[]{:S(2)}) copy-start(f32[1,2,128,256]{3,2,1,0:T(8,128)} %iterate.5) | copy-start | bytes 786436
  1.6 1.6 %collective-permute-start.3 = (f32[2,128,256]{2,1,0:T(8,128)S(1)}, f32[2,128,256]{2,1,0:T(8,128)S(1)}, u32[]{:S(2)}, u32[]{:S(2)}) collective-permute-start(f32[2,128,256]{2,1,0:T(8,128)S(1)} %get-tuple-element.39), channel_id=1, source_target_pairs={{0,1},{1,0},{2,3},{3,2},{4,5},{5,4},{6,7},{7,6},{8,9},{9,8},{10,11... | collective-permute-start | bytes 786440 | tf_op jit(solution)/shard_map/ppermute | solution.py:446
  1.7 9.6 %collective-permute-start.2 = (f32[2,128,256]{2,1,0:T(8,128)S(1)}, f32[2,128,256]{2,1,0:T(8,128)S(1)}, u32[]{:S(2)}, u32[]{:S(2)}) collective-permute-start(f32[2,128,256]{2,1,0:T(8,128)S(1)} %get-tuple-element.37), channel_id=1, source_target_pairs={{1,2},{3,4},{5,6},{7,8},{9,10},{11,12},{13,14},{15,0},{2,1},{4,3},... | collective-permute-start | bytes 786440 | tf_op jit(solution)/shard_map/ppermute | solution.py:445
  3.3 8.1 %collective-permute-start.4 = (f32[4,2,32,128]{3,2,1,0:T(8,128)S(1)}, f32[4,2,32,128]{3,2,1,0:T(8,128)S(1)}, u32[]{:S(2)}, u32[]{:S(2)}) collective-permute-start(f32[4,2,32,128]{3,2,1,0:T(8,128)S(1)} %get-tuple-element.52.fields), channel_id=1, source_target_pairs={{0,2},{1,3},{2,0},{3,1},{4,6},{5,7},{6,4},{7,5},{8,10},{9,11},{10,... | collective-permute-start | bytes 393224 | tf_op jit(solution)/shard_map/ppermute | solution.py:448
  4.0 9.1 %collective-permute-start.5 = (f32[4,2,32,128]{3,2,1,0:T(8,128)S(1)}, f32[4,2,32,128]{3,2,1,0:T(8,128)S(1)}, u32[]{:S(2)}, u32[]{:S(2)}) collective-permute-start(f32[4,2,32,128]{3,2,1,0:T(8,128)S(1)} %get-tuple-element.52.fields), channel_id=1, source_target_pairs={{2,4},{3,5},{6,8},{7,9},{10,12},{11,13},{4,2},{5,3},{8,6},{9,7},{1... | collective-permute-start | bytes 393224 | tf_op jit(solution)/shard_map/ppermute | solution.py:449
  6.4 16.8 %collective-permute-start = (f32[128,256]{1,0:T(8,128)S(1)}, f32[128,256]{1,0:T(8,128)S(1)}, u32[]{:S(2)}, u32[]{:S(2)}) collective-permute-start(f32[128,256]{1,0:T(8,128)S(1)} %get-tuple-element.35), channel_id=1, source_target_pairs={{0,16},{16,32},{32,48},{48,64},{64,80},{80,96},{96,112},{112,128},... | collective-permute-start | bytes 393224 | tf_op jit(solution)/shard_map/ppermute | solution.py:443
  7.9 15.3 %collective-permute-start.1 = (f32[128,256]{1,0:T(8,128)S(1)}, f32[128,256]{1,0:T(8,128)S(1)}, u32[]{:S(2)}, u32[]{:S(2)}) collective-permute-start(f32[128,256]{1,0:T(8,128)S(1)} %get-tuple-element.36), channel_id=1, source_target_pairs={{0,16},{16,32},{32,48},{48,0},{64,80},{80,96},{96,112},{112,64},{1... | collective-permute-start | bytes 393224 | tf_op jit(solution)/shard_map/ppermute | solution.py:444
  46.0 1.4 %collective-permute-start.9 = (f32[8,32,128]{2,1,0:T(8,128)S(1)}, f32[8,32,128]{2,1,0:T(8,128)S(1)}, u32[]{:S(2)}, u32[]{:S(2)}) collective-permute-start(f32[8,32,128]{2,1,0:T(8,128)S(1)} %get-tuple-element.50), channel_id=1, source_target_pairs={{0,1},{1,0},{2,3},{3,2},{4,5},{5,4},{6,7},{7,6},{8,9},{9,8},{10,11... | collective-permute-start | bytes 393224 | tf_op jit(solution)/shard_map/ppermute | solution.py:472
  47.5 4.9 %collective-permute-start.10 = (f32[3,4,2,32,128]{4,3,2,1,0:T(8,128)S(1)}, f32[3,4,2,32,128]{4,3,2,1,0:T(8,128)S(1)}, u32[]{:S(2)}, u32[]{:S(2)}) collective-permute-start(f32[3,4,2,32,128]{4,3,2,1,0:T(8,128)S(1)} %shard_map.52), channel_id=1, source_target_pairs={{0,1},{1,0},{2,3},{3,2},{4,5},{5,4},{6,7},{7,6},{8,9},{9,8},{10,11... | collective-permute-start | bytes 1179656 | tf_op jit(solution)/shard_map/ppermute | solution.py:482
  47.8 2.3 %collective-permute-start.6 = (f32[8,32,128]{2,1,0:T(8,128)S(1)}, f32[8,32,128]{2,1,0:T(8,128)S(1)}, u32[]{:S(2)}, u32[]{:S(2)}) collective-permute-start(f32[8,32,128]{2,1,0:T(8,128)S(1)} %get-tuple-element.44), channel_id=1, source_target_pairs={{0,1},{1,0},{2,3},{3,2},{4,5},{5,4},{6,7},{7,6},{8,9},{9,8},{10,11... | collective-permute-start | bytes 393224 | tf_op jit(solution)/shard_map/ppermute | solution.py:472
  48.1 9.9 %collective-permute-start.13 = (f32[3,4,32,128]{3,2,1,0:T(8,128)S(1)}, f32[3,4,32,128]{3,2,1,0:T(8,128)S(1)}, u32[]{:S(2)}, u32[]{:S(2)}) collective-permute-start(f32[3,4,32,128]{3,2,1,0:T(8,128)S(1)} %get-tuple-element.56), channel_id=1, source_target_pairs={{2,4},{3,5},{6,8},{7,9},{10,12},{11,13},{4,2},{5,3},{8,6},{9,7},{1... | collective-permute-start | bytes 589832 | tf_op jit(solution)/shard_map/ppermute | solution.py:478
  48.9 9.1 %collective-permute-start.14 = (f32[3,4,32,128]{3,2,1,0:T(8,128)S(1)}, f32[3,4,32,128]{3,2,1,0:T(8,128)S(1)}, u32[]{:S(2)}, u32[]{:S(2)}) collective-permute-start(f32[3,4,32,128]{3,2,1,0:T(8,128)S(1)} %get-tuple-element.57), channel_id=1, source_target_pairs={{0,2},{1,3},{2,0},{3,1},{4,6},{5,7},{6,4},{7,5},{8,10},{9,11},{10,... | collective-permute-start | bytes 589832 | tf_op jit(solution)/shard_map/ppermute | solution.py:479
  50.2 11.2 %collective-permute-start.7 = (f32[3,4,32,128]{3,2,1,0:T(8,128)S(1)}, f32[3,4,32,128]{3,2,1,0:T(8,128)S(1)}, u32[]{:S(2)}, u32[]{:S(2)}) collective-permute-start(f32[3,4,32,128]{3,2,1,0:T(8,128)S(1)} %get-tuple-element.46), channel_id=1, source_target_pairs={{2,4},{3,5},{6,8},{7,9},{10,12},{11,13},{4,2},{5,3},{8,6},{9,7},{1... | collective-permute-start | bytes 589832 | tf_op jit(solution)/shard_map/ppermute | solution.py:478
  52.4 9.0 %collective-permute-start.8 = (f32[3,4,32,128]{3,2,1,0:T(8,128)S(1)}, f32[3,4,32,128]{3,2,1,0:T(8,128)S(1)}, u32[]{:S(2)}, u32[]{:S(2)}) collective-permute-start(f32[3,4,32,128]{3,2,1,0:T(8,128)S(1)} %get-tuple-element.47), channel_id=1, source_target_pairs={{0,2},{1,3},{2,0},{3,1},{4,6},{5,7},{6,4},{7,5},{8,10},{9,11},{10,... | collective-permute-start | bytes 589832 | tf_op jit(solution)/shard_map/ppermute | solution.py:479
  58.8 8.1 %collective-permute-start.15 = (f32[4,4,24,128]{3,2,1,0:T(8,128)S(1)}, f32[4,4,24,128]{3,2,1,0:T(8,128)S(1)}, u32[]{:S(2)}, u32[]{:S(2)}) collective-permute-start(f32[4,4,24,128]{3,2,1,0:T(8,128)S(1)} %shard_map.56.own), channel_id=1, source_target_pairs={{2,4},{3,5},{6,8},{7,9},{10,12},{11,13},{4,2},{5,3},{8,6},{9,7},{1... | collective-permute-start | bytes 589832 | tf_op jit(solution)/shard_map/ppermute | solution.py:498
  61.0 6.9 %collective-permute-start.16 = (f32[4,4,24,128]{3,2,1,0:T(8,128)S(1)}, f32[4,4,24,128]{3,2,1,0:T(8,128)S(1)}, u32[]{:S(2)}, u32[]{:S(2)}) collective-permute-start(f32[4,4,24,128]{3,2,1,0:T(8,128)S(1)} %shard_map.56.own), channel_id=1, source_target_pairs={{0,2},{1,3},{2,0},{3,1},{4,6},{5,7},{6,4},{7,5},{8,10},{9,11},{10,... | collective-permute-start | bytes 589832 | tf_op jit(solution)/shard_map/ppermute | solution.py:499
  62.2 8.7 %collective-permute-start.11 = (f32[4,4,24,128]{3,2,1,0:T(8,128)S(1)}, f32[4,4,24,128]{3,2,1,0:T(8,128)S(1)}, u32[]{:S(2)}, u32[]{:S(2)}) collective-permute-start(f32[4,4,24,128]{3,2,1,0:T(8,128)S(1)} %shard_map.54.own), channel_id=1, source_target_pairs={{2,4},{3,5},{6,8},{7,9},{10,12},{11,13},{4,2},{5,3},{8,6},{9,7},{1... | collective-permute-start | bytes 589832 | tf_op jit(solution)/shard_map/ppermute | solution.py:498
  64.1 6.8 %collective-permute-start.12 = (f32[4,4,24,128]{3,2,1,0:T(8,128)S(1)}, f32[4,4,24,128]{3,2,1,0:T(8,128)S(1)}, u32[]{:S(2)}, u32[]{:S(2)}) collective-permute-start(f32[4,4,24,128]{3,2,1,0:T(8,128)S(1)} %shard_map.54.own), channel_id=1, source_target_pairs={{0,2},{1,3},{2,0},{3,1},{4,6},{5,7},{6,4},{7,5},{8,10},{9,11},{10,... | collective-permute-start | bytes 589832 | tf_op jit(solution)/shard_map/ppermute | solution.py:499
  69.0 3.1 %collective-permute-start.18 = (f32[2,4,16,128]{3,2,1,0:T(8,128)S(1)}, f32[2,4,16,128]{3,2,1,0:T(8,128)S(1)}, u32[]{:S(2)}, u32[]{:S(2)}) collective-permute-start(f32[2,4,16,128]{3,2,1,0:T(8,128)S(1)} %get-tuple-element.60), channel_id=1, source_target_pairs={{0,1},{1,0},{2,3},{3,2},{4,5},{5,4},{6,7},{7,6},{8,9},{9,8},{10,11... | collective-permute-start | bytes 196616 | tf_op jit(solution)/shard_map/ppermute | solution.py:512
  72.0 1.3 %collective-permute-start.17 = (f32[2,4,16,128]{3,2,1,0:T(8,128)S(1)}, f32[2,4,16,128]{3,2,1,0:T(8,128)S(1)}, u32[]{:S(2)}, u32[]{:S(2)}) collective-permute-start(f32[2,4,16,128]{3,2,1,0:T(8,128)S(1)} %get-tuple-element.59), channel_id=1, source_target_pairs={{0,1},{1,0},{2,3},{3,2},{4,5},{5,4},{6,7},{7,6},{8,9},{9,8},{10,11... | collective-permute-start | bytes 196616 | tf_op jit(solution)/shard_map/ppermute | solution.py:512

commit v7 on v6

--- a/solution.py
+++ b/solution.py
@@ -445,8 +445,8 @@
     outer = lax.ppermute(outer, "space", facing)
     inner = lax.ppermute(inner, "space", cores)
     fields, inner = lax.optimization_barrier((fields, inner))
+    fields_other = lax.ppermute(fields, "space", others)
     fields_pair = lax.ppermute(fields, "space", pairs)
-    fields_other = lax.ppermute(fields, "space", others)
     base, rim = call(
         inside_kernel,
         [block, block],
@@ -455,7 +455,7 @@
         anywhere=True,
         mib=INSIDE_MIB,
     )
-    outer, fields_pair, fields_other = lax.optimization_barrier((outer, fields_pair, fields_other))
+    outer, fields_other, fields_pair = lax.optimization_barrier((outer, fields_other, fields_pair))
     sent = call(
         resid_kernel,
         (WINDOW, SLAB * WIDE + EXTRA, NY),

time: 91.1 us -> 91.9 us (level)
    ppermute x2, starting transfers between devices: 1.2 us -> 0.01 us  [shards(): pair_specs.append(lax.ppermute(pair, 'space', pairs))]
    ppermute x2, starting transfers between devices: 3.03 us -> 4.22 us  [shards(): other_specs.append(lax.ppermute(other, 'space', others))]
where the time goes in v7:
time: 91.9 us; the launch traced here: 91.6 us
  blocking collectives  39.7 us (43%)
  waiting for transfers between devices  26.6 us (29%)
  starting transfers between devices  15.8 us (17%)
  Pallas kernels  9.19 us (10%)
    all_to_all x1, blocking collectives, shards(): times = lax.all_to_all(sent, 'tm', 0, 0)  23.2 us
    all_to_all x1, blocking collectives, shards(): correction = lax.all_to_all(correction, 'tm', 0, 0)  16.5 us
    ppermute x1, waiting for transfers between devices, shards(): lax.ppermute(first, 'tm', [(i, (i + 1) % WINDOW) for i in range(WINDOW)])  10.1 us
    pallas_call x14, Pallas kernels, call(): pl.pallas_call(kernel, out_shape=out_shape if several else out_shape[0],...  9.19 us
    ppermute x2, waiting for transfers between devices, shards(): other_specs.append(lax.ppermute(other, 'space', others))  5.53 us
    ppermute x2, waiting for transfers between devices, shards(): other_owns.append(lax.ppermute(own, 'space', others))  5.08 us
    ppermute x2, starting transfers between devices, shards(): other_specs.append(lax.ppermute(other, 'space', others))  4.22 us
    ppermute x2, starting transfers between devices, shards(): other_owns.append(lax.ppermute(own, 'space', others))  4.08 us
  transfers between devices with their start and end apart: 19, of which 10 were waited for; matrix products, arithmetic and copies ran while one was open for 0% of the time, Pallas kernels for 7%

profile of v7, /device:TPU:24, one launch (start us, length us, event | category | flops | bytes accessed | tf_op | source)
XLA Modules:
  0.0 91.6 jit_solution(3345344202497526672)
XLA Ops:
  0.0 1.6 %shard_map.47 = (f32[128,256]{1,0:T(8,128)S(1)}, f32[128,256]{1,0:T(8,128)S(1)}, f32[2,128,256]{2,1,0:T(8,128)S(1)}, f32[2,128,256]{2,1,0:T(8,128)S(1)}, f32[4,2,32,128]{3,2,1,0:T(8,128)S(1)}) custom-call(f32[1,2,128,256]{3,2,1,0:T(8,128)} %iterate.5, f32[2,128,256]{2,1,0:T(8,128)} %kappa.1, f32[3,2,128,256]{3,2,1,0:T(8,128)} %velocity.1), custom_call_target="tpu_custom_call" | custom-call | tf_op jit(solution)/shard_map/pallas_call | solution.py:416
  1.7 0.8 collective-permute-start.2
  3.3 2.7 %collective-permute-start.4 = (f32[4,2,32,128]{3,2,1,0:T(8,128)S(1)}, f32[4,2,32,128]{3,2,1,0:T(8,128)S(1)}, u32[]{:S(2)}, u32[]{:S(2)}) collective-permute-start(f32[4,2,32,128]{3,2,1,0:T(8,128)S(1)} %get-tuple-element.52.fields), channel_id=1, source_target_pairs={{2,4},{3,5},{6,8},{7,9},{10,12},{11,13},{4,2},{5,3},{8,6},{9,7},{1... | collective-permute-start | bytes 393224 | tf_op jit(solution)/shard_map/ppermute | solution.py:448
  6.0 1.5 %collective-permute-start = (f32[128,256]{1,0:T(8,128)S(1)}, f32[128,256]{1,0:T(8,128)S(1)}, u32[]{:S(2)}, u32[]{:S(2)}) collective-permute-start(f32[128,256]{1,0:T(8,128)S(1)} %get-tuple-element.35), channel_id=1, source_target_pairs={{0,16},{16,32},{32,48},{48,64},{64,80},{80,96},{96,112},{112,128},... | collective-permute-start | bytes 393224 | tf_op jit(solution)/shard_map/ppermute | solution.py:443
  7.5 1.5 %collective-permute-start.1 = (f32[128,256]{1,0:T(8,128)S(1)}, f32[128,256]{1,0:T(8,128)S(1)}, u32[]{:S(2)}, u32[]{:S(2)}) collective-permute-start(f32[128,256]{1,0:T(8,128)S(1)} %get-tuple-element.36), channel_id=1, source_target_pairs={{0,16},{16,32},{32,48},{48,0},{64,80},{80,96},{96,112},{112,64},{1... | collective-permute-start | bytes 393224 | tf_op jit(solution)/shard_map/ppermute | solution.py:444
  9.0 1.9 %shard_map.46 = (f32[2,128,256]{2,1,0:T(8,128)S(1)}, f32[2,128,256]{2,1,0:T(8,128)S(1)}) custom-call(f32[1,2,128,256]{3,2,1,0:T(8,128)} %forcing_hbm.1, f32[1,2,128,256]{3,2,1,0:T(8,128)} %iterate.5, f32[2,128,256]{2,1,0:T(8,128)} %kappa.1, f32[3,2,128,256]{3,2,1,0:T(8,128)} %velocity.1), custom_call_target="tpu_custom_call" | custom-call | tf_op jit(solution)/shard_map/pallas_call | solution.py:416
  10.9 2.2 %collective-permute-done.4.other = f32[4,2,32,128]{3,2,1,0:T(8,128)S(1)} collective-permute-done((f32[4,2,32,128]{3,2,1,0:T(8,128)S(1)}, f32[4,2,32,128]{3,2,1,0:T(8,128)S(1)}, u32[]{:S(2)}, u32[]{:S(2)}) %collective-permute-start.4) | collective-permute-done | bytes 131104 | tf_op jit(solution)/shard_map/ppermute | solution.py:448
  13.1 10.1 %collective-permute-done.first = f32[128,256]{1,0:T(8,128)S(1)} collective-permute-done((f32[128,256]{1,0:T(8,128)S(1)}, f32[128,256]{1,0:T(8,128)S(1)}, u32[]{:S(2)}, u32[]{:S(2)}) %collective-permute-start) | collective-permute-done | bytes 131104 | tf_op jit(solution)/shard_map/ppermute | solution.py:443
  23.5 23.2 %all_to_all.10.times = f32[16,80,128]{2,1,0:T(8,128)S(1)} all-to-all(f32[16,80,128]{2,1,0:T(8,128)S(1)} %shard_map.48), channel_id=1, replica_groups=mesh['tm'=16,'space'=16] {'tm'}, dimensions={0} | all-to-all | bytes 1310720 | tf_op jit(solution)/shard_map/all_to_all | solution.py:465
  46.9 1.3 %collective-permute-done.9.got = f32[8,32,128]{2,1,0:T(8,128)S(1)} collective-permute-done((f32[8,32,128]{2,1,0:T(8,128)S(1)}, f32[8,32,128]{2,1,0:T(8,128)S(1)}, u32[]{:S(2)}, u32[]{:S(2)}) %collective-permute-start.9) | collective-permute-done | bytes 131104 | tf_op jit(solution)/shard_map/ppermute | solution.py:472
  49.0 1.8 %collective-permute-start.13 = (f32[3,4,32,128]{3,2,1,0:T(8,128)S(1)}, f32[3,4,32,128]{3,2,1,0:T(8,128)S(1)}, u32[]{:S(2)}, u32[]{:S(2)}) collective-permute-start(f32[3,4,32,128]{3,2,1,0:T(8,128)S(1)} %get-tuple-element.56), channel_id=1, source_target_pairs={{2,4},{3,5},{6,8},{7,9},{10,12},{11,13},{4,2},{5,3},{8,6},{9,7},{1... | collective-permute-start | bytes 589832 | tf_op jit(solution)/shard_map/ppermute | solution.py:478
  50.9 2.4 %collective-permute-start.7 = (f32[3,4,32,128]{3,2,1,0:T(8,128)S(1)}, f32[3,4,32,128]{3,2,1,0:T(8,128)S(1)}, u32[]{:S(2)}, u32[]{:S(2)}) collective-permute-start(f32[3,4,32,128]{3,2,1,0:T(8,128)S(1)} %get-tuple-element.46), channel_id=1, source_target_pairs={{2,4},{3,5},{6,8},{7,9},{10,12},{11,13},{4,2},{5,3},{8,6},{9,7},{1... | collective-permute-start | bytes 589832 | tf_op jit(solution)/shard_map/ppermute | solution.py:478
  53.7 5.1 %collective-permute-done.13.other = f32[3,4,32,128]{3,2,1,0:T(8,128)S(1)} collective-permute-done((f32[3,4,32,128]{3,2,1,0:T(8,128)S(1)}, f32[3,4,32,128]{3,2,1,0:T(8,128)S(1)}, u32[]{:S(2)}, u32[]{:S(2)}) %collective-permute-start.13) | collective-permute-done | bytes 196640 | tf_op jit(solution)/shard_map/ppermute | solution.py:478
  58.8 0.8 shard_map.56.own
  59.6 2.1 %collective-permute-start.15 = (f32[4,4,24,128]{3,2,1,0:T(8,128)S(1)}, f32[4,4,24,128]{3,2,1,0:T(8,128)S(1)}, u32[]{:S(2)}, u32[]{:S(2)}) collective-permute-start(f32[4,4,24,128]{3,2,1,0:T(8,128)S(1)} %shard_map.56.own), channel_id=1, source_target_pairs={{2,4},{3,5},{6,8},{7,9},{10,12},{11,13},{4,2},{5,3},{8,6},{9,7},{1... | collective-permute-start | bytes 589832 | tf_op jit(solution)/shard_map/ppermute | solution.py:498
  62.2 0.8 shard_map.54.own
  63.0 1.9 %collective-permute-start.11 = (f32[4,4,24,128]{3,2,1,0:T(8,128)S(1)}, f32[4,4,24,128]{3,2,1,0:T(8,128)S(1)}, u32[]{:S(2)}, u32[]{:S(2)}) collective-permute-start(f32[4,4,24,128]{3,2,1,0:T(8,128)S(1)} %shard_map.54.own), channel_id=1, source_target_pairs={{2,4},{3,5},{6,8},{7,9},{10,12},{11,13},{4,2},{5,3},{8,6},{9,7},{1... | collective-permute-start | bytes 589832 | tf_op jit(solution)/shard_map/ppermute | solution.py:498
  65.0 2.8 %collective-permute-done.15.other_own = f32[4,4,24,128]{3,2,1,0:T(8,128)S(1)} collective-permute-done((f32[4,4,24,128]{3,2,1,0:T(8,128)S(1)}, f32[4,4,24,128]{3,2,1,0:T(8,128)S(1)}, u32[]{:S(2)}, u32[]{:S(2)}) %collective-permute-start.15) | collective-permute-done | bytes 196640 | tf_op jit(solution)/shard_map/ppermute | solution.py:498
  68.2 1.1 %shard_map.57 = (f32[2,4,16,128]{3,2,1,0:T(8,128)S(1)}, f32[2,4,16,128]{3,2,1,0:T(8,128)S(1)}) custom-call(f32[4,4,32,128]{3,2,1,0:T(8,128)S(1)} %get-tuple-element.55.chip, f32[3,4,32,128]{3,2,1,0:T(8,128)S(1)} %collective-permute-done.13.other, f32[3,4,32,128]{3,2,1,0:T(8,128)S(1)} %collective-permute-done.14.pair, f32[10,15,32,128]{3,2,1,0:T(8,128)S(1)} %shard_map.53.cof, ...), custom_call_target="tpu_custom_call" | custom-call | tf_op jit(solution)/shard_map/pallas_call | solution.py:416
  69.4 2.3 %collective-permute-done.11.other_own = f32[4,4,24,128]{3,2,1,0:T(8,128)S(1)} collective-permute-done((f32[4,4,24,128]{3,2,1,0:T(8,128)S(1)}, f32[4,4,24,128]{3,2,1,0:T(8,128)S(1)}, u32[]{:S(2)}, u32[]{:S(2)}) %collective-permute-start.11) | collective-permute-done | bytes 196640 | tf_op jit(solution)/shard_map/ppermute | solution.py:498
  71.7 1.1 %shard_map.55 = (f32[2,4,16,128]{3,2,1,0:T(8,128)S(1)}, f32[2,4,16,128]{3,2,1,0:T(8,128)S(1)}) custom-call(f32[4,4,32,128]{3,2,1,0:T(8,128)S(1)} %get-tuple-element.45.chip, f32[3,4,32,128]{3,2,1,0:T(8,128)S(1)} %collective-permute-done.7.other, f32[3,4,32,128]{3,2,1,0:T(8,128)S(1)} %collective-permute-done.8.pair, f32[10,15,32,128]{3,2,1,0:T(8,128)S(1)} %shard_map.53.cof, ...), custom_call_target="tpu_custom_call" | custom-call | tf_op jit(solution)/shard_map/pallas_call | solution.py:416
  72.9 1.2 %collective-permute-done.17.refs_2_ = f32[2,4,16,128]{3,2,1,0:T(8,128)S(1)} collective-permute-done((f32[2,4,16,128]{3,2,1,0:T(8,128)S(1)}, f32[2,4,16,128]{3,2,1,0:T(8,128)S(1)}, u32[]{:S(2)}, u32[]{:S(2)}) %collective-permute-start.17) | collective-permute-done | bytes 65568 | tf_op jit(solution)/shard_map/ppermute | solution.py:512
  74.2 16.5 %all_to_all.11.correction = f32[16,2,16,128]{3,2,1,0:T(8,128)S(1)} all-to-all(f32[16,2,16,128]{3,2,1,0:T(8,128)S(1)} %shard_map.58), channel_id=1, replica_groups=mesh['tm'=16,'space'=16] {'tm'}, dimensions={0} | all-to-all | bytes 524288 | tf_op jit(solution)/shard_map/all_to_all | solution.py:514
  90.7 0.8 shard_map.59
  (32 shorter events, 3.7 us)
Async XLA Ops:
  0.0 23.2 %copy-start = (f32[1,2,128,256]{3,2,1,0:T(8,128)S(1)}, f32[1,2,128,256]{3,2,1,0:T(8,128)}, u32[]{:S(2)}) copy-start(f32[1,2,128,256]{3,2,1,0:T(8,128)} %iterate.5) | copy-start | bytes 786436
  1.6 1.6 %collective-permute-start.3 = (f32[2,128,256]{2,1,0:T(8,128)S(1)}, f32[2,128,256]{2,1,0:T(8,128)S(1)}, u32[]{:S(2)}, u32[]{:S(2)}) collective-permute-start(f32[2,128,256]{2,1,0:T(8,128)S(1)} %get-tuple-element.39), channel_id=1, source_target_pairs={{0,1},{1,0},{2,3},{3,2},{4,5},{5,4},{6,7},{7,6},{8,9},{9,8},{10,11... | collective-permute-start | bytes 786440 | tf_op jit(solution)/shard_map/ppermute | solution.py:446
  1.7 9.2 %collective-permute-start.2 = (f32[2,128,256]{2,1,0:T(8,128)S(1)}, f32[2,128,256]{2,1,0:T(8,128)S(1)}, u32[]{:S(2)}, u32[]{:S(2)}) collective-permute-start(f32[2,128,256]{2,1,0:T(8,128)S(1)} %get-tuple-element.37), channel_id=1, source_target_pairs={{1,2},{3,4},{5,6},{7,8},{9,10},{11,12},{13,14},{15,0},{2,1},{4,3},... | collective-permute-start | bytes 786440 | tf_op jit(solution)/shard_map/ppermute | solution.py:445
  3.3 9.9 %collective-permute-start.4 = (f32[4,2,32,128]{3,2,1,0:T(8,128)S(1)}, f32[4,2,32,128]{3,2,1,0:T(8,128)S(1)}, u32[]{:S(2)}, u32[]{:S(2)}) collective-permute-start(f32[4,2,32,128]{3,2,1,0:T(8,128)S(1)} %get-tuple-element.52.fields), channel_id=1, source_target_pairs={{2,4},{3,5},{6,8},{7,9},{10,12},{11,13},{4,2},{5,3},{8,6},{9,7},{1... | collective-permute-start | bytes 393224 | tf_op jit(solution)/shard_map/ppermute | solution.py:448
  6.0 7.2 %collective-permute-start.5 = (f32[4,2,32,128]{3,2,1,0:T(8,128)S(1)}, f32[4,2,32,128]{3,2,1,0:T(8,128)S(1)}, u32[]{:S(2)}, u32[]{:S(2)}) collective-permute-start(f32[4,2,32,128]{3,2,1,0:T(8,128)S(1)} %get-tuple-element.52.fields), channel_id=1, source_target_pairs={{0,2},{1,3},{2,0},{3,1},{4,6},{5,7},{6,4},{7,5},{8,10},{9,11},{10,... | collective-permute-start | bytes 393224 | tf_op jit(solution)/shard_map/ppermute | solution.py:449
  6.0 17.2 %collective-permute-start = (f32[128,256]{1,0:T(8,128)S(1)}, f32[128,256]{1,0:T(8,128)S(1)}, u32[]{:S(2)}, u32[]{:S(2)}) collective-permute-start(f32[128,256]{1,0:T(8,128)S(1)} %get-tuple-element.35), channel_id=1, source_target_pairs={{0,16},{16,32},{32,48},{48,64},{64,80},{80,96},{96,112},{112,128},... | collective-permute-start | bytes 393224 | tf_op jit(solution)/shard_map/ppermute | solution.py:443
  7.5 15.7 %collective-permute-start.1 = (f32[128,256]{1,0:T(8,128)S(1)}, f32[128,256]{1,0:T(8,128)S(1)}, u32[]{:S(2)}, u32[]{:S(2)}) collective-permute-start(f32[128,256]{1,0:T(8,128)S(1)} %get-tuple-element.36), channel_id=1, source_target_pairs={{0,16},{16,32},{32,48},{48,0},{64,80},{80,96},{96,112},{112,64},{1... | collective-permute-start | bytes 393224 | tf_op jit(solution)/shard_map/ppermute | solution.py:444
  46.8 1.4 %collective-permute-start.9 = (f32[8,32,128]{2,1,0:T(8,128)S(1)}, f32[8,32,128]{2,1,0:T(8,128)S(1)}, u32[]{:S(2)}, u32[]{:S(2)}) collective-permute-start(f32[8,32,128]{2,1,0:T(8,128)S(1)} %get-tuple-element.50), channel_id=1, source_target_pairs={{0,1},{1,0},{2,3},{3,2},{4,5},{5,4},{6,7},{7,6},{8,9},{9,8},{10,11... | collective-permute-start | bytes 393224 | tf_op jit(solution)/shard_map/ppermute | solution.py:472
  48.4 4.9 %collective-permute-start.10 = (f32[3,4,2,32,128]{4,3,2,1,0:T(8,128)S(1)}, f32[3,4,2,32,128]{4,3,2,1,0:T(8,128)S(1)}, u32[]{:S(2)}, u32[]{:S(2)}) collective-permute-start(f32[3,4,2,32,128]{4,3,2,1,0:T(8,128)S(1)} %shard_map.52), channel_id=1, source_target_pairs={{0,1},{1,0},{2,3},{3,2},{4,5},{5,4},{6,7},{7,6},{8,9},{9,8},{10,11... | collective-permute-start | bytes 1179656 | tf_op jit(solution)/shard_map/ppermute | solution.py:482
  48.6 2.2 %collective-permute-start.6 = (f32[8,32,128]{2,1,0:T(8,128)S(1)}, f32[8,32,128]{2,1,0:T(8,128)S(1)}, u32[]{:S(2)}, u32[]{:S(2)}) collective-permute-start(f32[8,32,128]{2,1,0:T(8,128)S(1)} %get-tuple-element.44), channel_id=1, source_target_pairs={{0,1},{1,0},{2,3},{3,2},{4,5},{5,4},{6,7},{7,6},{8,9},{9,8},{10,11... | collective-permute-start | bytes 393224 | tf_op jit(solution)/shard_map/ppermute | solution.py:472
  49.0 9.9 %collective-permute-start.13 = (f32[3,4,32,128]{3,2,1,0:T(8,128)S(1)}, f32[3,4,32,128]{3,2,1,0:T(8,128)S(1)}, u32[]{:S(2)}, u32[]{:S(2)}) collective-permute-start(f32[3,4,32,128]{3,2,1,0:T(8,128)S(1)} %get-tuple-element.56), channel_id=1, source_target_pairs={{2,4},{3,5},{6,8},{7,9},{10,12},{11,13},{4,2},{5,3},{8,6},{9,7},{1... | collective-permute-start | bytes 589832 | tf_op jit(solution)/shard_map/ppermute | solution.py:478
  50.8 8.0 %collective-permute-start.14 = (f32[3,4,32,128]{3,2,1,0:T(8,128)S(1)}, f32[3,4,32,128]{3,2,1,0:T(8,128)S(1)}, u32[]{:S(2)}, u32[]{:S(2)}) collective-permute-start(f32[3,4,32,128]{3,2,1,0:T(8,128)S(1)} %get-tuple-element.57), channel_id=1, source_target_pairs={{0,2},{1,3},{2,0},{3,1},{4,6},{5,7},{6,4},{7,5},{8,10},{9,11},{10,... | collective-permute-start | bytes 589832 | tf_op jit(solution)/shard_map/ppermute | solution.py:479
  50.9 11.4 %collective-permute-start.7 = (f32[3,4,32,128]{3,2,1,0:T(8,128)S(1)}, f32[3,4,32,128]{3,2,1,0:T(8,128)S(1)}, u32[]{:S(2)}, u32[]{:S(2)}) collective-permute-start(f32[3,4,32,128]{3,2,1,0:T(8,128)S(1)} %get-tuple-element.46), channel_id=1, source_target_pairs={{2,4},{3,5},{6,8},{7,9},{10,12},{11,13},{4,2},{5,3},{8,6},{9,7},{1... | collective-permute-start | bytes 589832 | tf_op jit(solution)/shard_map/ppermute | solution.py:478
  53.2 9.0 %collective-permute-start.8 = (f32[3,4,32,128]{3,2,1,0:T(8,128)S(1)}, f32[3,4,32,128]{3,2,1,0:T(8,128)S(1)}, u32[]{:S(2)}, u32[]{:S(2)}) collective-permute-start(f32[3,4,32,128]{3,2,1,0:T(8,128)S(1)} %get-tuple-element.47), channel_id=1, source_target_pairs={{0,2},{1,3},{2,0},{3,1},{4,6},{5,7},{6,4},{7,5},{8,10},{9,11},{10,... | collective-permute-start | bytes 589832 | tf_op jit(solution)/shard_map/ppermute | solution.py:479
  59.6 8.1 %collective-permute-start.15 = (f32[4,4,24,128]{3,2,1,0:T(8,128)S(1)}, f32[4,4,24,128]{3,2,1,0:T(8,128)S(1)}, u32[]{:S(2)}, u32[]{:S(2)}) collective-permute-start(f32[4,4,24,128]{3,2,1,0:T(8,128)S(1)} %shard_map.56.own), channel_id=1, source_target_pairs={{2,4},{3,5},{6,8},{7,9},{10,12},{11,13},{4,2},{5,3},{8,6},{9,7},{1... | collective-permute-start | bytes 589832 | tf_op jit(solution)/shard_map/ppermute | solution.py:498
  61.8 6.5 %collective-permute-start.16 = (f32[4,4,24,128]{3,2,1,0:T(8,128)S(1)}, f32[4,4,24,128]{3,2,1,0:T(8,128)S(1)}, u32[]{:S(2)}, u32[]{:S(2)}) collective-permute-start(f32[4,4,24,128]{3,2,1,0:T(8,128)S(1)} %shard_map.56.own), channel_id=1, source_target_pairs={{0,2},{1,3},{2,0},{3,1},{4,6},{5,7},{6,4},{7,5},{8,10},{9,11},{10,... | collective-permute-start | bytes 589832 | tf_op jit(solution)/shard_map/ppermute | solution.py:499
  63.0 8.7 %collective-permute-start.11 = (f32[4,4,24,128]{3,2,1,0:T(8,128)S(1)}, f32[4,4,24,128]{3,2,1,0:T(8,128)S(1)}, u32[]{:S(2)}, u32[]{:S(2)}) collective-permute-start(f32[4,4,24,128]{3,2,1,0:T(8,128)S(1)} %shard_map.54.own), channel_id=1, source_target_pairs={{2,4},{3,5},{6,8},{7,9},{10,12},{11,13},{4,2},{5,3},{8,6},{9,7},{1... | collective-permute-start | bytes 589832 | tf_op jit(solution)/shard_map/ppermute | solution.py:498
  65.0 6.7 %collective-permute-start.12 = (f32[4,4,24,128]{3,2,1,0:T(8,128)S(1)}, f32[4,4,24,128]{3,2,1,0:T(8,128)S(1)}, u32[]{:S(2)}, u32[]{:S(2)}) collective-permute-start(f32[4,4,24,128]{3,2,1,0:T(8,128)S(1)} %shard_map.54.own), channel_id=1, source_target_pairs={{0,2},{1,3},{2,0},{3,1},{4,6},{5,7},{6,4},{7,5},{8,10},{9,11},{10,... | collective-permute-start | bytes 589832 | tf_op jit(solution)/shard_map/ppermute | solution.py:499
  69.3 3.6 %collective-permute-start.18 = (f32[2,4,16,128]{3,2,1,0:T(8,128)S(1)}, f32[2,4,16,128]{3,2,1,0:T(8,128)S(1)}, u32[]{:S(2)}, u32[]{:S(2)}) collective-permute-start(f32[2,4,16,128]{3,2,1,0:T(8,128)S(1)} %get-tuple-element.60), channel_id=1, source_target_pairs={{0,1},{1,0},{2,3},{3,2},{4,5},{5,4},{6,7},{7,6},{8,9},{9,8},{10,11... | collective-permute-start | bytes 196616 | tf_op jit(solution)/shard_map/ppermute | solution.py:512
  72.8 1.3 %collective-permute-start.17 = (f32[2,4,16,128]{3,2,1,0:T(8,128)S(1)}, f32[2,4,16,128]{3,2,1,0:T(8,128)S(1)}, u32[]{:S(2)}, u32[]{:S(2)}) collective-permute-start(f32[2,4,16,128]{3,2,1,0:T(8,128)S(1)} %get-tuple-element.59), channel_id=1, source_target_pairs={{0,1},{1,0},{2,3},{3,2},{4,5},{5,4},{6,7},{7,6},{8,9},{9,8},{10,11... | collective-permute-start | bytes 196616 | tf_op jit(solution)/shard_map/ppermute | solution.py:512
